TPU v7x, 32 devices: a whole 2x2x4 slice. The times are simulated.
32 devices in a mesh: lat: 16 (over z, y, core), lon: 2 (over x).
Axes of the slice: x: 2, y: 2, z: 4, core: 2. Of those that a mesh axis runs over, the one named last changes fastest.
Arguments:
- state_field: bfloat16 [73, 128, 256], P(None, 'lat', 'lon'), may hold values from -6 to 6
- support_rows: int32 [64, 5], P('lat'), may hold values from -2 to 2, as said below
- window_bands: int32 [16], replicated, may hold values from 0 to 63, as said below
- conv_weight: bfloat16 [5, 3, 73, 256], replicated, may hold values from -0.1875 to 0.1875
- w_query: bfloat16 [256, 256], replicated
- w_key: bfloat16 [256, 256], replicated
- w_value: bfloat16 [256, 256], replicated, may hold values from -0.375 to 0.375
- w_out: bfloat16 [256, 256], replicated, may hold values from -0.75 to 0.75
Outputs:
- window_out: bfloat16 [16, 128, 256], P('lat', 'lon')
Inputs may be any that keep to these rules, and one draw needn't show every extreme that they name: `support_rows`: each row is a permutation of the 5 offsets from -2 to 2. `window_bands`: 16 distinct token bands.
All inputs are finite; a program needn't handle non-finite values.
Results may differ from a plain program's by a relative error of at most 0.019.
Values may be sent and summed in bfloat16 or wider, within the bound.
No kernel may reach another device: no remote copies, remote signals or barrier semaphores. Data moves between devices by JAX's collectives and lax.ppermute only.
A program may use at most 64 MiB of HBM per device.

v0:
```python
import math

import jax
import jax.numpy as jnp
from jax import lax
from jax.sharding import PartitionSpec as P

D = 256
H = 4


def padded(x, sides, width):
    for axis, dim in sides:
        devices, length = (lax.axis_size(axis), x.shape[dim])
        up = [(i, (i + 1) % devices) for i in range(devices - 1)]
        down = [(j, i) for i, j in up]
        last = lax.slice_in_dim(x, length - width, length, axis=dim)
        leading = lax.slice_in_dim(x, 0, width, axis=dim)
        before = lax.ppermute(last, axis, up)
        after = lax.ppermute(leading, axis, down)
        x = jnp.concatenate([before, x, after], axis=dim)
    return x


def shifted(x, axis, by):
    devices = lax.axis_size(axis)
    return lax.ppermute(x, axis, [(i, (i + by) % devices) for i in range(devices)])


def conv_features(extended, support_rows, conv_weight):
    bands = support_rows.shape[0]
    width = (extended.shape[2] - 1) // 2
    row_index = 2 * jnp.arange(bands, dtype=jnp.int32)[:, None] + support_rows + 2
    picked = jnp.take(extended, row_index, axis=1)
    tapped = jnp.stack(
        [picked[..., column_tap : column_tap + 2 * width : 2] for column_tap in range(3)], axis=3
    )
    patches = jnp.transpose(tapped, (1, 4, 2, 3, 0)).reshape(bands * width, -1)
    raw = jnp.dot(
        patches, conv_weight.reshape(-1, conv_weight.shape[-1]), preferred_element_type=jnp.float32
    )
    factor = lax.rsqrt(jnp.mean(raw * raw, axis=-1, keepdims=True) + 1e-06)
    return (raw * factor).astype(jnp.bfloat16).reshape(bands, width, -1)


def absorb(carry, block_keys, block_values, block_area, queries, scale):
    running_max, running_sum, mixed = carry
    scores = (
        jnp.einsum("qhd,khd->qhk", queries, block_keys, preferred_element_type=jnp.float32) * scale
        + block_area
    )
    new_max = jnp.maximum(running_max, jnp.max(scores, axis=-1))
    factor = jnp.exp(running_max - new_max)
    weights = jnp.exp(scores - new_max[..., None])
    running_sum = running_sum * factor + jnp.sum(weights, axis=-1)
    update = jnp.einsum(
        "qhk,khd->qhd",
        weights.astype(jnp.bfloat16),
        block_values,
        preferred_element_type=jnp.float32,
    )
    mixed = mixed * factor[..., None] + update
    return (new_max, running_sum, mixed)


def sweep(carry, keys, values, queries, band_total):
    rows = keys.shape[0]
    lon_tile = keys.shape[1]
    head_size = D // H
    band_block = math.gcd(rows, max(1, 512 // lon_tile))
    blocks = rows // band_block
    block_len = band_block * lon_tile
    keys_blocks = keys.reshape(blocks, block_len, H, head_size)
    values_blocks = values.reshape(blocks, block_len, H, head_size)
    band_index = jnp.arange(rows, dtype=jnp.int32).astype(jnp.float32)
    centre = (band_index + 0.5) * (math.pi / band_total) - math.pi / 2
    area_rows = jnp.repeat(jnp.log(jnp.cos(centre)), lon_tile).reshape(blocks, block_len)
    scale = 1.0 / math.sqrt(head_size)

    def step_block(state, inputs):
        return (absorb(state, inputs[0], inputs[1], inputs[2], queries, scale), None)

    result, unused = lax.scan(step_block, carry, (keys_blocks, values_blocks, area_rows))
    return result


def per_device(
    state_field, support_rows, window_bands, conv_weight, w_query, w_key, w_value, w_out
):
    lat_tile = support_rows.shape[0]
    lon_tile = state_field.shape[2] // 2
    whole_lon = lon_tile * lax.axis_size("lon")
    band_total = lat_tile * lax.axis_size("lat")
    head_size = D // H
    extended = padded(state_field, (("lat", 1),), 2)
    western = shifted(extended[:, :, -1:], "lon", 1)
    extended = jnp.concatenate([western, extended], axis=2)
    features = conv_features(extended, support_rows, conv_weight)
    flat = features.reshape(-1, D)
    slot_count = window_bands.shape[0] // lax.axis_size("lat")
    local_queries = jnp.dot(flat, w_query, preferred_element_type=jnp.float32).astype(jnp.bfloat16)
    local_queries = local_queries.reshape(lat_tile, lon_tile * D)
    first_band = lax.axis_index("lat") * lat_tile
    wanted = window_bands - first_band
    onehot = (wanted[:, None] == jnp.arange(lat_tile, dtype=jnp.int32)[None, :]).astype(
        jnp.bfloat16
    )
    picked = jnp.dot(onehot, local_queries, preferred_element_type=jnp.float32)
    picked = picked.astype(jnp.bfloat16).astype(jnp.float32)
    mine = lax.psum_scatter(
        picked.reshape(slot_count * lax.axis_size("lat"), lon_tile, D).astype(jnp.bfloat16),
        "lat",
        scatter_dimension=0,
        tiled=True,
    )
    gathered = lax.all_gather(mine, "lon", axis=1, tiled=True)
    query_count = slot_count * whole_lon
    queries = gathered.reshape(query_count, H, head_size)
    initial = (
        jnp.full((query_count, H), -1e30, jnp.float32),
        jnp.zeros((query_count, H), jnp.float32),
        jnp.zeros((query_count, H, head_size), jnp.float32),
    )
    piece = lax.all_gather(features, "lat", axis=0, tiled=True)
    piece_rows = piece.reshape(-1, D)
    keys = (
        jnp.dot(piece_rows, w_key, preferred_element_type=jnp.float32)
        .astype(jnp.bfloat16)
        .reshape(piece.shape)
    )
    values = (
        jnp.dot(piece_rows, w_value, preferred_element_type=jnp.float32)
        .astype(jnp.bfloat16)
        .reshape(piece.shape)
    )
    carry = sweep(initial, keys, values, queries, band_total)
    running_max, running_sum, mixed = carry
    best = lax.pmax(running_max, "lon")
    factor = jnp.exp(running_max - best)
    scaled_mix = (mixed * factor[..., None]).reshape(slot_count, whole_lon, D)
    scaled_sum = (running_sum * factor).reshape(slot_count, whole_lon, H)
    mix_share, sum_share = (
        lax.psum_scatter(
            scaled_mix.astype(jnp.bfloat16), "lon", scatter_dimension=1, tiled=True
        ).astype(jnp.float32),
        lax.psum_scatter(
            scaled_sum.astype(jnp.bfloat16), "lon", scatter_dimension=1, tiled=True
        ).astype(jnp.float32),
    )
    attended = mix_share.reshape(slot_count, lon_tile, H, head_size) / sum_share[..., None]
    attended = attended.astype(jnp.bfloat16).reshape(slot_count * lon_tile, D)
    result = jnp.dot(attended, w_out, preferred_element_type=jnp.float32).astype(jnp.bfloat16)
    return result.reshape(slot_count, lon_tile, D)


def solution(mesh):
    return jax.shard_map(
        per_device,
        mesh=mesh,
        in_specs=(P(None, "lat", "lon"), P("lat", None), P(), P(), P(), P(), P(), P()),
        out_specs=P("lat", "lon", None),
        check_vma=False,
    )
```

profile of v0, /device:TPU:0, one launch (start us, length us, event | category | flops | bytes accessed | tf_op | source)
XLA Modules:
  0.0 208.5 jit_solution(12876466638075801712)
XLA Ops:
  7.7 2.4 %collective-permute-start = (bf16[73,2,128]{0,2,1:T(8,128)(2,1)S(1)}, bf16[73,2,128]{0,2,1:T(8,128)(2,1)S(1)}, u32[]{:S(2)}, u32[]{:S(2)}) collective-permute-start(bf16[73,2,128]{0,2,1:T(8,128)(2,1)S(1)} %get-tuple-element.127), channel_id=1, source_target_pairs={{0,2},{2,4},{4,6},{6,8},{8,10},{10,12},{12,14},{14,16},{16,18},{18... | collective-permute-start | bytes 112136 | tf_op jit(solution)/shard_map/ppermute | solution.py:19
  12.9 2.5 %collective-permute-done.1 = bf16[73,2,128]{0,2,1:T(8,128)(2,1)S(1)} collective-permute-done((bf16[73,2,128]{0,2,1:T(8,128)(2,1)S(1)}, bf16[73,2,128]{0,2,1:T(8,128)(2,1)S(1)}, u32[]{:S(2)}, u32[]{:S(2)}) %collective-permute-start.1) | collective-permute-done | bytes 37408 | tf_op jit(solution)/shard_map/ppermute | solution.py:20
  15.4 1.6 collective-permute-start.2
  22.4 1.8 slice.23
  29.8 57.5 %reduce-scatter.8.cloned.1.call-done = bf16[1,64,256]{2,1,0:T(8,128)(2,1)} async-done(((bf16[16,64,256]{2,1,0:T(8,128)(2,1)}), bf16[1,64,256]{2,1,0:T(8,128)(2,1)}) %reduce-scatter.8.cloned.1.call-update) | async-done | bytes 32784 | tf_op jit(solution)/shard_map/reduce_scatter | solution.py:110
  87.3 4.8 %all_gather.7 = bf16[1,128,256]{2,1,0:T(8,128)(2,1)S(1)} all-gather(bf16[1,64,256]{2,1,0:T(8,128)(2,1)} %reduce-scatter.8.cloned.1.call-done), channel_id=1, replica_groups=mesh['lat'=16,'lon'=2] {'lon'}, dimensions={1}, use_global_device_ids=true | all-gather | bytes 98304 | tf_op jit(solution)/shard_map/all_gather | solution.py:116
  92.2 37.9 %all-gather.2.cloned.1.call-done = bf16[64,64,256]{2,1,0:T(8,128)(2,1)} async-done(((bf16[4,64,256]{2,1,0:T(8,128)(2,1)}), bf16[64,64,256]{2,1,0:T(8,128)(2,1)}) %all-gather.2.cloned.1.call-update) | async-done | bytes 2097168 | tf_op jit(solution)/shard_map/all_gather | solution.py:124
  130.1 2.3 %convolution_convert_fusion.2 = bf16[4096,256]{1,0:T(8,128)(2,1)S(1)} fusion(bf16[4096,256]{1,0:T(8,128)(2,1)} %bitcast.79, bf16[256,256]{1,0:T(8,128)(2,1)S(1)} %copy-done), kind=kOutput, calls=%fused_computation.24 | convolution fusion | flops 537919488 | bytes 4325376 | tf_op jit(solution)/shard_map/dot_general | solution.py:127
  132.4 3.3 %reshape.105 = bf16[8,512,4,64]{3,2,1,0:T(4,128)(2,1)} reshape(bf16[4096,256]{1,0:T(8,128)(2,1)S(1)} %convolution_convert_fusion.2) | data formatting | bytes 4194304 | tf_op jit(solution)/shard_map/reshape;reshape | solution.py:73
  135.7 7.1 %copy.31 = bf16[8,512,4,64]{1,3,2,0:T(8,128)(2,1)} copy(bf16[8,512,4,64]{3,2,1,0:T(4,128)(2,1)} %reshape.105) | data formatting | bytes 4194304
  142.8 2.1 convolution_convert_fusion.1
  144.8 7.1 %reshape.106 = bf16[8,512,4,64]{3,2,1,0:T(4,128)(2,1)} reshape(bf16[4096,256]{1,0:T(8,128)(2,1)} %convolution_convert_fusion.1) | data formatting | bytes 4194304 | tf_op jit(solution)/shard_map/reshape;reshape | solution.py:74
  151.9 5.6 %copy.32 = bf16[8,512,4,64]{1,3,2,0:T(8,128)(2,1)S(1)} copy(bf16[8,512,4,64]{3,2,1,0:T(4,128)(2,1)} %reshape.106) | data formatting | bytes 4194304
  157.5 15.2 %while.15 = (s32[]{:T(128)}, f32[128,4]{0,1:T(4,128)S(1)}, f32[128,4]{0,1:T(4,128)S(1)}, f32[128,4,64]{0,2,1:T(8,128)S(1)}, bf16[8,512,4,64]{1,3,2,0:T(8,128)(2,...) while((s32[]{:T(128)}, f32[128,4]{0,1:T(4,128)S(1)}, ...), condition=%wide.region_5.6_spmd.clone, body=%wide.region_2.0_spmd.clone.sunk | while | flops 69044736 | bytes 4037241 | solution.py:83
  157.5 1.3 fusion.42
  161.3 1.3 fusion.42
  163.2 1.3 fusion.42
  165.1 1.3 fusion.42
  167.0 1.3 fusion.42
  170.9 1.3 fusion.42
  172.7 4.9 %pmax.7 = f32[128,4]{0,1:T(4,128)S(1)} all-reduce(f32[128,4]{0,1:T(4,128)S(1)} %get-tuple-element.50), channel_id=1, replica_groups=mesh['lat'=16,'lon'=2] {'lon'}, use_global_device_ids=true, to_apply=%region_6.7 | all-reduce | flops 512 | bytes 4096 | tf_op jit(solution)/shard_map/pmax | solution.py:138
  179.4 7.9 %reduce-scatter.12.cloned.1.call-done = bf16[64,4]{1,0:T(8,128)(2,1)} async-done(((bf16[128,4]{1,0:T(8,128)(2,1)}), bf16[64,4]{1,0:T(8,128)(2,1)}) %reduce-scatter.12.cloned.1.call-update) | async-done | bytes 528
  188.1 11.2 %reduce-scatter.10.cloned.1.call-done = bf16[64,256]{1,0:T(8,128)(2,1)} async-done(((bf16[128,256]{1,0:T(8,128)(2,1)}), bf16[64,256]{1,0:T(8,128)(2,1)}) %reduce-scatter.10.cloned.1.call-update) | async-done | bytes 32784
  200.2 1.7 fusion.14
  (114 shorter events, 25.1 us)
Async XLA Ops:
  6.5 123.6 %copy-start = (bf16[256,256]{1,0:T(8,128)(2,1)S(1)}, bf16[256,256]{1,0:T(8,128)(2,1)}, u32[]{:S(2)}) copy-start(bf16[256,256]{1,0:T(8,128)(2,1)} %param.15) | copy-start | bytes 393220
  6.5 80.8 %reduce-scatter.8.cloned.1.call-start = ((), (), s32[]{:S(2)}) async-start(), calls=%async_computation.4 | async-start | bytes 557056 | tf_op jit(solution)/shard_map/reduce_scatter | solution.py:110
  7.7 5.2 %collective-permute-start = (bf16[73,2,128]{0,2,1:T(8,128)(2,1)S(1)}, bf16[73,2,128]{0,2,1:T(8,128)(2,1)S(1)}, u32[]{:S(2)}, u32[]{:S(2)}) collective-permute-start(bf16[73,2,128]{0,2,1:T(8,128)(2,1)S(1)} %get-tuple-element.127), channel_id=1, source_target_pairs={{0,2},{2,4},{4,6},{6,8},{8,10},{10,12},{12,14},{14,16},{16,18},{18... | collective-permute-start | bytes 112136 | tf_op jit(solution)/shard_map/ppermute | solution.py:19
  10.1 5.3 %collective-permute-start.1 = (bf16[73,2,128]{0,2,1:T(8,128)(2,1)S(1)}, bf16[73,2,128]{0,2,1:T(8,128)(2,1)S(1)}, u32[]{:S(2)}, u32[]{:S(2)}) collective-permute-start(bf16[73,2,128]{0,2,1:T(8,128)(2,1)S(1)} %get-tuple-element.128), channel_id=1, source_target_pairs={{2,0},{4,2},{6,4},{8,6},{10,8},{12,10},{14,12},{16,14},{18,16},{20... | collective-permute-start | bytes 112136 | tf_op jit(solution)/shard_map/ppermute | solution.py:20
  15.4 3.7 %collective-permute-start.2 = (bf16[73,12,1]{0,2,1:T(2,128)(2,1)S(1)}, bf16[73,12,1]{0,2,1:T(2,128)(2,1)S(1)}, u32[]{:S(2)}, u32[]{:S(2)}) collective-permute-start(bf16[73,12,1]{0,2,1:T(2,128)(2,1)S(1)} %pad_maximum_fusion), channel_id=1, source_target_pairs={{0,1},{1,0},{2,3},{3,2},{4,5},{5,4},{6,7},{7,6},{8,9},{9,8},{10,11... | collective-permute-start | bytes 5264 | tf_op jit(solution)/shard_map/ppermute | solution.py:27
  25.4 1.8 copy-start.4
  27.2 1.6 copy-start.2
  28.8 101.3 %all-gather.2.cloned.1.call-start = ((), (), s32[]{:S(2)}) async-start(), calls=%async_computation.3 | async-start | bytes 2228224 | tf_op jit(solution)/shard_map/all_gather | solution.py:124
  29.5 157.7 %reduce-scatter.12.cloned.1.call-start = ((), (), s32[]{:S(2)}) async-start(), calls=%async_computation.6 | async-start | bytes 49152
  135.7 7.1 %copy-start.1 = (bf16[64,64,256]{2,1,0:T(8,128)(2,1)S(1)}, bf16[64,64,256]{2,1,0:T(8,128)(2,1)}, u32[]{:S(2)}) copy-start(bf16[64,64,256]{2,1,0:T(8,128)(2,1)} %all-gather.2.cloned.1.call-done) | copy-start | bytes 6291460
  135.7 7.1 %copy-start.3 = (bf16[256,256]{1,0:T(8,128)(2,1)S(1)}, bf16[256,256]{1,0:T(8,128)(2,1)}, u32[]{:S(2)}) copy-start(bf16[256,256]{1,0:T(8,128)(2,1)} %param.16) | copy-start | bytes 393220
  178.5 20.8 %reduce-scatter.10.cloned.1.call-start = ((), (), s32[]{:S(2)}) async-start(), calls=%async_computation.5 | async-start | bytes 98304
Sparse Core Ops, SparseCore 0:
  28.9 58.3 reduce-scatter.7
  89.7 40.3 all-gather.1
  178.6 8.5 reduce-scatter.11
  189.4 9.8 reduce-scatter.9
where the time goes:
time: 210 us; the launch traced here: 208 us
  waiting for transfers between devices  119 us (57%)
  local copies, waits for them, and re-layouts  37.1 us (18%)
  matrix products  20.3 us (10%)
  between operations  13.4 us (6%)
  blocking collectives  9.73 us (5%)
  starting transfers between devices  5.33 us (3%)
  other arithmetic  3.68 us (2%)
    reduce_scatter x1, waiting for transfers between devices, per_device(): lax.psum_scatter(picked.reshape(slot_count * lax.axis_size('lat'), lon_ti...  57.5 us
    all_gather x1, waiting for transfers between devices, per_device(): piece = lax.all_gather(features, 'lat', axis=0, tiled=True)  37.9 us
    unnamed x6, waiting for transfers between devices  19.8 us
    unnamed x22, local copies, waits for them, and re-layouts  18 us
    dot_general x8, matrix products, absorb(): jnp.einsum('qhd,khd->qhk', queries, block_keys, preferred_element_type=jn...  10.8 us
    another operation x1, local copies, waits for them, and re-layouts, sweep(): values_blocks = values.reshape(blocks, block_len, H, head_size)  7.07 us
    pmax x1, blocking collectives, per_device(): best = lax.pmax(running_max, 'lon')  4.94 us
    all_gather x1, blocking collectives, per_device(): gathered = lax.all_gather(mine, 'lon', axis=1, tiled=True)  4.79 us
  transfers between devices with their start and end apart: 7, of which 6 were waited for; matrix products, arithmetic and copies ran while one was open for 2% of the time, Pallas kernels for 0%

commit v1 on v0

v1 whole, which is shorter than its diff:
```python
import math

import jax
import jax.numpy as jnp
from jax import lax
from jax.experimental import pallas as pl
from jax.experimental.pallas import tpu as pltpu
from jax.sharding import PartitionSpec as P

D = 256
H = 4
AXES = ("lat", "lon")
F32 = jnp.float32
BF16 = jnp.bfloat16


def padded(x, sides, width):
    for axis, dim in sides:
        devices, length = (lax.axis_size(axis), x.shape[dim])
        up = [(i, (i + 1) % devices) for i in range(devices - 1)]
        down = [(j, i) for i, j in up]
        last = lax.slice_in_dim(x, length - width, length, axis=dim)
        leading = lax.slice_in_dim(x, 0, width, axis=dim)
        before = lax.ppermute(last, axis, up)
        after = lax.ppermute(leading, axis, down)
        x = jnp.concatenate([before, x, after], axis=dim)
    return x


def shifted(x, axis, by):
    devices = lax.axis_size(axis)
    return lax.ppermute(x, axis, [(i, (i + by) % devices) for i in range(devices)])


def conv_features(extended, support_rows, conv_weight):
    bands = support_rows.shape[0]
    width = (extended.shape[2] - 1) // 2
    row_index = 2 * jnp.arange(bands, dtype=jnp.int32)[:, None] + support_rows + 2
    picked = jnp.take(extended, row_index, axis=1)
    tapped = jnp.stack(
        [picked[..., column_tap : column_tap + 2 * width : 2] for column_tap in range(3)], axis=3
    )
    patches = jnp.transpose(tapped, (1, 4, 2, 3, 0)).reshape(bands * width, -1)
    raw = jnp.dot(
        patches, conv_weight.reshape(-1, conv_weight.shape[-1]), preferred_element_type=F32
    )
    factor = lax.rsqrt(jnp.mean(raw * raw, axis=-1, keepdims=True) + 1e-06)
    return (raw * factor).astype(BF16).reshape(bands, width, -1)


def absorb(carry, block_keys, block_values, block_area, queries, scale):
    running_max, running_sum, mixed = carry
    scores = (
        jnp.einsum("qhd,khd->qhk", queries, block_keys, preferred_element_type=F32) * scale
        + block_area
    )
    new_max = jnp.maximum(running_max, jnp.max(scores, axis=-1))
    factor = jnp.exp(running_max - new_max)
    weights = jnp.exp(scores - new_max[..., None])
    running_sum = running_sum * factor + jnp.sum(weights, axis=-1)
    update = jnp.einsum(
        "qhk,khd->qhd", weights.astype(BF16), block_values, preferred_element_type=F32
    )
    mixed = mixed * factor[..., None] + update
    return (new_max, running_sum, mixed)


def sweep(carry, keys, values, queries, band_total):
    rows = keys.shape[0]
    lon_tile = keys.shape[1]
    head_size = D // H
    band_block = math.gcd(rows, max(1, 512 // lon_tile))
    blocks = rows // band_block
    block_len = band_block * lon_tile
    keys_blocks = keys.reshape(blocks, block_len, H, head_size)
    values_blocks = values.reshape(blocks, block_len, H, head_size)
    band_index = jnp.arange(rows, dtype=jnp.int32)
    area_rows = jnp.repeat(log_area(band_index, band_total), lon_tile).reshape(blocks, block_len)
    scale = 1.0 / math.sqrt(head_size)

    def step_block(state, inputs):
        return (absorb(state, inputs[0], inputs[1], inputs[2], queries, scale), None)

    result, unused = lax.scan(step_block, carry, (keys_blocks, values_blocks, area_rows))
    return result


def log_area(bands, band_total):
    centre = (bands.astype(F32) + 0.5) * (math.pi / band_total) - math.pi / 2
    return jnp.log(jnp.cos(centre))


def general(state_field, support_rows, window_bands, conv_weight, w_query, w_key, w_value, w_out):
    lat_tile = support_rows.shape[0]
    lon_tile = state_field.shape[2] // 2
    whole_lon = lon_tile * lax.axis_size("lon")
    band_total = lat_tile * lax.axis_size("lat")
    head_size = D // H
    extended = padded(state_field, (("lat", 1),), 2)
    western = shifted(extended[:, :, -1:], "lon", 1)
    extended = jnp.concatenate([western, extended], axis=2)
    features = conv_features(extended, support_rows, conv_weight)
    slot_count = window_bands.shape[0] // lax.axis_size("lat")
    piece = lax.all_gather(features, "lat", axis=0, tiled=True)
    mine = lax.dynamic_slice_in_dim(
        window_bands, lax.axis_index("lat") * slot_count, slot_count, axis=0
    )
    picked = jnp.take(piece, mine, axis=0)
    gathered = lax.all_gather(picked, "lon", axis=1, tiled=True)
    query_count = slot_count * whole_lon
    queries = jnp.dot(gathered.reshape(query_count, D), w_query, preferred_element_type=F32)
    queries = queries.astype(BF16).reshape(query_count, H, head_size)
    initial = (
        jnp.full((query_count, H), -1e30, F32),
        jnp.zeros((query_count, H), F32),
        jnp.zeros((query_count, H, head_size), F32),
    )
    piece_rows = piece.reshape(-1, D)
    keys = jnp.dot(piece_rows, w_key, preferred_element_type=F32).astype(BF16)
    values = jnp.dot(piece_rows, w_value, preferred_element_type=F32).astype(BF16)
    running_max, running_sum, mixed = sweep(
        initial, keys.reshape(piece.shape), values.reshape(piece.shape), queries, band_total
    )
    best = lax.pmax(running_max, "lon")
    factor = jnp.exp(running_max - best)
    scaled_mix = (mixed * factor[..., None]).reshape(slot_count, whole_lon, D)
    scaled_sum = (running_sum * factor).reshape(slot_count, whole_lon, H)
    mix_share, sum_share = (
        lax.psum_scatter(part.astype(BF16), "lon", scatter_dimension=1, tiled=True).astype(F32)
        for part in (scaled_mix, scaled_sum)
    )
    attended = mix_share.reshape(slot_count, lon_tile, H, head_size) / sum_share[..., None]
    attended = attended.astype(BF16).reshape(slot_count * lon_tile, D)
    result = jnp.dot(attended, w_out, preferred_element_type=F32).astype(BF16)
    return result.reshape(slot_count, lon_tile, D)


def exchange(x, lat_mask, lon_mask):
    lats, lons = lax.axis_size("lat"), lax.axis_size("lon")
    pairs = [
        (i * lons + j, (i ^ lat_mask) * lons + (j ^ lon_mask))
        for i in range(lats)
        for j in range(lons)
    ]
    return lax.ppermute(x, AXES, pairs)


def vertical(x, cross):
    lats, lons = lax.axis_size("lat"), lax.axis_size("lon")
    pairs = []
    for i in range(lats):
        for j in range(lons):
            source = i - 1 if j == 0 else i + 1
            if 0 <= source < lats:
                pairs.append((source * lons + (j ^ cross), i * lons + j))
    return lax.ppermute(x, AXES, pairs)


def conv_kernel(
    rows_ref, own_ref, other_ref, edge_ref, edge_other_ref, weight_ref, out_ref,
    strided, taken, patches, weights,
):
    channels, rows, lons = own_ref.shape
    slots, taps = weight_ref.shape[:2]
    deep = taken.shape[1]
    width = lons
    bands = out_ref.shape[0] // width
    tail = jnp.zeros(((deep - channels) * rows, lons), F32)
    for side, ref in enumerate((own_ref, other_ref)):
        strided[side, 0 : channels * rows] = ref[...].astype(F32).reshape(channels * rows, lons)
        strided[side, channels * rows :] = tail
    column = lax.broadcasted_iota(jnp.int32, (2 * lons, taps * width), 0)
    place = lax.broadcasted_iota(jnp.int32, (2 * lons, taps * width), 1)
    wanted = lax.rem(2 * (place % width) + place // width - 1 + 2 * lons, 2 * lons)
    choose = (column == wanted).astype(F32).astype(BF16)
    lines = []
    for row in range(rows):
        lines.append(
            jnp.concatenate(
                [strided[side, pl.ds(row, deep, stride=rows), :] for side in range(2)], axis=1
            )
        )
    edge_rows = edge_ref.shape[0]
    short = jnp.zeros((deep - channels, 2 * lons), F32)
    for row in range(edge_rows):
        line = jnp.concatenate(
            [edge_ref[row].astype(F32), edge_other_ref[row].astype(F32)], axis=1
        )
        lines.append(jnp.concatenate([line, short], axis=0))
    split = jnp.dot(
        jnp.concatenate(lines, axis=0).astype(BF16), choose, preferred_element_type=F32
    ).astype(BF16)
    for row in range(rows):
        taken[edge_rows + row] = split[row * deep : (row + 1) * deep]
    for row in range(edge_rows):
        piece = split[(rows + row) * deep : (rows + row + 1) * deep]
        taken[row] = piece
        taken[edge_rows + rows + row] = piece
    blank = jnp.zeros((deep - channels, weight_ref.shape[3]), BF16)
    for slot in range(slots):
        for band in range(bands):
            line = taken[rows_ref[band, slot]]
            for tap in range(taps):
                at = (slot * taps + tap) * deep
                patches[at : at + deep, band * width : (band + 1) * width] = line[
                    :, tap * width : (tap + 1) * width
                ]
        for tap in range(taps):
            at = (slot * taps + tap) * deep
            weights[at : at + deep] = jnp.concatenate([weight_ref[slot, tap], blank], axis=0)
    raw = lax.dot_general(
        patches[...], weights[...], (((0,), (0,)), ((), ())), preferred_element_type=F32
    )
    factor = lax.rsqrt(jnp.mean(raw * raw, axis=-1, keepdims=True) + 1e-06)
    out_ref[...] = (raw * factor).astype(BF16)


def features_of(own, other, edge, edge_other, row_index, conv_weight):
    channels, rows, lons = own.shape
    slots, taps, _, width = conv_weight.shape
    bands = row_index.shape[0]
    deep = -(-channels // 16) * 16
    vmem = pl.BlockSpec(memory_space=pltpu.VMEM)
    return pl.pallas_call(
        conv_kernel,
        out_shape=jax.ShapeDtypeStruct((bands * lons, width), BF16),
        in_specs=[pl.BlockSpec(memory_space=pltpu.SMEM)] + [vmem] * 5,
        out_specs=vmem,
        scratch_shapes=[
            pltpu.VMEM((2, deep * rows, lons), F32),
            pltpu.VMEM((rows + 2 * edge.shape[0], deep, taps * lons), BF16),
            pltpu.VMEM((slots * taps * deep, bands * lons), BF16),
            pltpu.VMEM((slots * taps * deep, width), BF16),
        ],
        compiler_params=pltpu.CompilerParams(vmem_limit_bytes=32 * 2**20),
        cost_estimate=pl.CostEstimate(
            flops=2 * slots * taps * deep * bands * lons * width,
            bytes_accessed=2 * (conv_weight.size + 2 * own.size),
            transcendentals=0,
        ),
        name="conv",
    )(row_index, own, other, edge, edge_other, conv_weight)


def select_kernel(where_ref, near_ref, far_ref, out_ref, sems):
    slots, rows, _ = out_ref.shape

    def copy(slot, ref):
        start = pl.multiple_of(where_ref[slot, 1], rows)
        return pltpu.make_async_copy(ref.at[pl.ds(start, rows)], out_ref.at[slot], sems.at[slot])

    for slot in range(slots):
        kind = where_ref[slot, 0]

        @pl.when(kind == 0)
        def _():
            copy(slot, near_ref).start()

        @pl.when(kind == 1)
        def _():
            copy(slot, far_ref).start()

        @pl.when(kind == 2)
        def _():
            out_ref[slot] = jnp.zeros(out_ref.shape[1:], out_ref.dtype)

    for slot in range(slots):

        @pl.when(where_ref[slot, 0] != 2)
        def _():
            copy(slot, near_ref).wait()


def selected(where, near, far, rows):
    slots = where.shape[0]
    return pl.pallas_call(
        select_kernel,
        out_shape=jax.ShapeDtypeStruct((slots, rows, near.shape[1]), near.dtype),
        in_specs=[
            pl.BlockSpec(memory_space=pltpu.SMEM),
            pl.BlockSpec(memory_space=pl.ANY),
            pl.BlockSpec(memory_space=pl.ANY),
        ],
        out_specs=pl.BlockSpec(memory_space=pltpu.VMEM),
        scratch_shapes=[pltpu.SemaphoreType.DMA((slots,))],
        name="select",
    )(where, near, far)


def split3(x):
    high = x.astype(BF16).astype(F32)
    middle = (x - high).astype(BF16).astype(F32)
    return high, middle, x - high - middle


def attend_kernel(
    mine_ref, sel_ref, got_ref, near_ref, far_ref, area_ref, wq_ref, wk_ref, wv_ref,
    send_ref, keep_ref, lse_ref, scores, outs, lses,
):
    slots, rows, width = sel_ref.shape
    count = slots * rows
    head_size = width // H
    half = near_ref.shape[0]
    chunk = math.gcd(half, 512)
    token = (sel_ref[...] + got_ref[...]).reshape(count, width)
    query = jnp.dot(token, wq_ref[...], preferred_element_type=F32).astype(BF16).astype(F32)
    query = query * (1.0 / math.sqrt(head_size))
    lane = lax.broadcasted_iota(jnp.int32, (1, width), 1) // head_size
    spread = jnp.concatenate(
        [jnp.where(lane == head, query, 0.0) for head in range(H)], axis=0
    ).astype(BF16)
    turned = lax.dot_general(
        spread, wk_ref[...], (((1,), (1,)), ((), ())), preferred_element_type=F32
    ).astype(BF16)
    parts = [(ref, at) for ref in (near_ref, far_ref) for at in range(0, half, chunk)]
    best = jnp.full((H * count, 128), -jnp.inf, F32)
    for index, (ref, at) in enumerate(parts):
        block = lax.dot_general(
            turned, ref[at : at + chunk], (((1,), (1,)), ((), ())), preferred_element_type=F32
        )
        block = block + area_ref[:, index * chunk : (index + 1) * chunk]
        scores[:, index * chunk : (index + 1) * chunk] = block
        for lanes in range(0, chunk, 128):
            best = jnp.maximum(best, block[:, lanes : lanes + 128])
    top = jnp.max(best, axis=1, keepdims=True)
    total = jnp.zeros((H * count, 128), F32)
    mixed = jnp.zeros((H * count, width), F32)
    for index, (ref, at) in enumerate(parts):
        weight = jnp.exp(scores[:, index * chunk : (index + 1) * chunk] - top)
        for lanes in range(0, chunk, 128):
            total = total + weight[:, lanes : lanes + 128]
        mixed = mixed + jnp.dot(
            weight.astype(BF16), ref[at : at + chunk], preferred_element_type=F32
        )
    total = jnp.sum(total, axis=1, keepdims=True)
    value = jnp.dot((mixed / total).astype(BF16), wv_ref[...], preferred_element_type=F32)
    lse = top + jnp.log(total)
    out = jnp.zeros((count, width), F32)
    stat_lane = lax.broadcasted_iota(jnp.int32, (1, 128), 1)
    stats = jnp.zeros((count, 128), F32)
    for head in range(H):
        out = jnp.where(lane == head, value[head * count : (head + 1) * count], out)
        for order, piece in enumerate(split3(lse[head * count : (head + 1) * count])):
            stats = jnp.where(stat_lane == 3 * head + order, piece, stats)
    outs[...] = out.reshape(outs.shape)
    lses[...] = stats.reshape(lses.shape)
    own = mine_ref[0]
    half_slots = slots // 2
    keep_ref[...] = outs[pl.ds(own * half_slots, half_slots)]
    lse_ref[...] = lses[pl.ds(own * half_slots, half_slots)]
    send_ref[:, :, 0:width] = outs[pl.ds((1 - own) * half_slots, half_slots)].astype(BF16)
    send_ref[:, :, width:] = lses[pl.ds((1 - own) * half_slots, half_slots)].astype(BF16)


def attended(mine, sel, got, near, far, area, w_query, w_key, w_value):
    slots, rows, width = sel.shape
    keys = near.shape[0] + far.shape[0]
    count = slots * rows
    vmem = pl.BlockSpec(memory_space=pltpu.VMEM)
    half_slots = slots // 2
    return pl.pallas_call(
        attend_kernel,
        out_shape=(
            jax.ShapeDtypeStruct((half_slots, rows, width + 128), BF16),
            jax.ShapeDtypeStruct((half_slots, rows, width), F32),
            jax.ShapeDtypeStruct((half_slots, rows, 128), F32),
        ),
        in_specs=[pl.BlockSpec(memory_space=pltpu.SMEM)] + [vmem] * 8,
        out_specs=(vmem, vmem, vmem),
        scratch_shapes=[
            pltpu.VMEM((H * count, keys), F32),
            pltpu.VMEM((slots, rows, width), F32),
            pltpu.VMEM((slots, rows, 128), F32),
        ],
        compiler_params=pltpu.CompilerParams(vmem_limit_bytes=48 * 2**20),
        cost_estimate=pl.CostEstimate(
            flops=4 * H * count * keys * width,
            bytes_accessed=2 * keys * width,
            transcendentals=H * count * keys,
        ),
        name="attend",
    )(mine, sel, got, near, far, area, w_query, w_key, w_value)


def finish_kernel(keep_ref, lse_ref, got_ref, wo_ref, out_ref):
    slots, rows, width = keep_ref.shape
    head_size = width // H
    count = slots * rows
    keep = keep_ref[...].reshape(count, width)
    got = got_ref[:, :, 0:width].astype(F32).reshape(count, width)
    ours = lse_ref[...].reshape(count, 128)
    theirs = got_ref[:, :, width:].astype(F32).reshape(count, 128)
    lane = lax.broadcasted_iota(jnp.int32, (1, width), 1) // head_size
    share = jnp.zeros((count, width), F32)
    for head in range(H):
        own = ours[:, 3 * head : 3 * head + 1] + ours[:, 3 * head + 1 : 3 * head + 2]
        own = own + ours[:, 3 * head + 2 : 3 * head + 3]
        far = theirs[:, 3 * head : 3 * head + 1] + theirs[:, 3 * head + 1 : 3 * head + 2]
        far = far + theirs[:, 3 * head + 2 : 3 * head + 3]
        top = jnp.maximum(own, far)
        own = jnp.exp(own - top)
        far = jnp.exp(far - top)
        share = jnp.where(lane == head, own / (own + far), share)
    mixed = (keep * share + got * (1.0 - share)).astype(BF16)
    result = jnp.dot(mixed, wo_ref[...], preferred_element_type=F32).astype(BF16)
    out_ref[...] = result.reshape(out_ref.shape)


def finished(keep, lse, got, w_out):
    vmem = pl.BlockSpec(memory_space=pltpu.VMEM)
    return pl.pallas_call(
        finish_kernel,
        out_shape=jax.ShapeDtypeStruct(keep.shape, BF16),
        in_specs=[vmem] * 4,
        out_specs=vmem,
        name="finish",
    )(keep, lse, got, w_out)


def gathered(block, masks):
    blocks = {(0, 0): block}
    for size in range(1, len(masks) + 1):
        for start in range(len(masks)):
            if size == len(masks) and start > 0:
                break
            chosen = [masks[(start + k) % len(masks)] for k in range(size)]
            key = (0, 0)
            for mask in chosen:
                key = (key[0] ^ mask[0], key[1] ^ mask[1])
            step = chosen[-1]
            before = (key[0] ^ step[0], key[1] ^ step[1])
            if key not in blocks:
                blocks[key] = exchange(blocks[before], *step)
    return blocks


def halves(state_field, support_rows, window_bands, conv_weight, w_query, w_key, w_value, w_out):
    lats = lax.axis_size("lat")
    lat, lon = lax.axis_index("lat"), lax.axis_index("lon")
    channels, rows, lons = state_field.shape
    lat_tile = support_rows.shape[0]
    bands = lat_tile // 2
    lon_tile = lons // 2
    band_total = lat_tile * lats
    half = lats // 2

    other = exchange(state_field, 0, 1)
    top = jnp.transpose(state_field[:, :2], (1, 0, 2))
    bottom = jnp.transpose(state_field[:, rows - 2 :], (1, 0, 2))
    edge = vertical(jnp.where(lon == 0, bottom, top), 0)
    edge_other = vertical(jnp.where(lon == 0, top, bottom), 1)
    row_index = 2 * jnp.arange(lat_tile, dtype=jnp.int32)[:, None] + support_rows + 2
    row_index = lax.dynamic_slice_in_dim(row_index, lon * bands, bands, axis=0)
    features = features_of(state_field, other, edge, edge_other, row_index, conv_weight)

    masks = [(0, 1)] + [(1 << k, 0) for k in range(1, half.bit_length() - 1)]
    blocks = gathered(features, masks)
    order = [(i, j) for i in range(0, half, 2) for j in range(2)]
    near = jnp.concatenate([blocks[key] for key in order], axis=0)
    far = exchange(near, 1, 0)

    size = bands * lons
    slot_count = window_bands.shape[0] // lats
    pair_slots = jnp.concatenate(
        [(lat % half + k * half) * slot_count + jnp.arange(slot_count) for k in range(2)]
    )
    wanted = window_bands[pair_slots]
    owner = wanted // lat_tile
    owner_lon = (wanted % lat_tile) // bands
    apart = (owner ^ lat) % half
    place = ((apart - apart % 2) + (owner_lon ^ lon)) * size
    place = place + (wanted % bands) * lons + (owner_lon ^ lon) * lon_tile
    kind = jnp.where(owner // half == lat // half, apart % 2, 2)
    where = jnp.stack([kind, place], axis=1).astype(jnp.int32)
    sel = selected(where, near, far, lon_tile)
    got = exchange(sel, half, 0)

    masks_lat = jnp.array([i + core for core in range(2) for i, j in order], jnp.int32)
    masks_lon = jnp.array([j for core in range(2) for i, j in order], jnp.int32)
    first = (lat ^ masks_lat) * lat_tile + (lon ^ masks_lon) * bands
    key_band = first[:, None] + jnp.arange(bands, dtype=jnp.int32)[None, :]
    area = jnp.repeat(log_area(key_band.reshape(-1), band_total), lons)[None, :]
    mine = (lat // half).astype(jnp.int32).reshape(1)
    send, keep, lse = attended(mine, sel, got, near, far, area, w_query, w_key, w_value)
    return finished(keep, lse, exchange(send, half, 0), w_out)


def solution(mesh):
    lats, lons = mesh.shape["lat"], mesh.shape["lon"]
    paired = lons == 2 and lats >= 4 and lats & (lats - 1) == 0
    return jax.shard_map(
        halves if paired else general,
        mesh=mesh,
        in_specs=(P(None, "lat", "lon"), P("lat", None), P(), P(), P(), P(), P(), P()),
        out_specs=P("lat", "lon", None),
        check_vma=False,
    )
```

time: 210 us -> 63.7 us (0.30)
  waiting for transfers between devices: 119 us -> 16.5 us
  local copies, waits for them, and re-layouts: 37.1 us -> 9.31 us
  matrix products: 20.3 us -> 0 us
  starting transfers between devices: 5.33 us -> 24.4 us
  between operations: 13.4 us -> 0.24 us
  Pallas kernels: 0 us -> 11.8 us
  blocking collectives: 9.73 us -> 0 us
  other arithmetic: 3.68 us -> 1.04 us
    reduce_scatter x1 -> x0, waiting for transfers between devices: 57.5 us -> none  [per_device(): lax.psum_scatter(picked.reshape(slot_count * lax.axis_size('lat'), lon_ti...]
    all_gather x1 -> x0, waiting for transfers between devices: 37.9 us -> none  [per_device(): piece = lax.all_gather(features, 'lat', axis=0, tiled=True)]
    dot_general x22 -> x0, matrix products: 20.3 us -> none  [the longest x8 10.8 us: absorb(): jnp.einsum('qhd,khd->qhk', queries, block_keys, preferred_element_type=jn...]
    unnamed x6 -> x0, waiting for transfers between devices: 19.8 us -> none
    ppermute x3 -> x13, starting transfers between devices: 5.21 us -> 24.4 us  [the longest x11 22.3 us: exchange(): return lax.ppermute(x, AXES, pairs)]
    ppermute x3 -> x13, waiting for transfers between devices: 3.34 us -> 16.5 us  [the longest x11 16.4 us: exchange(): return lax.ppermute(x, AXES, pairs)]
    pallas_call x0 -> x4, Pallas kernels: none -> 11.8 us  [the longest x1 6.01 us: attended(): pl.pallas_call(attend_kernel, out_shape=(jax.ShapeDtypeStruct((half_slots...]
    unnamed x22 -> x41, local copies, waits for them, and re-layouts: 18 us -> 7.28 us
  transfers between devices with their start and end apart: 7 -> 13, of which waited for: 6 -> 11; matrix products, arithmetic and copies ran while one was open for 2% -> 5% of each run, Pallas kernels for 0% -> 0%
where the time goes in v1:
time: 63.7 us; the launch traced here: 63.2 us
  starting transfers between devices  24.4 us (38%)
  waiting for transfers between devices  16.5 us (26%)
  Pallas kernels  11.8 us (19%)
  local copies, waits for them, and re-layouts  9.31 us (15%)
  other arithmetic  1.04 us (2%)
    ppermute x11, starting transfers between devices, exchange(): return lax.ppermute(x, AXES, pairs)  22.3 us
    ppermute x11, waiting for transfers between devices, exchange(): return lax.ppermute(x, AXES, pairs)  16.4 us
    unnamed x41, local copies, waits for them, and re-layouts  7.28 us
    pallas_call x1, Pallas kernels, attended(): pl.pallas_call(attend_kernel, out_shape=(jax.ShapeDtypeStruct((half_slots...  6.01 us
    ppermute x2, starting transfers between devices, vertical(): return lax.ppermute(x, AXES, pairs)  2.12 us
    pallas_call x1, Pallas kernels, selected(): pl.pallas_call(select_kernel, out_shape=jax.ShapeDtypeStruct((slots, rows...  2.09 us
    pallas_call x1, Pallas kernels, finished(): pl.pallas_call(finish_kernel, out_shape=jax.ShapeDtypeStruct(keep.shape,...  1.94 us
    pallas_call x1, Pallas kernels, features_of(): pl.pallas_call(conv_kernel, out_shape=jax.ShapeDtypeStruct((bands * lons,...  1.74 us
  transfers between devices with their start and end apart: 13, of which 11 were waited for; matrix products, arithmetic and copies ran while one was open for 5% of the time, Pallas kernels for 0%

profile of v1, /device:TPU:0, one launch (start us, length us, event | category | flops | bytes accessed | tf_op | source)
XLA Modules:
  0.0 63.2 jit_solution(997989875987549374)
XLA Ops:
  0.0 2.9 %collective-permute-start = (bf16[73,8,128]{2,1,0:T(8,128)(2,1)}, bf16[73,8,128]{2,1,0:T(8,128)(2,1)S(1)}, u32[]{:S(2)}, u32[]{:S(2)}) collective-permute-start(bf16[73,8,128]{2,1,0:T(8,128)(2,1)} %own_ref.1), channel_id=1, source_target_pairs={{0,1},{1,0},{2,3},{3,2},{4,5},{5,4},{6,7},{7,6},{8,9},{9,8},{10,11... | collective-permute-start | bytes 448520 | tf_op jit(solution)/shard_map/ppermute | solution.py:145
  2.9 1.1 %fusion.4 = (bf16[73,2,128]{2,1,0:T(2,128)(2,1)S(1)}, bf16[73,2,128]{2,1,0:T(2,128)(2,1)S(1)}) fusion(bf16[73,8,128]{2,1,0:T(8,128)(2,1)} %own_ref.1), kind=kLoop, calls=%fused_computation.46 | loop fusion | bytes 149504 | tf_op jit(solution)/shard_map/slice | solution.py:449
  4.1 1.5 %collective-permute-start.1 = (bf16[2,73,128]{2,1,0:T(8,128)(2,1)S(1)}, bf16[2,73,128]{2,1,0:T(8,128)(2,1)S(1)}, u32[]{:S(2)}, u32[]{:S(2)}) collective-permute-start(bf16[2,73,128]{2,1,0:T(8,128)(2,1)S(1)} %get-tuple-element.16), channel_id=1, source_target_pairs={{3,1},{0,2},{5,3},{2,4},{7,5},{4,6},{9,7},{6,8},{11,9},{8,10},{13,... | collective-permute-start | bytes 112136 | tf_op jit(solution)/shard_map/ppermute | solution.py:156
  7.0 1.1 %copy-done.5 = bf16[5,3,73,256]{3,2,1,0:T(8,128)(2,1)S(1)} copy-done((bf16[5,3,73,256]{3,2,1,0:T(8,128)(2,1)S(1)}, bf16[5,3,73,256]{3,2,1,0:T(8,128)(2,1)}, u32[]{:S(2)}) %copy-start.5) | copy-done | bytes 560664
  8.1 1.7 %conv.1 = bf16[256,256]{1,0:T(8,128)(2,1)S(1)} custom-call(s32[2,5]{1,0:T(2,128)S(1)} %constant_dynamic-slice_fusion.rows_ref, bf16[73,8,128]{2,1,0:T(8,128)(2,1)S(1)} %copy-done.6, bf16[73,8,128]{2,1,0:T(8,128)(2,1)S(1)} %collective-permute-done.other_ref, bf16[2,73,128]{2,1,0:T(8,128)(2,1)S(1)} %collective-permute-done.1.edge_ref, ...), custom_call_target="tpu_custom_call" | custom-call | flops 157286400 | bytes 859648 | tf_op jit(solution)/shard_map/conv/pallas_call | solution.py:224
  9.9 5.9 %collective-permute-start.3 = (bf16[256,256]{1,0:T(8,128)(2,1)S(1)}, bf16[256,256]{1,0:T(8,128)(2,1)S(1)}, u32[]{:S(2)}, u32[]{:S(2)}) collective-permute-start(bf16[256,256]{1,0:T(8,128)(2,1)S(1)} %conv.1), channel_id=1, source_target_pairs={{0,1},{1,0},{2,3},{3,2},{4,5},{5,4},{6,7},{7,6},{8,9},{9,8},{10,11... | collective-permute-start | bytes 393224 | tf_op jit(solution)/shard_map/ppermute | solution.py:145
  15.8 1.5 %collective-permute-start.4 = (bf16[256,256]{1,0:T(8,128)(2,1)S(1)}, bf16[256,256]{1,0:T(8,128)(2,1)S(1)}, u32[]{:S(2)}, u32[]{:S(2)}) collective-permute-start(bf16[256,256]{1,0:T(8,128)(2,1)S(1)} %conv.1), channel_id=1, source_target_pairs={{0,4},{1,5},{2,6},{3,7},{4,0},{5,1},{6,2},{7,3},{8,12},{9,13},{10,... | collective-permute-start | bytes 393224 | tf_op jit(solution)/shard_map/ppermute | solution.py:145
  17.3 1.7 %collective-permute-start.6 = (bf16[256,256]{1,0:T(8,128)(2,1)S(1)}, bf16[256,256]{1,0:T(8,128)(2,1)S(1)}, u32[]{:S(2)}, u32[]{:S(2)}) collective-permute-start(bf16[256,256]{1,0:T(8,128)(2,1)S(1)} %conv.1), channel_id=1, source_target_pairs={{0,8},{1,9},{2,10},{3,11},{4,12},{5,13},{6,14},{7,15},{8,0},{9,1},... | collective-permute-start | bytes 393224 | tf_op jit(solution)/shard_map/ppermute | solution.py:145
  19.1 3.7 %collective-permute-start.5 = (bf16[256,256]{1,0:T(8,128)(2,1)S(1)}, bf16[256,256]{1,0:T(8,128)(2,1)S(1)}, u32[]{:S(2)}, u32[]{:S(2)}) collective-permute-start(bf16[256,256]{1,0:T(8,128)(2,1)S(1)} %collective-permute-done.3), channel_id=1, source_target_pairs={{0,4},{1,5},{2,6},{3,7},{4,0},{5,1},{6,2},{7,3},{8,12},{9,13},{10,... | collective-permute-start | bytes 393224 | tf_op jit(solution)/shard_map/ppermute | solution.py:145
  24.3 1.6 %collective-permute-start.8 = (bf16[256,256]{1,0:T(8,128)(2,1)S(1)}, bf16[256,256]{1,0:T(8,128)(2,1)S(1)}, u32[]{:S(2)}, u32[]{:S(2)}) collective-permute-start(bf16[256,256]{1,0:T(8,128)(2,1)S(1)} %collective-permute-done.4), channel_id=1, source_target_pairs={{0,8},{1,9},{2,10},{3,11},{4,12},{5,13},{6,14},{7,15},{8,0},{9,1},... | collective-permute-start | bytes 393224 | tf_op jit(solution)/shard_map/ppermute | solution.py:145
  26.3 1.8 %collective-permute-start.9 = (bf16[256,256]{1,0:T(8,128)(2,1)S(1)}, bf16[256,256]{1,0:T(8,128)(2,1)S(1)}, u32[]{:S(2)}, u32[]{:S(2)}) collective-permute-start(bf16[256,256]{1,0:T(8,128)(2,1)S(1)} %collective-permute-done.5), channel_id=1, source_target_pairs={{0,8},{1,9},{2,10},{3,11},{4,12},{5,13},{6,14},{7,15},{8,0},{9,1},... | collective-permute-start | bytes 393224 | tf_op jit(solution)/shard_map/ppermute | solution.py:145
  28.7 1.6 %collective-permute-done.8 = bf16[256,256]{1,0:T(8,128)(2,1)S(1)} collective-permute-done((bf16[256,256]{1,0:T(8,128)(2,1)S(1)}, bf16[256,256]{1,0:T(8,128)(2,1)S(1)}, u32[]{:S(2)}, u32[]{:S(2)}) %collective-permute-start.8) | collective-permute-done | bytes 131104 | tf_op jit(solution)/shard_map/ppermute | solution.py:145
  30.3 1.7 %collective-permute-done.9 = bf16[256,256]{1,0:T(8,128)(2,1)S(1)} collective-permute-done((bf16[256,256]{1,0:T(8,128)(2,1)S(1)}, bf16[256,256]{1,0:T(8,128)(2,1)S(1)}, u32[]{:S(2)}, u32[]{:S(2)}) %collective-permute-start.9) | collective-permute-done | bytes 131104 | tf_op jit(solution)/shard_map/ppermute | solution.py:145
  33.8 1.0 %collective-permute-done.10.far_ref = bf16[2048,256]{1,0:T(8,128)(2,1)S(1)} collective-permute-done((bf16[2048,256]{1,0:T(8,128)(2,1)S(1)}, bf16[2048,256]{1,0:T(8,128)(2,1)S(1)}, u32[]{:S(2)}, u32[]{:S(2)}) %collective-permute-start.10) | collective-permute-done | bytes 1048608 | tf_op jit(solution)/shard_map/ppermute | solution.py:145
  34.8 1.0 %copy-done.3 = bf16[2048,256]{1,0:T(8,128)(2,1)} copy-done((bf16[2048,256]{1,0:T(8,128)(2,1)}, bf16[2048,256]{1,0:T(8,128)(2,1)S(1)}, u32[]{:S(2)}) %copy-start.3) | copy-done | bytes 1048600
  35.7 2.1 %select.154.sel_ref = bf16[2,64,256]{2,1,0:T(8,128)(2,1)} custom-call(s32[2,2]{1,0:T(2,128)} %pad_add_fusion.where_ref, bf16[2048,256]{1,0:T(8,128)(2,1)} %copy-done.1, bf16[2048,256]{1,0:T(8,128)(2,1)} %copy-done.3), custom_call_target="tpu_custom_call" | custom-call | tf_op jit(solution)/shard_map/select/pallas_call | solution.py:276
  37.9 1.5 %collective-permute-start.11 = (bf16[2,64,256]{2,1,0:T(8,128)(2,1)}, bf16[2,64,256]{2,1,0:T(8,128)(2,1)S(1)}, u32[]{:S(2)}, u32[]{:S(2)}) collective-permute-start(bf16[2,64,256]{2,1,0:T(8,128)(2,1)} %select.154.sel_ref), channel_id=1, source_target_pairs={{0,16},{1,17},{2,18},{3,19},{4,20},{5,21},{6,22},{7,23},{8,24},{9,... | collective-permute-start | bytes 196616 | tf_op jit(solution)/shard_map/ppermute | solution.py:145
  39.5 5.0 %collective-permute-done.11.got_ref = bf16[2,64,256]{2,1,0:T(8,128)(2,1)S(1)} collective-permute-done((bf16[2,64,256]{2,1,0:T(8,128)(2,1)}, bf16[2,64,256]{2,1,0:T(8,128)(2,1)S(1)}, u32[]{:S(2)}, u32[]{:S(2)}) %collective-permute-start.11) | collective-permute-done | bytes 65568 | tf_op jit(solution)/shard_map/ppermute | solution.py:145
  44.6 1.2 %copy-done.2 = bf16[2048,256]{1,0:T(8,128)(2,1)S(1)} copy-done((bf16[2048,256]{1,0:T(8,128)(2,1)S(1)}, bf16[2048,256]{1,0:T(8,128)(2,1)}, u32[]{:S(2)}) %copy-start.2) | copy-done | bytes 1048600
  45.9 1.2 %copy-done.4 = bf16[2048,256]{1,0:T(8,128)(2,1)S(1)} copy-done((bf16[2048,256]{1,0:T(8,128)(2,1)S(1)}, bf16[2048,256]{1,0:T(8,128)(2,1)}, u32[]{:S(2)}) %copy-start.4) | copy-done | bytes 1048600
  47.9 6.0 %attend.1 = (bf16[1,64,384]{2,1,0:T(8,128)(2,1)S(1)}, f32[1,64,256]{2,1,0:T(8,128)S(1)}, f32[1,64,128]{2,1,0:T(8,128)S(1)}) custom-call(s32[1]{0:T(128)} %bitcast.mine_ref, bf16[2,64,256]{2,1,0:T(8,128)(2,1)S(1)} %copy-done.7, bf16[2,64,256]{2,1,0:T(8,128)(2,1)S(1)} %collective-permute-done.11.got_ref, bf16[2048,256]{1,0:T(8,128)(2,1)S(1)} %copy-done.2, ...), custom_call_target="tpu_custom_call" | custom-call | flops 2147483648 | bytes 2097152 | tf_op jit(solution)/shard_map/attend/pallas_call | solution.py:361
  55.2 0.8 %collective-permute-start.12 = (bf16[1,64,384]{2,1,0:T(8,128)(2,1)S(1)}, bf16[1,64,384]{2,1,0:T(8,128)(2,1)S(1)}, u32[]{:S(2)}, u32[]{:S(2)}) collective-permute-start(bf16[1,64,384]{2,1,0:T(8,128)(2,1)S(1)} %get-tuple-element.10), channel_id=1, source_target_pairs={{0,16},{1,17},{2,18},{3,19},{4,20},{5,21},{6,22},{7,23},{8,24},{9,... | collective-permute-start | bytes 147464 | tf_op jit(solution)/shard_map/ppermute | solution.py:145
  56.0 4.7 %collective-permute-done.12.got_ref = bf16[1,64,384]{2,1,0:T(8,128)(2,1)S(1)} collective-permute-done((bf16[1,64,384]{2,1,0:T(8,128)(2,1)S(1)}, bf16[1,64,384]{2,1,0:T(8,128)(2,1)S(1)}, u32[]{:S(2)}, u32[]{:S(2)}) %collective-permute-start.12) | collective-permute-done | bytes 49184 | tf_op jit(solution)/shard_map/ppermute | solution.py:145
  61.3 1.9 %finish.1 = bf16[1,64,256]{2,1,0:T(8,128)(2,1)} custom-call(f32[1,64,256]{2,1,0:T(8,128)} %copy-done.8, f32[1,64,128]{2,1,0:T(8,128)} %copy-done.9, bf16[1,64,384]{2,1,0:T(8,128)(2,1)} %copy-done.13, bf16[256,256]{1,0:T(8,128)(2,1)} %wo_ref.1), custom_call_target="tpu_custom_call" | custom-call | tf_op jit(solution)/shard_map/finish/pallas_call | solution.py:411
  (64 shorter events, 8.8 us)
Async XLA Ops:
  0.0 32.3 %copy-start = (s32[16]{0:T(128)S(1)}, s32[16]{0:T(128)}, u32[]{:S(2)}) copy-start(s32[16]{0:T(128)} %param.12) | copy-start | bytes 196
  0.0 7.0 %collective-permute-start = (bf16[73,8,128]{2,1,0:T(8,128)(2,1)}, bf16[73,8,128]{2,1,0:T(8,128)(2,1)S(1)}, u32[]{:S(2)}, u32[]{:S(2)}) collective-permute-start(bf16[73,8,128]{2,1,0:T(8,128)(2,1)} %own_ref.1), channel_id=1, source_target_pairs={{0,1},{1,0},{2,3},{3,2},{4,5},{5,4},{6,7},{7,6},{8,9},{9,8},{10,11... | collective-permute-start | bytes 448520 | tf_op jit(solution)/shard_map/ppermute | solution.py:145
  2.9 4.1 %copy-start.6 = (bf16[73,8,128]{2,1,0:T(8,128)(2,1)S(1)}, bf16[73,8,128]{2,1,0:T(8,128)(2,1)}, u32[]{:S(2)}) copy-start(bf16[73,8,128]{2,1,0:T(8,128)(2,1)} %own_ref.1) | copy-start | bytes 448516
  4.1 2.2 %copy-start.14 = (s32[4,5]{1,0:T(4,128)S(1)}, s32[4,5]{1,0:T(4,128)}, u32[]{:S(2)}) copy-start(s32[4,5]{1,0:T(4,128)} %param.11) | copy-start | bytes 244
  4.1 2.3 %collective-permute-start.1 = (bf16[2,73,128]{2,1,0:T(8,128)(2,1)S(1)}, bf16[2,73,128]{2,1,0:T(8,128)(2,1)S(1)}, u32[]{:S(2)}, u32[]{:S(2)}) collective-permute-start(bf16[2,73,128]{2,1,0:T(8,128)(2,1)S(1)} %get-tuple-element.16), channel_id=1, source_target_pairs={{3,1},{0,2},{5,3},{2,4},{7,5},{4,6},{9,7},{6,8},{11,9},{8,10},{13,... | collective-permute-start | bytes 112136 | tf_op jit(solution)/shard_map/ppermute | solution.py:156
  5.6 0.9 %collective-permute-start.2 = (bf16[2,73,128]{2,1,0:T(8,128)(2,1)S(1)}, bf16[2,73,128]{2,1,0:T(8,128)(2,1)S(1)}, u32[]{:S(2)}, u32[]{:S(2)}) collective-permute-start(bf16[2,73,128]{2,1,0:T(8,128)(2,1)S(1)} %get-tuple-element.15), channel_id=1, source_target_pairs={{2,1},{1,2},{4,3},{3,4},{6,5},{5,6},{8,7},{7,8},{10,9},{9,10},{12,... | collective-permute-start | bytes 112136 | tf_op jit(solution)/shard_map/ppermute | solution.py:156
  7.0 1.1 %copy-start.5 = (bf16[5,3,73,256]{3,2,1,0:T(8,128)(2,1)S(1)}, bf16[5,3,73,256]{3,2,1,0:T(8,128)(2,1)}, u32[]{:S(2)}) copy-start(bf16[5,3,73,256]{3,2,1,0:T(8,128)(2,1)} %weight_ref.1) | copy-start | bytes 1681924
  9.9 9.2 %collective-permute-start.3 = (bf16[256,256]{1,0:T(8,128)(2,1)S(1)}, bf16[256,256]{1,0:T(8,128)(2,1)S(1)}, u32[]{:S(2)}, u32[]{:S(2)}) collective-permute-start(bf16[256,256]{1,0:T(8,128)(2,1)S(1)} %conv.1), channel_id=1, source_target_pairs={{0,1},{1,0},{2,3},{3,2},{4,5},{5,4},{6,7},{7,6},{8,9},{9,8},{10,11... | collective-permute-start | bytes 393224 | tf_op jit(solution)/shard_map/ppermute | solution.py:145
  15.8 8.5 %collective-permute-start.4 = (bf16[256,256]{1,0:T(8,128)(2,1)S(1)}, bf16[256,256]{1,0:T(8,128)(2,1)S(1)}, u32[]{:S(2)}, u32[]{:S(2)}) collective-permute-start(bf16[256,256]{1,0:T(8,128)(2,1)S(1)} %conv.1), channel_id=1, source_target_pairs={{0,4},{1,5},{2,6},{3,7},{4,0},{5,1},{6,2},{7,3},{8,12},{9,13},{10,... | collective-permute-start | bytes 393224 | tf_op jit(solution)/shard_map/ppermute | solution.py:145
  17.3 6.2 %collective-permute-start.6 = (bf16[256,256]{1,0:T(8,128)(2,1)S(1)}, bf16[256,256]{1,0:T(8,128)(2,1)S(1)}, u32[]{:S(2)}, u32[]{:S(2)}) collective-permute-start(bf16[256,256]{1,0:T(8,128)(2,1)S(1)} %conv.1), channel_id=1, source_target_pairs={{0,8},{1,9},{2,10},{3,11},{4,12},{5,13},{6,14},{7,15},{8,0},{9,1},... | collective-permute-start | bytes 393224 | tf_op jit(solution)/shard_map/ppermute | solution.py:145
  19.1 7.2 %collective-permute-start.5 = (bf16[256,256]{1,0:T(8,128)(2,1)S(1)}, bf16[256,256]{1,0:T(8,128)(2,1)S(1)}, u32[]{:S(2)}, u32[]{:S(2)}) collective-permute-start(bf16[256,256]{1,0:T(8,128)(2,1)S(1)} %collective-permute-done.3), channel_id=1, source_target_pairs={{0,4},{1,5},{2,6},{3,7},{4,0},{5,1},{6,2},{7,3},{8,12},{9,13},{10,... | collective-permute-start | bytes 393224 | tf_op jit(solution)/shard_map/ppermute | solution.py:145
  23.4 5.3 %collective-permute-start.7 = (bf16[256,256]{1,0:T(8,128)(2,1)S(1)}, bf16[256,256]{1,0:T(8,128)(2,1)S(1)}, u32[]{:S(2)}, u32[]{:S(2)}) collective-permute-start(bf16[256,256]{1,0:T(8,128)(2,1)S(1)} %collective-permute-done.6), channel_id=1, source_target_pairs={{0,1},{1,0},{2,3},{3,2},{4,5},{5,4},{6,7},{7,6},{8,9},{9,8},{10,11... | collective-permute-start | bytes 393224 | tf_op jit(solution)/shard_map/ppermute | solution.py:145
  24.3 6.0 %collective-permute-start.8 = (bf16[256,256]{1,0:T(8,128)(2,1)S(1)}, bf16[256,256]{1,0:T(8,128)(2,1)S(1)}, u32[]{:S(2)}, u32[]{:S(2)}) collective-permute-start(bf16[256,256]{1,0:T(8,128)(2,1)S(1)} %collective-permute-done.4), channel_id=1, source_target_pairs={{0,8},{1,9},{2,10},{3,11},{4,12},{5,13},{6,14},{7,15},{8,0},{9,1},... | collective-permute-start | bytes 393224 | tf_op jit(solution)/shard_map/ppermute | solution.py:145
  26.3 5.7 %collective-permute-start.9 = (bf16[256,256]{1,0:T(8,128)(2,1)S(1)}, bf16[256,256]{1,0:T(8,128)(2,1)S(1)}, u32[]{:S(2)}, u32[]{:S(2)}) collective-permute-start(bf16[256,256]{1,0:T(8,128)(2,1)S(1)} %collective-permute-done.5), channel_id=1, source_target_pairs={{0,8},{1,9},{2,10},{3,11},{4,12},{5,13},{6,14},{7,15},{8,0},{9,1},... | collective-permute-start | bytes 393224 | tf_op jit(solution)/shard_map/ppermute | solution.py:145
  32.0 2.7 %copy-start.1 = (bf16[2048,256]{1,0:T(8,128)(2,1)}, bf16[2048,256]{1,0:T(8,128)(2,1)S(1)}, u32[]{:S(2)}) copy-start(bf16[2048,256]{1,0:T(8,128)(2,1)S(1)} %constant_dynamic-update-slice_fusion.near_ref) | copy-start | bytes 3145732
  32.1 2.7 %collective-permute-start.10 = (bf16[2048,256]{1,0:T(8,128)(2,1)S(1)}, bf16[2048,256]{1,0:T(8,128)(2,1)S(1)}, u32[]{:S(2)}, u32[]{:S(2)}) collective-permute-start(bf16[2048,256]{1,0:T(8,128)(2,1)S(1)} %constant_dynamic-update-slice_fusion.near_ref), channel_id=1, source_target_pairs={{0,2},{1,3},{2,0},{3,1},{4,6},{5,7},{6,4},{7,5},{8,10},{9,11},{10,... | collective-permute-start | bytes 3145736 | tf_op jit(solution)/shard_map/ppermute | solution.py:145
  33.8 10.9 %copy-start.10 = (bf16[256,256]{1,0:T(8,128)(2,1)S(1)}, bf16[256,256]{1,0:T(8,128)(2,1)}, u32[]{:S(2)}) copy-start(bf16[256,256]{1,0:T(8,128)(2,1)} %wq_ref.1) | copy-start | bytes 393220
  33.8 10.9 %copy-start.11 = (bf16[256,256]{1,0:T(8,128)(2,1)S(1)}, bf16[256,256]{1,0:T(8,128)(2,1)}, u32[]{:S(2)}) copy-start(bf16[256,256]{1,0:T(8,128)(2,1)} %wk_ref.1) | copy-start | bytes 393220
  33.8 10.8 %copy-start.12 = (bf16[256,256]{1,0:T(8,128)(2,1)S(1)}, bf16[256,256]{1,0:T(8,128)(2,1)}, u32[]{:S(2)}) copy-start(bf16[256,256]{1,0:T(8,128)(2,1)} %wv_ref.1) | copy-start | bytes 393220
  34.8 1.0 %copy-start.3 = (bf16[2048,256]{1,0:T(8,128)(2,1)}, bf16[2048,256]{1,0:T(8,128)(2,1)S(1)}, u32[]{:S(2)}) copy-start(bf16[2048,256]{1,0:T(8,128)(2,1)S(1)} %collective-permute-done.10.far_ref) | copy-start | bytes 3145732
  37.9 6.7 %collective-permute-start.11 = (bf16[2,64,256]{2,1,0:T(8,128)(2,1)}, bf16[2,64,256]{2,1,0:T(8,128)(2,1)S(1)}, u32[]{:S(2)}, u32[]{:S(2)}) collective-permute-start(bf16[2,64,256]{2,1,0:T(8,128)(2,1)} %select.154.sel_ref), channel_id=1, source_target_pairs={{0,16},{1,17},{2,18},{3,19},{4,20},{5,21},{6,22},{7,23},{8,24},{9,... | collective-permute-start | bytes 196616 | tf_op jit(solution)/shard_map/ppermute | solution.py:145
  44.6 1.2 %copy-start.2 = (bf16[2048,256]{1,0:T(8,128)(2,1)S(1)}, bf16[2048,256]{1,0:T(8,128)(2,1)}, u32[]{:S(2)}) copy-start(bf16[2048,256]{1,0:T(8,128)(2,1)} %copy-done.1) | copy-start | bytes 3145732
  45.9 1.2 %copy-start.4 = (bf16[2048,256]{1,0:T(8,128)(2,1)S(1)}, bf16[2048,256]{1,0:T(8,128)(2,1)}, u32[]{:S(2)}) copy-start(bf16[2048,256]{1,0:T(8,128)(2,1)} %copy-done.3) | copy-start | bytes 3145732
  55.2 5.5 %collective-permute-start.12 = (bf16[1,64,384]{2,1,0:T(8,128)(2,1)S(1)}, bf16[1,64,384]{2,1,0:T(8,128)(2,1)S(1)}, u32[]{:S(2)}, u32[]{:S(2)}) collective-permute-start(bf16[1,64,384]{2,1,0:T(8,128)(2,1)S(1)} %get-tuple-element.10), channel_id=1, source_target_pairs={{0,16},{1,17},{2,18},{3,19},{4,20},{5,21},{6,22},{7,23},{8,24},{9,... | collective-permute-start | bytes 147464 | tf_op jit(solution)/shard_map/ppermute | solution.py:145
  (6 other events, 4.0 us)

commit v2 on v1

--- a/solution.py
+++ b/solution.py
@@ -232,7 +232,7 @@
             pltpu.VMEM((slots * taps * deep, bands * lons), BF16),
             pltpu.VMEM((slots * taps * deep, width), BF16),
         ],
-        compiler_params=pltpu.CompilerParams(vmem_limit_bytes=32 * 2**20),
+        compiler_params=pltpu.CompilerParams(vmem_limit_bytes=12 * 2**20),
         cost_estimate=pl.CostEstimate(
             flops=2 * slots * taps * deep * bands * lons * width,
             bytes_accessed=2 * (conv_weight.size + 2 * own.size),
@@ -242,47 +242,34 @@
     )(row_index, own, other, edge, edge_other, conv_weight)
 
 
-def select_kernel(where_ref, near_ref, far_ref, out_ref, sems):
+def select_kernel(where_ref, near_ref, far_ref, out_ref):
     slots, rows, _ = out_ref.shape
-
-    def copy(slot, ref):
-        start = pl.multiple_of(where_ref[slot, 1], rows)
-        return pltpu.make_async_copy(ref.at[pl.ds(start, rows)], out_ref.at[slot], sems.at[slot])
-
     for slot in range(slots):
         kind = where_ref[slot, 0]
+        start = pl.multiple_of(where_ref[slot, 1], rows)
 
         @pl.when(kind == 0)
         def _():
-            copy(slot, near_ref).start()
+            out_ref[slot] = near_ref[pl.ds(start, rows)]
 
         @pl.when(kind == 1)
         def _():
-            copy(slot, far_ref).start()
+            out_ref[slot] = far_ref[pl.ds(start, rows)]
 
         @pl.when(kind == 2)
         def _():
             out_ref[slot] = jnp.zeros(out_ref.shape[1:], out_ref.dtype)
 
-    for slot in range(slots):
-
-        @pl.when(where_ref[slot, 0] != 2)
-        def _():
-            copy(slot, near_ref).wait()
-
 
 def selected(where, near, far, rows):
     slots = where.shape[0]
+    vmem = pl.BlockSpec(memory_space=pltpu.VMEM)
     return pl.pallas_call(
         select_kernel,
         out_shape=jax.ShapeDtypeStruct((slots, rows, near.shape[1]), near.dtype),
-        in_specs=[
-            pl.BlockSpec(memory_space=pltpu.SMEM),
-            pl.BlockSpec(memory_space=pl.ANY),
-            pl.BlockSpec(memory_space=pl.ANY),
-        ],
-        out_specs=pl.BlockSpec(memory_space=pltpu.VMEM),
-        scratch_shapes=[pltpu.SemaphoreType.DMA((slots,))],
+        in_specs=[pl.BlockSpec(memory_space=pltpu.SMEM), vmem, vmem],
+        out_specs=vmem,
+        compiler_params=pltpu.CompilerParams(vmem_limit_bytes=2**20 + 2 * 2 * near.size),
         name="select",
     )(where, near, far)
 
@@ -372,7 +359,7 @@
             pltpu.VMEM((slots, rows, width), F32),
             pltpu.VMEM((slots, rows, 128), F32),
         ],
-        compiler_params=pltpu.CompilerParams(vmem_limit_bytes=48 * 2**20),
+        compiler_params=pltpu.CompilerParams(vmem_limit_bytes=24 * 2**20),
         cost_estimate=pl.CostEstimate(
             flops=4 * H * count * keys * width,
             bytes_accessed=2 * keys * width,
@@ -413,6 +400,7 @@
         out_shape=jax.ShapeDtypeStruct(keep.shape, BF16),
         in_specs=[vmem] * 4,
         out_specs=vmem,
+        compiler_params=pltpu.CompilerParams(vmem_limit_bytes=4 * 2**20),
         name="finish",
     )(keep, lse, got, w_out)
 

time: 63.7 us -> 54.8 us (0.86)
  local copies, waits for them, and re-layouts: 9.31 us -> 3.78 us
  Pallas kernels: 11.8 us -> 9.3 us
  waiting for transfers between devices: 16.5 us -> 15.5 us
  starting transfers between devices: 24.4 us -> 25.3 us
    unnamed x41 -> x27, local copies, waits for them, and re-layouts: 7.28 us -> 1.76 us
    pallas_call x1, Pallas kernels: 2.09 us -> 0.58 us  [selected(): pl.pallas_call(select_kernel, out_shape=jax.ShapeDtypeStruct((slots, rows...]
    pallas_call x1, Pallas kernels: 1.94 us -> 0.95 us  [finished(): pl.pallas_call(finish_kernel, out_shape=jax.ShapeDtypeStruct(keep.shape,...]
    ppermute x11, waiting for transfers between devices: 16.4 us -> 15.4 us  [exchange(): return lax.ppermute(x, AXES, pairs)]
    ppermute x11, starting transfers between devices: 22.3 us -> 23.1 us  [exchange(): return lax.ppermute(x, AXES, pairs)]
where the time goes in v2:
time: 54.8 us; the launch traced here: 54.5 us
  starting transfers between devices  25.3 us (46%)
  waiting for transfers between devices  15.5 us (28%)
  Pallas kernels  9.3 us (17%)
  local copies, waits for them, and re-layouts  3.78 us (7%)
    ppermute x11, starting transfers between devices, exchange(): return lax.ppermute(x, AXES, pairs)  23.1 us
    ppermute x11, waiting for transfers between devices, exchange(): return lax.ppermute(x, AXES, pairs)  15.4 us
    pallas_call x1, Pallas kernels, attended(): pl.pallas_call(attend_kernel, out_shape=(jax.ShapeDtypeStruct((half_slots...  6.03 us
    ppermute x2, starting transfers between devices, vertical(): return lax.ppermute(x, AXES, pairs)  2.12 us
    unnamed x27, local copies, waits for them, and re-layouts  1.76 us
    pallas_call x1, Pallas kernels, features_of(): pl.pallas_call(conv_kernel, out_shape=jax.ShapeDtypeStruct((bands * lons,...  1.74 us
    slice x1, local copies, waits for them, and re-layouts, halves(): bottom = jnp.transpose(state_field[:, rows - 2:], (1, 0, 2))  1.11 us
  transfers between devices with their start and end apart: 13, of which 11 were waited for; matrix products, arithmetic and copies ran while one was open for 5% of the time, Pallas kernels for 0%

profile of v2, /device:TPU:0, one launch (start us, length us, event | category | flops | bytes accessed | tf_op | source)
XLA Modules:
  0.0 54.5 jit_solution(8020287447927675187)
XLA Ops:
  0.0 2.9 %collective-permute-start = (bf16[73,8,128]{2,1,0:T(8,128)(2,1)}, bf16[73,8,128]{2,1,0:T(8,128)(2,1)S(1)}, u32[]{:S(2)}, u32[]{:S(2)}) collective-permute-start(bf16[73,8,128]{2,1,0:T(8,128)(2,1)} %own_ref.1), channel_id=1, source_target_pairs={{0,1},{1,0},{2,3},{3,2},{4,5},{5,4},{6,7},{7,6},{8,9},{9,8},{10,11... | collective-permute-start | bytes 448520 | tf_op jit(solution)/shard_map/ppermute | solution.py:145
  2.9 1.1 %fusion.4 = (bf16[73,2,128]{2,1,0:T(2,128)(2,1)S(1)}, bf16[73,2,128]{2,1,0:T(2,128)(2,1)S(1)}) fusion(bf16[73,8,128]{2,1,0:T(8,128)(2,1)} %own_ref.1), kind=kLoop, calls=%fused_computation.46 | loop fusion | bytes 149504 | tf_op jit(solution)/shard_map/slice | solution.py:437
  4.1 1.5 %collective-permute-start.1 = (bf16[2,73,128]{2,1,0:T(8,128)(2,1)S(1)}, bf16[2,73,128]{2,1,0:T(8,128)(2,1)S(1)}, u32[]{:S(2)}, u32[]{:S(2)}) collective-permute-start(bf16[2,73,128]{2,1,0:T(8,128)(2,1)S(1)} %get-tuple-element.16), channel_id=1, source_target_pairs={{3,1},{0,2},{5,3},{2,4},{7,5},{4,6},{9,7},{6,8},{11,9},{8,10},{13,... | collective-permute-start | bytes 112136 | tf_op jit(solution)/shard_map/ppermute | solution.py:156
  5.6 0.7 %collective-permute-start.2 = (bf16[2,73,128]{2,1,0:T(8,128)(2,1)S(1)}, bf16[2,73,128]{2,1,0:T(8,128)(2,1)S(1)}, u32[]{:S(2)}, u32[]{:S(2)}) collective-permute-start(bf16[2,73,128]{2,1,0:T(8,128)(2,1)S(1)} %get-tuple-element.15), channel_id=1, source_target_pairs={{2,1},{1,2},{4,3},{3,4},{6,5},{5,6},{8,7},{7,8},{10,9},{9,10},{12,... | collective-permute-start | bytes 112136 | tf_op jit(solution)/shard_map/ppermute | solution.py:156
  7.0 1.1 %copy-done.1 = bf16[5,3,73,256]{3,2,1,0:T(8,128)(2,1)S(1)} copy-done((bf16[5,3,73,256]{3,2,1,0:T(8,128)(2,1)S(1)}, bf16[5,3,73,256]{3,2,1,0:T(8,128)(2,1)}, u32[]{:S(2)}) %copy-start.1) | copy-done | bytes 560664
  8.1 1.7 %conv.1 = bf16[256,256]{1,0:T(8,128)(2,1)S(1)} custom-call(s32[2,5]{1,0:T(2,128)S(1)} %constant_dynamic-slice_fusion.rows_ref, bf16[73,8,128]{2,1,0:T(8,128)(2,1)S(1)} %copy-done.2, bf16[73,8,128]{2,1,0:T(8,128)(2,1)S(1)} %collective-permute-done.other_ref, bf16[2,73,128]{2,1,0:T(8,128)(2,1)S(1)} %collective-permute-done.1.edge_ref, ...), custom_call_target="tpu_custom_call" | custom-call | flops 157286400 | bytes 859648 | tf_op jit(solution)/shard_map/conv/pallas_call | solution.py:224
  9.9 5.9 %collective-permute-start.3 = (bf16[256,256]{1,0:T(8,128)(2,1)S(1)}, bf16[256,256]{1,0:T(8,128)(2,1)S(1)}, u32[]{:S(2)}, u32[]{:S(2)}) collective-permute-start(bf16[256,256]{1,0:T(8,128)(2,1)S(1)} %conv.1), channel_id=1, source_target_pairs={{0,1},{1,0},{2,3},{3,2},{4,5},{5,4},{6,7},{7,6},{8,9},{9,8},{10,11... | collective-permute-start | bytes 393224 | tf_op jit(solution)/shard_map/ppermute | solution.py:145
  15.8 1.5 %collective-permute-start.4 = (bf16[256,256]{1,0:T(8,128)(2,1)S(1)}, bf16[256,256]{1,0:T(8,128)(2,1)S(1)}, u32[]{:S(2)}, u32[]{:S(2)}) collective-permute-start(bf16[256,256]{1,0:T(8,128)(2,1)S(1)} %conv.1), channel_id=1, source_target_pairs={{0,4},{1,5},{2,6},{3,7},{4,0},{5,1},{6,2},{7,3},{8,12},{9,13},{10,... | collective-permute-start | bytes 393224 | tf_op jit(solution)/shard_map/ppermute | solution.py:145
  17.3 1.7 %collective-permute-start.6 = (bf16[256,256]{1,0:T(8,128)(2,1)S(1)}, bf16[256,256]{1,0:T(8,128)(2,1)S(1)}, u32[]{:S(2)}, u32[]{:S(2)}) collective-permute-start(bf16[256,256]{1,0:T(8,128)(2,1)S(1)} %conv.1), channel_id=1, source_target_pairs={{0,8},{1,9},{2,10},{3,11},{4,12},{5,13},{6,14},{7,15},{8,0},{9,1},... | collective-permute-start | bytes 393224 | tf_op jit(solution)/shard_map/ppermute | solution.py:145
  19.1 3.7 %collective-permute-start.5 = (bf16[256,256]{1,0:T(8,128)(2,1)S(1)}, bf16[256,256]{1,0:T(8,128)(2,1)S(1)}, u32[]{:S(2)}, u32[]{:S(2)}) collective-permute-start(bf16[256,256]{1,0:T(8,128)(2,1)S(1)} %collective-permute-done.3), channel_id=1, source_target_pairs={{0,4},{1,5},{2,6},{3,7},{4,0},{5,1},{6,2},{7,3},{8,12},{9,13},{10,... | collective-permute-start | bytes 393224 | tf_op jit(solution)/shard_map/ppermute | solution.py:145
  22.8 0.6 %collective-permute-done.6 = bf16[256,256]{1,0:T(8,128)(2,1)S(1)} collective-permute-done((bf16[256,256]{1,0:T(8,128)(2,1)S(1)}, bf16[256,256]{1,0:T(8,128)(2,1)S(1)}, u32[]{:S(2)}, u32[]{:S(2)}) %collective-permute-start.6) | collective-permute-done | bytes 131104 | tf_op jit(solution)/shard_map/ppermute | solution.py:145
  23.4 0.8 %collective-permute-start.7 = (bf16[256,256]{1,0:T(8,128)(2,1)S(1)}, bf16[256,256]{1,0:T(8,128)(2,1)S(1)}, u32[]{:S(2)}, u32[]{:S(2)}) collective-permute-start(bf16[256,256]{1,0:T(8,128)(2,1)S(1)} %collective-permute-done.6), channel_id=1, source_target_pairs={{0,1},{1,0},{2,3},{3,2},{4,5},{5,4},{6,7},{7,6},{8,9},{9,8},{10,11... | collective-permute-start | bytes 393224 | tf_op jit(solution)/shard_map/ppermute | solution.py:145
  24.3 1.6 %collective-permute-start.8 = (bf16[256,256]{1,0:T(8,128)(2,1)S(1)}, bf16[256,256]{1,0:T(8,128)(2,1)S(1)}, u32[]{:S(2)}, u32[]{:S(2)}) collective-permute-start(bf16[256,256]{1,0:T(8,128)(2,1)S(1)} %collective-permute-done.4), channel_id=1, source_target_pairs={{0,8},{1,9},{2,10},{3,11},{4,12},{5,13},{6,14},{7,15},{8,0},{9,1},... | collective-permute-start | bytes 393224 | tf_op jit(solution)/shard_map/ppermute | solution.py:145
  26.3 1.8 %collective-permute-start.9 = (bf16[256,256]{1,0:T(8,128)(2,1)S(1)}, bf16[256,256]{1,0:T(8,128)(2,1)S(1)}, u32[]{:S(2)}, u32[]{:S(2)}) collective-permute-start(bf16[256,256]{1,0:T(8,128)(2,1)S(1)} %collective-permute-done.5), channel_id=1, source_target_pairs={{0,8},{1,9},{2,10},{3,11},{4,12},{5,13},{6,14},{7,15},{8,0},{9,1},... | collective-permute-start | bytes 393224 | tf_op jit(solution)/shard_map/ppermute | solution.py:145
  28.7 1.6 %collective-permute-done.8 = bf16[256,256]{1,0:T(8,128)(2,1)S(1)} collective-permute-done((bf16[256,256]{1,0:T(8,128)(2,1)S(1)}, bf16[256,256]{1,0:T(8,128)(2,1)S(1)}, u32[]{:S(2)}, u32[]{:S(2)}) %collective-permute-start.8) | collective-permute-done | bytes 131104 | tf_op jit(solution)/shard_map/ppermute | solution.py:145
  30.3 1.7 %collective-permute-done.9 = bf16[256,256]{1,0:T(8,128)(2,1)S(1)} collective-permute-done((bf16[256,256]{1,0:T(8,128)(2,1)S(1)}, bf16[256,256]{1,0:T(8,128)(2,1)S(1)}, u32[]{:S(2)}, u32[]{:S(2)}) %collective-permute-start.9) | collective-permute-done | bytes 131104 | tf_op jit(solution)/shard_map/ppermute | solution.py:145
  32.3 0.6 %gather_fusion = s32[2]{0:T(128)S(1)} fusion(s32[16]{0:T(128)S(1)} %copy-done, s32[1024]{0:T(1024)S(1)} %pad_clamp_fusion), kind=kCustom, calls=%fused_computation | custom fusion | bytes 24 | tf_op jit(solution)/shard_map/gather | solution.py:455
  33.8 1.0 %collective-permute-done.10.far_ref = bf16[2048,256]{1,0:T(8,128)(2,1)S(1)} collective-permute-done((bf16[2048,256]{1,0:T(8,128)(2,1)S(1)}, bf16[2048,256]{1,0:T(8,128)(2,1)S(1)}, u32[]{:S(2)}, u32[]{:S(2)}) %collective-permute-start.10) | collective-permute-done | bytes 1048608 | tf_op jit(solution)/shard_map/ppermute | solution.py:145
  35.4 2.2 %collective-permute-start.11 = (bf16[2,64,256]{2,1,0:T(8,128)(2,1)S(1)}, bf16[2,64,256]{2,1,0:T(8,128)(2,1)S(1)}, u32[]{:S(2)}, u32[]{:S(2)}) collective-permute-start(bf16[2,64,256]{2,1,0:T(8,128)(2,1)S(1)} %select.154.sel_ref), channel_id=1, source_target_pairs={{0,16},{1,17},{2,18},{3,19},{4,20},{5,21},{6,22},{7,23},{8,24},{9,... | collective-permute-start | bytes 196616 | tf_op jit(solution)/shard_map/ppermute | solution.py:145
  37.8 4.1 %collective-permute-done.11.got_ref = bf16[2,64,256]{2,1,0:T(8,128)(2,1)S(1)} collective-permute-done((bf16[2,64,256]{2,1,0:T(8,128)(2,1)S(1)}, bf16[2,64,256]{2,1,0:T(8,128)(2,1)S(1)}, u32[]{:S(2)}, u32[]{:S(2)}) %collective-permute-start.11) | collective-permute-done | bytes 65568 | tf_op jit(solution)/shard_map/ppermute | solution.py:145
  42.0 6.0 %attend.1 = (bf16[1,64,384]{2,1,0:T(8,128)(2,1)S(1)}, f32[1,64,256]{2,1,0:T(8,128)S(1)}, f32[1,64,128]{2,1,0:T(8,128)S(1)}) custom-call(s32[1]{0:T(128)} %bitcast.mine_ref, bf16[2,64,256]{2,1,0:T(8,128)(2,1)S(1)} %select.154.sel_ref, bf16[2,64,256]{2,1,0:T(8,128)(2,1)S(1)} %collective-permute-done.11.got_ref, ...), custom_call_target="tpu_custom_call" | custom-call | flops 2147483648 | bytes 2097152 | tf_op jit(solution)/shard_map/attend/pallas_call | solution.py:348
  48.0 0.9 %collective-permute-start.12 = (bf16[1,64,384]{2,1,0:T(8,128)(2,1)S(1)}, bf16[1,64,384]{2,1,0:T(8,128)(2,1)S(1)}, u32[]{:S(2)}, u32[]{:S(2)}) collective-permute-start(bf16[1,64,384]{2,1,0:T(8,128)(2,1)S(1)} %get-tuple-element.10), channel_id=1, source_target_pairs={{0,16},{1,17},{2,18},{3,19},{4,20},{5,21},{6,22},{7,23},{8,24},{9,... | collective-permute-start | bytes 147464 | tf_op jit(solution)/shard_map/ppermute | solution.py:145
  48.9 4.6 %collective-permute-done.12.got_ref = bf16[1,64,384]{2,1,0:T(8,128)(2,1)S(1)} collective-permute-done((bf16[1,64,384]{2,1,0:T(8,128)(2,1)S(1)}, bf16[1,64,384]{2,1,0:T(8,128)(2,1)S(1)}, u32[]{:S(2)}, u32[]{:S(2)}) %collective-permute-start.12) | collective-permute-done | bytes 49184 | tf_op jit(solution)/shard_map/ppermute | solution.py:145
  53.6 0.9 %finish.1 = bf16[1,64,256]{2,1,0:T(8,128)(2,1)} custom-call(f32[1,64,256]{2,1,0:T(8,128)S(1)} %get-tuple-element.8.keep_ref, f32[1,64,128]{2,1,0:T(8,128)S(1)} %get-tuple-element.9.lse_ref, bf16[1,64,384]{2,1,0:T(8,128)(2,1)S(1)} %collective-permute-done.12.got_ref, bf16[256,256]{1,0:T(8,128)(2,1)S(1)} %copy-done.3), custom_call_target="tpu_custom_call" | custom-call | tf_op jit(solution)/shard_map/finish/pallas_call | solution.py:398
  (50 shorter events, 4.0 us)
Async XLA Ops:
  0.0 32.3 %copy-start = (s32[16]{0:T(128)S(1)}, s32[16]{0:T(128)}, u32[]{:S(2)}) copy-start(s32[16]{0:T(128)} %param.12) | copy-start | bytes 196
  0.0 7.0 %collective-permute-start = (bf16[73,8,128]{2,1,0:T(8,128)(2,1)}, bf16[73,8,128]{2,1,0:T(8,128)(2,1)S(1)}, u32[]{:S(2)}, u32[]{:S(2)}) collective-permute-start(bf16[73,8,128]{2,1,0:T(8,128)(2,1)} %own_ref.1), channel_id=1, source_target_pairs={{0,1},{1,0},{2,3},{3,2},{4,5},{5,4},{6,7},{7,6},{8,9},{9,8},{10,11... | collective-permute-start | bytes 448520 | tf_op jit(solution)/shard_map/ppermute | solution.py:145
  2.9 4.1 %copy-start.2 = (bf16[73,8,128]{2,1,0:T(8,128)(2,1)S(1)}, bf16[73,8,128]{2,1,0:T(8,128)(2,1)}, u32[]{:S(2)}) copy-start(bf16[73,8,128]{2,1,0:T(8,128)(2,1)} %own_ref.1) | copy-start | bytes 448516
  4.1 2.2 %copy-start.7 = (s32[4,5]{1,0:T(4,128)S(1)}, s32[4,5]{1,0:T(4,128)}, u32[]{:S(2)}) copy-start(s32[4,5]{1,0:T(4,128)} %param.11) | copy-start | bytes 244
  4.1 2.3 %collective-permute-start.1 = (bf16[2,73,128]{2,1,0:T(8,128)(2,1)S(1)}, bf16[2,73,128]{2,1,0:T(8,128)(2,1)S(1)}, u32[]{:S(2)}, u32[]{:S(2)}) collective-permute-start(bf16[2,73,128]{2,1,0:T(8,128)(2,1)S(1)} %get-tuple-element.16), channel_id=1, source_target_pairs={{3,1},{0,2},{5,3},{2,4},{7,5},{4,6},{9,7},{6,8},{11,9},{8,10},{13,... | collective-permute-start | bytes 112136 | tf_op jit(solution)/shard_map/ppermute | solution.py:156
  5.6 0.9 %collective-permute-start.2 = (bf16[2,73,128]{2,1,0:T(8,128)(2,1)S(1)}, bf16[2,73,128]{2,1,0:T(8,128)(2,1)S(1)}, u32[]{:S(2)}, u32[]{:S(2)}) collective-permute-start(bf16[2,73,128]{2,1,0:T(8,128)(2,1)S(1)} %get-tuple-element.15), channel_id=1, source_target_pairs={{2,1},{1,2},{4,3},{3,4},{6,5},{5,6},{8,7},{7,8},{10,9},{9,10},{12,... | collective-permute-start | bytes 112136 | tf_op jit(solution)/shard_map/ppermute | solution.py:156
  7.0 1.1 %copy-start.1 = (bf16[5,3,73,256]{3,2,1,0:T(8,128)(2,1)S(1)}, bf16[5,3,73,256]{3,2,1,0:T(8,128)(2,1)}, u32[]{:S(2)}) copy-start(bf16[5,3,73,256]{3,2,1,0:T(8,128)(2,1)} %weight_ref.1) | copy-start | bytes 1681924
  9.9 9.2 %collective-permute-start.3 = (bf16[256,256]{1,0:T(8,128)(2,1)S(1)}, bf16[256,256]{1,0:T(8,128)(2,1)S(1)}, u32[]{:S(2)}, u32[]{:S(2)}) collective-permute-start(bf16[256,256]{1,0:T(8,128)(2,1)S(1)} %conv.1), channel_id=1, source_target_pairs={{0,1},{1,0},{2,3},{3,2},{4,5},{5,4},{6,7},{7,6},{8,9},{9,8},{10,11... | collective-permute-start | bytes 393224 | tf_op jit(solution)/shard_map/ppermute | solution.py:145
  15.8 8.5 %collective-permute-start.4 = (bf16[256,256]{1,0:T(8,128)(2,1)S(1)}, bf16[256,256]{1,0:T(8,128)(2,1)S(1)}, u32[]{:S(2)}, u32[]{:S(2)}) collective-permute-start(bf16[256,256]{1,0:T(8,128)(2,1)S(1)} %conv.1), channel_id=1, source_target_pairs={{0,4},{1,5},{2,6},{3,7},{4,0},{5,1},{6,2},{7,3},{8,12},{9,13},{10,... | collective-permute-start | bytes 393224 | tf_op jit(solution)/shard_map/ppermute | solution.py:145
  17.3 6.2 %collective-permute-start.6 = (bf16[256,256]{1,0:T(8,128)(2,1)S(1)}, bf16[256,256]{1,0:T(8,128)(2,1)S(1)}, u32[]{:S(2)}, u32[]{:S(2)}) collective-permute-start(bf16[256,256]{1,0:T(8,128)(2,1)S(1)} %conv.1), channel_id=1, source_target_pairs={{0,8},{1,9},{2,10},{3,11},{4,12},{5,13},{6,14},{7,15},{8,0},{9,1},... | collective-permute-start | bytes 393224 | tf_op jit(solution)/shard_map/ppermute | solution.py:145
  19.1 7.2 %collective-permute-start.5 = (bf16[256,256]{1,0:T(8,128)(2,1)S(1)}, bf16[256,256]{1,0:T(8,128)(2,1)S(1)}, u32[]{:S(2)}, u32[]{:S(2)}) collective-permute-start(bf16[256,256]{1,0:T(8,128)(2,1)S(1)} %collective-permute-done.3), channel_id=1, source_target_pairs={{0,4},{1,5},{2,6},{3,7},{4,0},{5,1},{6,2},{7,3},{8,12},{9,13},{10,... | collective-permute-start | bytes 393224 | tf_op jit(solution)/shard_map/ppermute | solution.py:145
  23.4 5.3 %collective-permute-start.7 = (bf16[256,256]{1,0:T(8,128)(2,1)S(1)}, bf16[256,256]{1,0:T(8,128)(2,1)S(1)}, u32[]{:S(2)}, u32[]{:S(2)}) collective-permute-start(bf16[256,256]{1,0:T(8,128)(2,1)S(1)} %collective-permute-done.6), channel_id=1, source_target_pairs={{0,1},{1,0},{2,3},{3,2},{4,5},{5,4},{6,7},{7,6},{8,9},{9,8},{10,11... | collective-permute-start | bytes 393224 | tf_op jit(solution)/shard_map/ppermute | solution.py:145
  24.3 6.1 %collective-permute-start.8 = (bf16[256,256]{1,0:T(8,128)(2,1)S(1)}, bf16[256,256]{1,0:T(8,128)(2,1)S(1)}, u32[]{:S(2)}, u32[]{:S(2)}) collective-permute-start(bf16[256,256]{1,0:T(8,128)(2,1)S(1)} %collective-permute-done.4), channel_id=1, source_target_pairs={{0,8},{1,9},{2,10},{3,11},{4,12},{5,13},{6,14},{7,15},{8,0},{9,1},... | collective-permute-start | bytes 393224 | tf_op jit(solution)/shard_map/ppermute | solution.py:145
  26.3 5.7 %collective-permute-start.9 = (bf16[256,256]{1,0:T(8,128)(2,1)S(1)}, bf16[256,256]{1,0:T(8,128)(2,1)S(1)}, u32[]{:S(2)}, u32[]{:S(2)}) collective-permute-start(bf16[256,256]{1,0:T(8,128)(2,1)S(1)} %collective-permute-done.5), channel_id=1, source_target_pairs={{0,8},{1,9},{2,10},{3,11},{4,12},{5,13},{6,14},{7,15},{8,0},{9,1},... | collective-permute-start | bytes 393224 | tf_op jit(solution)/shard_map/ppermute | solution.py:145
  32.0 2.7 %collective-permute-start.10 = (bf16[2048,256]{1,0:T(8,128)(2,1)S(1)}, bf16[2048,256]{1,0:T(8,128)(2,1)S(1)}, u32[]{:S(2)}, u32[]{:S(2)}) collective-permute-start(bf16[2048,256]{1,0:T(8,128)(2,1)S(1)} %constant_dynamic-update-slice_fusion.near_ref), channel_id=1, source_target_pairs={{0,2},{1,3},{2,0},{3,1},{4,6},{5,7},{6,4},{7,5},{8,10},{9,11},{10,... | collective-permute-start | bytes 3145736 | tf_op jit(solution)/shard_map/ppermute | solution.py:145
  33.1 0.7 %copy-start.8 = (s32[16]{0:T(128)S(1)}, s32[16]{0:T(128)}, u32[]{:S(2)}) copy-start(s32[16]{0:T(128)} %constant.124.clone) | copy-start | bytes 196
  33.1 0.7 %copy-start.9 = (s32[16]{0:T(128)S(1)}, s32[16]{0:T(128)}, u32[]{:S(2)}) copy-start(s32[16]{0:T(128)} %constant.125.clone) | copy-start | bytes 196
  33.8 8.2 %copy-start.4 = (bf16[256,256]{1,0:T(8,128)(2,1)S(1)}, bf16[256,256]{1,0:T(8,128)(2,1)}, u32[]{:S(2)}) copy-start(bf16[256,256]{1,0:T(8,128)(2,1)} %wq_ref.1) | copy-start | bytes 393220
  33.8 8.2 %copy-start.5 = (bf16[256,256]{1,0:T(8,128)(2,1)S(1)}, bf16[256,256]{1,0:T(8,128)(2,1)}, u32[]{:S(2)}) copy-start(bf16[256,256]{1,0:T(8,128)(2,1)} %wk_ref.1) | copy-start | bytes 393220
  33.8 8.2 %copy-start.6 = (bf16[256,256]{1,0:T(8,128)(2,1)S(1)}, bf16[256,256]{1,0:T(8,128)(2,1)}, u32[]{:S(2)}) copy-start(bf16[256,256]{1,0:T(8,128)(2,1)} %wv_ref.1) | copy-start | bytes 393220
  35.4 6.5 %collective-permute-start.11 = (bf16[2,64,256]{2,1,0:T(8,128)(2,1)S(1)}, bf16[2,64,256]{2,1,0:T(8,128)(2,1)S(1)}, u32[]{:S(2)}, u32[]{:S(2)}) collective-permute-start(bf16[2,64,256]{2,1,0:T(8,128)(2,1)S(1)} %select.154.sel_ref), channel_id=1, source_target_pairs={{0,16},{1,17},{2,18},{3,19},{4,20},{5,21},{6,22},{7,23},{8,24},{9,... | collective-permute-start | bytes 196616 | tf_op jit(solution)/shard_map/ppermute | solution.py:145
  42.0 11.6 %copy-start.3 = (bf16[256,256]{1,0:T(8,128)(2,1)S(1)}, bf16[256,256]{1,0:T(8,128)(2,1)}, u32[]{:S(2)}) copy-start(bf16[256,256]{1,0:T(8,128)(2,1)} %wo_ref.1) | copy-start | bytes 393220
  48.0 5.6 %collective-permute-start.12 = (bf16[1,64,384]{2,1,0:T(8,128)(2,1)S(1)}, bf16[1,64,384]{2,1,0:T(8,128)(2,1)S(1)}, u32[]{:S(2)}, u32[]{:S(2)}) collective-permute-start(bf16[1,64,384]{2,1,0:T(8,128)(2,1)S(1)} %get-tuple-element.10), channel_id=1, source_target_pairs={{0,16},{1,17},{2,18},{3,19},{4,20},{5,21},{6,22},{7,23},{8,24},{9,... | collective-permute-start | bytes 147464 | tf_op jit(solution)/shard_map/ppermute | solution.py:145

commit v3 on v2

v3 whole, which is shorter than its diff:
```python
import functools
import math

import jax
import jax.numpy as jnp
from jax import lax
from jax.experimental import pallas as pl
from jax.experimental.pallas import tpu as pltpu
from jax.sharding import PartitionSpec as P

D = 256
H = 4
AXES = ("lat", "lon")
LOG2E = 1.0 / math.log(2.0)
F32 = jnp.float32
BF16 = jnp.bfloat16


def padded(x, sides, width):
    for axis, dim in sides:
        devices, length = (lax.axis_size(axis), x.shape[dim])
        up = [(i, (i + 1) % devices) for i in range(devices - 1)]
        down = [(j, i) for i, j in up]
        last = lax.slice_in_dim(x, length - width, length, axis=dim)
        leading = lax.slice_in_dim(x, 0, width, axis=dim)
        before = lax.ppermute(last, axis, up)
        after = lax.ppermute(leading, axis, down)
        x = jnp.concatenate([before, x, after], axis=dim)
    return x


def shifted(x, axis, by):
    devices = lax.axis_size(axis)
    return lax.ppermute(x, axis, [(i, (i + by) % devices) for i in range(devices)])


def conv_features(extended, support_rows, conv_weight):
    bands = support_rows.shape[0]
    width = (extended.shape[2] - 1) // 2
    row_index = 2 * jnp.arange(bands, dtype=jnp.int32)[:, None] + support_rows + 2
    picked = jnp.take(extended, row_index, axis=1)
    tapped = jnp.stack(
        [picked[..., column_tap : column_tap + 2 * width : 2] for column_tap in range(3)], axis=3
    )
    patches = jnp.transpose(tapped, (1, 4, 2, 3, 0)).reshape(bands * width, -1)
    raw = jnp.dot(
        patches, conv_weight.reshape(-1, conv_weight.shape[-1]), preferred_element_type=F32
    )
    factor = lax.rsqrt(jnp.mean(raw * raw, axis=-1, keepdims=True) + 1e-06)
    return (raw * factor).astype(BF16).reshape(bands, width, -1)


def absorb(carry, block_keys, block_values, block_area, queries, scale):
    running_max, running_sum, mixed = carry
    scores = (
        jnp.einsum("qhd,khd->qhk", queries, block_keys, preferred_element_type=F32) * scale
        + block_area
    )
    new_max = jnp.maximum(running_max, jnp.max(scores, axis=-1))
    factor = jnp.exp(running_max - new_max)
    weights = jnp.exp(scores - new_max[..., None])
    running_sum = running_sum * factor + jnp.sum(weights, axis=-1)
    update = jnp.einsum(
        "qhk,khd->qhd", weights.astype(BF16), block_values, preferred_element_type=F32
    )
    mixed = mixed * factor[..., None] + update
    return (new_max, running_sum, mixed)


def sweep(carry, keys, values, queries, band_total):
    rows = keys.shape[0]
    lon_tile = keys.shape[1]
    head_size = D // H
    band_block = math.gcd(rows, max(1, 512 // lon_tile))
    blocks = rows // band_block
    block_len = band_block * lon_tile
    keys_blocks = keys.reshape(blocks, block_len, H, head_size)
    values_blocks = values.reshape(blocks, block_len, H, head_size)
    band_index = jnp.arange(rows, dtype=jnp.int32)
    area_rows = jnp.repeat(log_area(band_index, band_total), lon_tile).reshape(blocks, block_len)
    scale = 1.0 / math.sqrt(head_size)

    def step_block(state, inputs):
        return (absorb(state, inputs[0], inputs[1], inputs[2], queries, scale), None)

    result, unused = lax.scan(step_block, carry, (keys_blocks, values_blocks, area_rows))
    return result


def log_area(bands, band_total):
    centre = (bands.astype(F32) + 0.5) * (math.pi / band_total) - math.pi / 2
    return jnp.log(jnp.cos(centre))


def general(state_field, support_rows, window_bands, conv_weight, w_query, w_key, w_value, w_out):
    lat_tile = support_rows.shape[0]
    lon_tile = state_field.shape[2] // 2
    whole_lon = lon_tile * lax.axis_size("lon")
    band_total = lat_tile * lax.axis_size("lat")
    head_size = D // H
    extended = padded(state_field, (("lat", 1),), 2)
    western = shifted(extended[:, :, -1:], "lon", 1)
    extended = jnp.concatenate([western, extended], axis=2)
    features = conv_features(extended, support_rows, conv_weight)
    slot_count = window_bands.shape[0] // lax.axis_size("lat")
    piece = lax.all_gather(features, "lat", axis=0, tiled=True)
    mine = lax.dynamic_slice_in_dim(
        window_bands, lax.axis_index("lat") * slot_count, slot_count, axis=0
    )
    picked = jnp.take(piece, mine, axis=0)
    gathered = lax.all_gather(picked, "lon", axis=1, tiled=True)
    query_count = slot_count * whole_lon
    queries = jnp.dot(gathered.reshape(query_count, D), w_query, preferred_element_type=F32)
    queries = queries.astype(BF16).reshape(query_count, H, head_size)
    initial = (
        jnp.full((query_count, H), -1e30, F32),
        jnp.zeros((query_count, H), F32),
        jnp.zeros((query_count, H, head_size), F32),
    )
    piece_rows = piece.reshape(-1, D)
    keys = jnp.dot(piece_rows, w_key, preferred_element_type=F32).astype(BF16)
    values = jnp.dot(piece_rows, w_value, preferred_element_type=F32).astype(BF16)
    running_max, running_sum, mixed = sweep(
        initial, keys.reshape(piece.shape), values.reshape(piece.shape), queries, band_total
    )
    best = lax.pmax(running_max, "lon")
    factor = jnp.exp(running_max - best)
    scaled_mix = (mixed * factor[..., None]).reshape(slot_count, whole_lon, D)
    scaled_sum = (running_sum * factor).reshape(slot_count, whole_lon, H)
    mix_share, sum_share = (
        lax.psum_scatter(part.astype(BF16), "lon", scatter_dimension=1, tiled=True).astype(F32)
        for part in (scaled_mix, scaled_sum)
    )
    attended = mix_share.reshape(slot_count, lon_tile, H, head_size) / sum_share[..., None]
    attended = attended.astype(BF16).reshape(slot_count * lon_tile, D)
    result = jnp.dot(attended, w_out, preferred_element_type=F32).astype(BF16)
    return result.reshape(slot_count, lon_tile, D)


def exchange(x, lat_mask, lon_mask):
    lats, lons = lax.axis_size("lat"), lax.axis_size("lon")
    pairs = [
        (i * lons + j, (i ^ lat_mask) * lons + (j ^ lon_mask))
        for i in range(lats)
        for j in range(lons)
    ]
    return lax.ppermute(x, AXES, pairs)


def vertical(x):
    lats, lons = lax.axis_size("lat"), lax.axis_size("lon")
    pairs = []
    for i in range(1, lats):
        j = i % lons
        pairs += [((i - 1) * lons + j, i * lons + j), (i * lons + j, (i - 1) * lons + j)]
    return lax.ppermute(x, AXES, pairs)


def lines_of(ref, strided, deep):
    channels, rows, lons = ref.shape
    strided[0 : channels * rows] = ref[...].astype(F32).reshape(channels * rows, lons)
    strided[channels * rows :] = jnp.zeros(((deep - channels) * rows, lons), F32)
    return [strided[pl.ds(row, deep, stride=rows), :].astype(BF16) for row in range(rows)]


def rows_kernel(lower_ref, own_ref, lines_ref, same_ref, cross_ref, strided):
    rows, deep, _ = lines_ref.shape
    edge = same_ref.shape[0]
    lines = lines_of(own_ref, strided, deep)
    for row in range(rows):
        lines_ref[row] = lines[row]
    lower = lower_ref[0] != 0
    for row in range(edge):
        top, bottom = lines[row], lines[rows - edge + row]
        same_ref[row] = jnp.where(lower, bottom, top)
        cross_ref[row] = jnp.where(lower, top, bottom)


def rows_of(lower, own, edge, deep):
    _, rows, lons = own.shape
    vmem = pl.BlockSpec(memory_space=pltpu.VMEM)
    return pl.pallas_call(
        rows_kernel,
        out_shape=(
            jax.ShapeDtypeStruct((rows, deep, lons), BF16),
            jax.ShapeDtypeStruct((edge, deep, lons), BF16),
            jax.ShapeDtypeStruct((edge, deep, lons), BF16),
        ),
        in_specs=[pl.BlockSpec(memory_space=pltpu.SMEM), vmem],
        out_specs=(vmem, vmem, vmem),
        scratch_shapes=[pltpu.VMEM((deep * rows, lons), F32)],
        compiler_params=pltpu.CompilerParams(vmem_limit_bytes=4 * 2**20),
        name="rows",
    )(lower, own)


def weights_kernel(weight_ref, out_ref):
    slots, taps, channels, width = weight_ref.shape
    deep = out_ref.shape[0] // (slots * taps)
    blank = jnp.zeros((deep - channels, width), BF16)
    for slot in range(slots):
        for tap in range(taps):
            at = (slot * taps + tap) * deep
            out_ref[at : at + deep] = jnp.concatenate([weight_ref[slot, tap], blank], axis=0)


def weights_of(conv_weight, deep):
    slots, taps, _, width = conv_weight.shape
    vmem = pl.BlockSpec(memory_space=pltpu.VMEM)
    return pl.pallas_call(
        weights_kernel,
        out_shape=jax.ShapeDtypeStruct((slots * taps * deep, width), BF16),
        in_specs=[vmem],
        out_specs=vmem,
        compiler_params=pltpu.CompilerParams(vmem_limit_bytes=4 * 2**20),
        cost_estimate=pl.CostEstimate(
            flops=0, bytes_accessed=4 * conv_weight.size, transcendentals=0
        ),
        name="weights",
    )(conv_weight)


def conv_kernel(
    rows_ref, own_ref, other_ref, edge_ref, weight_ref, out_ref, taken, patches
):
    rows, deep, lons = own_ref.shape
    edge = edge_ref.shape[0] // 2
    width = lons
    bands = out_ref.shape[0] // width
    slots = rows_ref.shape[1]
    taps = weight_ref.shape[0] // (slots * deep)
    column = lax.broadcasted_iota(jnp.int32, (2 * lons, taps * width), 0)
    place = lax.broadcasted_iota(jnp.int32, (2 * lons, taps * width), 1)
    wanted = lax.rem(2 * (place % width) + place // width - 1 + 2 * lons, 2 * lons)
    choose = (column == wanted).astype(F32).astype(BF16)
    near = [own_ref[row] for row in range(rows)] + [edge_ref[row] for row in range(edge)]
    far = [other_ref[row] for row in range(rows)] + [edge_ref[edge + row] for row in range(edge)]
    both = jnp.concatenate(
        [jnp.concatenate(near, axis=0), jnp.concatenate(far, axis=0)], axis=1
    )
    split = jnp.dot(both, choose, preferred_element_type=F32).astype(BF16)
    for row in range(rows):
        taken[edge + row] = split[row * deep : (row + 1) * deep]
    for row in range(edge):
        piece = split[(rows + row) * deep : (rows + row + 1) * deep]
        taken[row] = piece
        taken[edge + rows + row] = piece
    for slot in range(slots):
        for band in range(bands):
            line = taken[rows_ref[band, slot]]
            for tap in range(taps):
                at = (slot * taps + tap) * deep
                patches[at : at + deep, band * width : (band + 1) * width] = line[
                    :, tap * width : (tap + 1) * width
                ]
    raw = lax.dot_general(
        patches[...], weight_ref[...], (((0,), (0,)), ((), ())), preferred_element_type=F32
    )
    factor = lax.rsqrt(jnp.mean(raw * raw, axis=-1, keepdims=True) + 1e-06)
    out_ref[...] = (raw * factor).astype(BF16)


def features_of(own, other, edge, row_index, weights):
    rows, deep, lons = own.shape
    width = weights.shape[1]
    bands = row_index.shape[0]
    taps = weights.shape[0] // (row_index.shape[1] * deep)
    vmem = pl.BlockSpec(memory_space=pltpu.VMEM)
    return pl.pallas_call(
        conv_kernel,
        out_shape=jax.ShapeDtypeStruct((bands * lons, width), BF16),
        in_specs=[pl.BlockSpec(memory_space=pltpu.SMEM)] + [vmem] * 4,
        out_specs=vmem,
        scratch_shapes=[
            pltpu.VMEM((rows + edge.shape[0], deep, taps * lons), BF16),
            pltpu.VMEM((weights.shape[0], bands * lons), BF16),
        ],
        compiler_params=pltpu.CompilerParams(vmem_limit_bytes=12 * 2**20),
        name="conv",
    )(row_index, own, other, edge, weights)


def select_kernel(where_ref, near_ref, own_ref, pair_ref, other_ref):
    slots, rows, _ = own_ref.shape
    for index in range(4 * slots):
        start = pl.multiple_of(where_ref[index, 1], rows)
        picked = near_ref[pl.ds(start, rows)]
        picked = jnp.where(where_ref[index, 0] != 0, picked, jnp.zeros_like(picked))
        if index < 2 * slots:
            (own_ref if index < slots else pair_ref)[index % slots] = picked
        else:
            other_ref[index - 2 * slots] = picked


def selected(where, near, rows):
    slots = where.shape[0] // 4
    vmem = pl.BlockSpec(memory_space=pltpu.VMEM)
    shape = jax.ShapeDtypeStruct((slots, rows, near.shape[1]), near.dtype)
    both = jax.ShapeDtypeStruct((2 * slots, rows, near.shape[1]), near.dtype)
    return pl.pallas_call(
        select_kernel,
        out_shape=(shape, shape, both),
        in_specs=[pl.BlockSpec(memory_space=pltpu.SMEM), vmem],
        out_specs=(vmem, vmem, vmem),
        compiler_params=pltpu.CompilerParams(vmem_limit_bytes=2**20 + 2 * near.size),
        name="select",
    )(where, near)


def split3(x):
    high = x.astype(BF16).astype(F32)
    middle = (x - high).astype(BF16).astype(F32)
    return high, middle, x - high - middle


def attend_kernel(
    keys_count, sel_ref, got_ref, area_ref, wq_ref, wk_ref, wv_ref, *refs
):
    held, (out_ref, *rest) = refs[:keys_count], refs[keys_count:]
    slots, rows, width = sel_ref.shape
    count = slots * rows
    head_size = width // H
    token = (sel_ref[...] + got_ref[...]).reshape(count, width)
    query = jnp.dot(token, wq_ref[...], preferred_element_type=F32).astype(BF16)
    lane = lax.broadcasted_iota(jnp.int32, (1, width), 1) // head_size
    spread = jnp.concatenate(
        [jnp.where(lane == head, query, jnp.zeros_like(query)) for head in range(H)], axis=0
    )
    turned = lax.dot_general(
        spread, wk_ref[...], (((1,), (1,)), ((), ())), preferred_element_type=F32
    )
    turned = (turned * (LOG2E / math.sqrt(head_size))).astype(BF16)
    parts, begin = [], 0
    for ref in held:
        for at in range(0, ref.shape[0], 512):
            chunk = min(512, ref.shape[0] - at)
            parts.append((ref, at, begin, chunk))
            begin += chunk
    top = None
    for ref, at, begin, chunk in parts:
        keys = ref[at : at + chunk]
        block = lax.dot_general(
            turned, keys, (((1,), (1,)), ((), ())), preferred_element_type=F32
        )
        block = block + area_ref[:, begin : begin + chunk]
        best = block[:, 0:128]
        for lanes in range(128, chunk, 128):
            best = jnp.maximum(best, block[:, lanes : lanes + 128])
        best = jnp.max(best, axis=1, keepdims=True)
        if top is not None:
            best = jnp.maximum(top, best)
        weight = jnp.exp2(block - best)
        added = weight[:, 0:128]
        for lanes in range(128, chunk, 128):
            added = added + weight[:, lanes : lanes + 128]
        update = jnp.dot(weight.astype(BF16), keys, preferred_element_type=F32)
        if top is None:
            total, mixed = added, update
        else:
            factor = jnp.exp2(top - best)
            total, mixed = total * factor + added, mixed * factor + update
        top = best
    total = jnp.sum(total, axis=1, keepdims=True)
    value = jnp.dot((mixed / total).astype(BF16), wv_ref[...], preferred_element_type=F32)
    lse = top + jnp.log2(total)
    out = jnp.zeros((count, width), F32)
    stat_lane = lax.broadcasted_iota(jnp.int32, (1, 128), 1)
    stats = jnp.zeros((count, 128), F32)
    for head in range(H):
        out = jnp.where(lane == head, value[head * count : (head + 1) * count], out)
        for order, piece in enumerate(split3(lse[head * count : (head + 1) * count])):
            stats = jnp.where(stat_lane == 3 * head + order, piece, stats)
    out_ref[:, :, 0:width] = out.reshape(sel_ref.shape).astype(out_ref.dtype)
    stats = stats.reshape(slots, rows, 128)
    if rest:
        rest[0][...] = stats
    else:
        out_ref[:, :, width:] = stats.astype(out_ref.dtype)


def attended(sent, sel, got, area, w_query, w_key, w_value, held):
    slots, rows, width = sel.shape
    keys = sum(part.shape[0] for part in held)
    count = slots * rows
    vmem = pl.BlockSpec(memory_space=pltpu.VMEM)
    if sent:
        out_shape = (jax.ShapeDtypeStruct((slots, rows, width + 128), BF16),)
    else:
        out_shape = (
            jax.ShapeDtypeStruct((slots, rows, width), F32),
            jax.ShapeDtypeStruct((slots, rows, 128), F32),
        )
    return pl.pallas_call(
        functools.partial(attend_kernel, len(held)),
        out_shape=out_shape,
        in_specs=[vmem] * (6 + len(held)),
        out_specs=(vmem,) * len(out_shape),
        compiler_params=pltpu.CompilerParams(vmem_limit_bytes=20 * 2**20),
        cost_estimate=pl.CostEstimate(
            flops=4 * H * count * keys * width,
            bytes_accessed=2 * keys * width,
            transcendentals=H * count * keys,
        ),
        name="attend_sent" if sent else "attend_kept",
    )(sel, got, area, w_query, w_key, w_value, *held)


def finish_kernel(keep_ref, lse_ref, got_ref, wo_ref, out_ref):
    slots, rows, width = keep_ref.shape
    count = slots * rows
    keep = keep_ref[...].reshape(count, width)
    got = got_ref[:, :, 0:width].astype(F32).reshape(count, width)
    ours = lse_ref[...].reshape(count, 128).astype(BF16)
    theirs = got_ref[:, :, width:].reshape(count, 128)
    piece = lax.broadcasted_iota(jnp.int32, (128, width), 0) // 3
    head = lax.broadcasted_iota(jnp.int32, (128, width), 1) // (width // H)
    spread = (piece == head).astype(F32).astype(BF16)
    sums = jnp.dot(
        jnp.concatenate([ours, theirs], axis=0), spread, preferred_element_type=F32
    )
    own, far = sums[:count], sums[count:]
    top = jnp.maximum(own, far)
    own = jnp.exp2(own - top)
    far = jnp.exp2(far - top)
    mixed = ((keep * own + got * far) / (own + far)).astype(BF16)
    result = jnp.dot(mixed, wo_ref[...], preferred_element_type=F32).astype(BF16)
    out_ref[...] = result.reshape(out_ref.shape)


def finished(keep, lse, got, w_out):
    vmem = pl.BlockSpec(memory_space=pltpu.VMEM)
    return pl.pallas_call(
        finish_kernel,
        out_shape=jax.ShapeDtypeStruct(keep.shape, BF16),
        in_specs=[vmem] * 4,
        out_specs=vmem,
        compiler_params=pltpu.CompilerParams(vmem_limit_bytes=4 * 2**20),
        name="finish",
    )(keep, lse, got, w_out)


def gathered(block, masks):
    blocks = {(0, 0): block}
    for size in range(1, len(masks) + 1):
        for start in range(len(masks)):
            if size == len(masks) and start > 0:
                break
            chosen = [masks[(start + k) % len(masks)] for k in range(size)]
            key = (0, 0)
            for mask in chosen:
                key = (key[0] ^ mask[0], key[1] ^ mask[1])
            step = chosen[-1]
            before = (key[0] ^ step[0], key[1] ^ step[1])
            if key not in blocks:
                blocks[key] = exchange(blocks[before], *step)
    return blocks


def halves(state_field, support_rows, window_bands, conv_weight, w_query, w_key, w_value, w_out):
    lats = lax.axis_size("lat")
    lat, lon = lax.axis_index("lat"), lax.axis_index("lon")
    channels, rows, lons = state_field.shape
    lat_tile = support_rows.shape[0]
    bands = lat_tile // 2
    lon_tile = lons // 2
    band_total = lat_tile * lats
    pair = lats // 2

    deep = -(-channels // 16) * 16
    lower = (lon ^ lat) & 1
    own, same, cross = rows_of(lower.astype(jnp.int32).reshape(1), state_field, 2, deep)
    edge = vertical(jnp.concatenate([same, exchange(cross, 0, 1)], axis=0))
    other = exchange(own, 0, 1)
    weights = weights_of(conv_weight, deep)
    row_index = 2 * jnp.arange(lat_tile, dtype=jnp.int32)[:, None] + support_rows + 2
    row_index = lax.dynamic_slice_in_dim(row_index, lower * bands, bands, axis=0)
    features = features_of(own, other, edge, row_index, weights)

    bits = [1 << k for k in range(1, lats.bit_length() - 1) if 1 << k != pair]
    masks = [(0, 1)] + [(bit, 0) for bit in bits]
    blocks = gathered(features, masks)
    order = [(i, j) for i in range(0, pair, 2) for j in range(2)]
    near = jnp.concatenate([blocks[key] for key in order], axis=0)

    size = bands * lons
    slot_count = window_bands.shape[0] // lats
    sides = jnp.stack([lat, lat ^ pair, lat ^ 1, lat ^ pair ^ 1])
    wanted = window_bands[
        (sides[:, None] * slot_count + jnp.arange(slot_count)[None, :]).reshape(-1)
    ]
    owner = wanted // lat_tile
    band = wanted % lat_tile
    owner_lower = band // bands
    turn = owner_lower ^ (owner & 1) ^ lon
    apart = owner ^ lat
    place = ((apart & (pair - 2)) + turn) * size + band % bands * lons + turn * lon_tile
    within = apart & (pair | 1) == 0
    where = jnp.stack([within.astype(jnp.int32), place.astype(jnp.int32)], axis=1)
    sel_own, sel_pair, sel_other = selected(where, near, lon_tile)
    got_other = exchange(sel_other, 1, 0)
    sel_own = sel_own + got_other[:slot_count]
    sel_pair = sel_pair + got_other[slot_count:]
    sel_own, sel_pair, near = lax.optimization_barrier((sel_own, sel_pair, near))
    got_pair = exchange(sel_own, pair, 0)
    got_own = exchange(sel_pair, pair, 0)
    held = (near, exchange(near, 1, 0))

    step = jnp.arange(2 * len(order) * bands, dtype=jnp.int32)
    masks = (step // bands) % len(order)
    tile = lat ^ ((masks & ~1) | (step // (len(order) * bands)))
    key_band = tile * lat_tile + ((tile ^ lon ^ masks) & 1) * bands + step % bands
    area = LOG2E * log_area(key_band, band_total)
    area = jnp.repeat(area, lons)[None, :]
    shared = (area, w_query, w_key, w_value, held)
    (send,) = attended(True, sel_pair, got_pair, *shared)
    received = exchange(send, pair, 0)
    keep, lse = attended(False, sel_own, got_own, *shared)
    return finished(keep, lse, received, w_out)


def solution(mesh):
    lats, lons = mesh.shape["lat"], mesh.shape["lon"]
    paired = lons == 2 and lats >= 4 and lats & (lats - 1) == 0
    return jax.shard_map(
        halves if paired else general,
        mesh=mesh,
        in_specs=(P(None, "lat", "lon"), P("lat", None), P(), P(), P(), P(), P(), P()),
        out_specs=P("lat", "lon", None),
        check_vma=False,
    )
```

time: 54.8 us -> 46.4 us (0.85)
  waiting for transfers between devices: 15.5 us -> 10.7 us
  Pallas kernels: 9.3 us -> 7.55 us
  local copies, waits for them, and re-layouts: 3.78 us -> 2.65 us
  starting transfers between devices: 25.3 us -> 24.6 us
    ppermute x11 -> x14, waiting for transfers between devices: 15.4 us -> 10.7 us  [exchange(): return lax.ppermute(x, AXES, pairs)]
    pallas_call x2 -> x5, Pallas kernels: 6.61 us -> 4.89 us  [the longest x2 4.18 us: attended(): pl.pallas_call(functools.partial(attend_kernel, len(held)), out_shape=out...]
    ppermute x2 -> x1, starting transfers between devices: 2.12 us -> 0.67 us  [vertical(): return lax.ppermute(x, AXES, pairs)]
    slice x1 -> x0, local copies, waits for them, and re-layouts: 1.11 us -> none  [halves(): bottom = jnp.transpose(state_field[:, rows - 2:], (1, 0, 2))]
    ppermute x11 -> x14, starting transfers between devices: 23.1 us -> 23.9 us  [exchange(): return lax.ppermute(x, AXES, pairs)]
    unnamed x27 -> x23, local copies, waits for them, and re-layouts: 1.76 us -> 1.73 us
  transfers between devices with their start and end apart: 13 -> 15, of which waited for: 11 -> 7; matrix products, arithmetic and copies ran while one was open for 5% -> 3% of each run, Pallas kernels for 0% -> 9%
where the time goes in v3:
time: 46.4 us; the launch traced here: 46.2 us
  starting transfers between devices  24.6 us (53%)
  waiting for transfers between devices  10.7 us (23%)
  Pallas kernels  7.55 us (16%)
  local copies, waits for them, and re-layouts  2.65 us (6%)
  other arithmetic  0.47 us (1%)
    ppermute x14, starting transfers between devices, exchange(): return lax.ppermute(x, AXES, pairs)  23.9 us
    ppermute x14, waiting for transfers between devices, exchange(): return lax.ppermute(x, AXES, pairs)  10.7 us
    pallas_call x2, Pallas kernels, attended(): pl.pallas_call(functools.partial(attend_kernel, len(held)), out_shape=out...  4.18 us
    unnamed x23, local copies, waits for them, and re-layouts  1.73 us
    pallas_call x1, Pallas kernels, features_of(): pl.pallas_call(conv_kernel, out_shape=jax.ShapeDtypeStruct((bands * lons,...  1.72 us
    pallas_call x1, Pallas kernels, finished(): pl.pallas_call(finish_kernel, out_shape=jax.ShapeDtypeStruct(keep.shape,...  0.93 us
  transfers between devices with their start and end apart: 15, of which 7 were waited for; matrix products, arithmetic and copies ran while one was open for 3% of the time, Pallas kernels for 9%

profile of v3, /device:TPU:0, one launch (start us, length us, event | category | flops | bytes accessed | tf_op | source)
XLA Modules:
  0.0 46.2 jit_solution(13095255755665710737)
XLA Ops:
  0.0 1.0 %copy-done.2 = bf16[73,8,128]{2,1,0:T(8,128)(2,1)S(1)} copy-done((bf16[73,8,128]{2,1,0:T(8,128)(2,1)S(1)}, bf16[73,8,128]{2,1,0:T(8,128)(2,1)}, u32[]{:S(2)}) %copy-start.2) | copy-done | bytes 149528
  1.1 3.0 %collective-permute-start.1 = (bf16[2,80,128]{2,1,0:T(8,128)(2,1)S(1)}, bf16[2,80,128]{2,1,0:T(8,128)(2,1)S(1)}, u32[]{:S(2)}, u32[]{:S(2)}) collective-permute-start(bf16[2,80,128]{2,1,0:T(8,128)(2,1)S(1)} %get-tuple-element.18), channel_id=1, source_target_pairs={{0,1},{1,0},{2,3},{3,2},{4,5},{5,4},{6,7},{7,6},{8,9},{9,8},{10,11... | collective-permute-start | bytes 122888 | tf_op jit(solution)/shard_map/ppermute | solution.py:147
  5.2 0.7 %copy-done.7 = s32[4,5]{1,0:T(4,128)S(1)} copy-done((s32[4,5]{1,0:T(4,128)S(1)}, s32[4,5]{1,0:T(4,128)}, u32[]{:S(2)}) %copy-start.7) | copy-done | bytes 104
  6.1 0.7 %collective-permute-start.2 = (bf16[4,80,128]{2,1,0:T(8,128)(2,1)S(1)}, bf16[4,80,128]{2,1,0:T(8,128)(2,1)S(1)}, u32[]{:S(2)}, u32[]{:S(2)}) collective-permute-start(bf16[4,80,128]{2,1,0:T(8,128)(2,1)S(1)} %pad_maximum_fusion), channel_id=1, source_target_pairs={{1,3},{3,1},{2,4},{4,2},{5,7},{7,5},{6,8},{8,6},{9,11},{11,9},{10,... | collective-permute-start | bytes 245768 | tf_op jit(solution)/shard_map/ppermute | solution.py:156
  6.8 3.0 %collective-permute-done.other_ref = bf16[8,80,128]{2,1,0:T(8,128)(2,1)S(1)} collective-permute-done((bf16[8,80,128]{2,1,0:T(8,128)(2,1)S(1)}, bf16[8,80,128]{2,1,0:T(8,128)(2,1)S(1)}, u32[]{:S(2)}, u32[]{:S(2)}) %collective-permute-start) | collective-permute-done | bytes 163872 | tf_op jit(solution)/shard_map/ppermute | solution.py:147
  9.7 1.7 %conv.1 = bf16[256,256]{1,0:T(8,128)(2,1)S(1)} custom-call(s32[2,5]{1,0:T(2,128)S(1)} %constant_dynamic-slice_fusion.rows_ref, bf16[8,80,128]{2,1,0:T(8,128)(2,1)S(1)} %get-tuple-element.16.own_ref, bf16[8,80,128]{2,1,0:T(8,128)(2,1)S(1)} %collective-permute-done.other_ref, bf16[4,80,128]{2,1,0:T(8,128)(2,1)S(1)} %collective-permute-done.2.edge_ref, ...), custom_call_target="tpu_custom_call" | custom-call | tf_op jit(solution)/shard_map/conv/pallas_call | solution.py:269
  11.5 2.1 %collective-permute-start.3 = (bf16[256,256]{1,0:T(8,128)(2,1)S(1)}, bf16[256,256]{1,0:T(8,128)(2,1)S(1)}, u32[]{:S(2)}, u32[]{:S(2)}) collective-permute-start(bf16[256,256]{1,0:T(8,128)(2,1)S(1)} %conv.1), channel_id=1, source_target_pairs={{0,1},{1,0},{2,3},{3,2},{4,5},{5,4},{6,7},{7,6},{8,9},{9,8},{10,11... | collective-permute-start | bytes 393224 | tf_op jit(solution)/shard_map/ppermute | solution.py:147
  13.6 3.4 %collective-permute-start.4 = (bf16[256,256]{1,0:T(8,128)(2,1)S(1)}, bf16[256,256]{1,0:T(8,128)(2,1)S(1)}, u32[]{:S(2)}, u32[]{:S(2)}) collective-permute-start(bf16[256,256]{1,0:T(8,128)(2,1)S(1)} %conv.1), channel_id=1, source_target_pairs={{0,4},{1,5},{2,6},{3,7},{4,0},{5,1},{6,2},{7,3},{8,12},{9,13},{10,... | collective-permute-start | bytes 393224 | tf_op jit(solution)/shard_map/ppermute | solution.py:147
  17.0 1.6 %collective-permute-start.6 = (bf16[256,256]{1,0:T(8,128)(2,1)S(1)}, bf16[256,256]{1,0:T(8,128)(2,1)S(1)}, u32[]{:S(2)}, u32[]{:S(2)}) collective-permute-start(bf16[256,256]{1,0:T(8,128)(2,1)S(1)} %conv.1), channel_id=1, source_target_pairs={{0,8},{1,9},{2,10},{3,11},{4,12},{5,13},{6,14},{7,15},{8,0},{9,1},... | collective-permute-start | bytes 393224 | tf_op jit(solution)/shard_map/ppermute | solution.py:147
  18.6 3.3 %collective-permute-start.5 = (bf16[256,256]{1,0:T(8,128)(2,1)S(1)}, bf16[256,256]{1,0:T(8,128)(2,1)S(1)}, u32[]{:S(2)}, u32[]{:S(2)}) collective-permute-start(bf16[256,256]{1,0:T(8,128)(2,1)S(1)} %collective-permute-done.3), channel_id=1, source_target_pairs={{0,4},{1,5},{2,6},{3,7},{4,0},{5,1},{6,2},{7,3},{8,12},{9,13},{10,... | collective-permute-start | bytes 393224 | tf_op jit(solution)/shard_map/ppermute | solution.py:147
  22.0 2.0 %collective-permute-start.7 = (bf16[256,256]{1,0:T(8,128)(2,1)S(1)}, bf16[256,256]{1,0:T(8,128)(2,1)S(1)}, u32[]{:S(2)}, u32[]{:S(2)}) collective-permute-start(bf16[256,256]{1,0:T(8,128)(2,1)S(1)} %collective-permute-done.6), channel_id=1, source_target_pairs={{0,1},{1,0},{2,3},{3,2},{4,5},{5,4},{6,7},{7,6},{8,9},{9,8},{10,11... | collective-permute-start | bytes 393224 | tf_op jit(solution)/shard_map/ppermute | solution.py:147
  24.0 1.6 %collective-permute-start.8 = (bf16[256,256]{1,0:T(8,128)(2,1)S(1)}, bf16[256,256]{1,0:T(8,128)(2,1)S(1)}, u32[]{:S(2)}, u32[]{:S(2)}) collective-permute-start(bf16[256,256]{1,0:T(8,128)(2,1)S(1)} %collective-permute-done.4), channel_id=1, source_target_pairs={{0,8},{1,9},{2,10},{3,11},{4,12},{5,13},{6,14},{7,15},{8,0},{9,1},... | collective-permute-start | bytes 393224 | tf_op jit(solution)/shard_map/ppermute | solution.py:147
  25.6 1.4 %collective-permute-start.9 = (bf16[256,256]{1,0:T(8,128)(2,1)S(1)}, bf16[256,256]{1,0:T(8,128)(2,1)S(1)}, u32[]{:S(2)}, u32[]{:S(2)}) collective-permute-start(bf16[256,256]{1,0:T(8,128)(2,1)S(1)} %collective-permute-done.5), channel_id=1, source_target_pairs={{0,8},{1,9},{2,10},{3,11},{4,12},{5,13},{6,14},{7,15},{8,0},{9,1},... | collective-permute-start | bytes 393224 | tf_op jit(solution)/shard_map/ppermute | solution.py:147
  27.1 1.9 %collective-permute-done.8 = bf16[256,256]{1,0:T(8,128)(2,1)S(1)} collective-permute-done((bf16[256,256]{1,0:T(8,128)(2,1)S(1)}, bf16[256,256]{1,0:T(8,128)(2,1)S(1)}, u32[]{:S(2)}, u32[]{:S(2)}) %collective-permute-start.8) | collective-permute-done | bytes 131104 | tf_op jit(solution)/shard_map/ppermute | solution.py:147
  29.0 1.7 %collective-permute-done.9 = bf16[256,256]{1,0:T(8,128)(2,1)S(1)} collective-permute-done((bf16[256,256]{1,0:T(8,128)(2,1)S(1)}, bf16[256,256]{1,0:T(8,128)(2,1)S(1)}, u32[]{:S(2)}, u32[]{:S(2)}) %collective-permute-start.9) | collective-permute-done | bytes 131104 | tf_op jit(solution)/shard_map/ppermute | solution.py:147
  31.4 1.2 %collective-permute-done.10 = bf16[2,64,256]{2,1,0:T(8,128)(2,1)S(1)} collective-permute-done((bf16[2,64,256]{2,1,0:T(8,128)(2,1)S(1)}, bf16[2,64,256]{2,1,0:T(8,128)(2,1)S(1)}, u32[]{:S(2)}, u32[]{:S(2)}) %collective-permute-start.10) | collective-permute-done | bytes 65568 | tf_op jit(solution)/shard_map/ppermute | solution.py:147
  32.8 2.3 %collective-permute-start.13 = (bf16[1,64,256]{2,1,0:T(8,128)(2,1)S(1)}, bf16[1,64,256]{2,1,0:T(8,128)(2,1)S(1)}, u32[]{:S(2)}, u32[]{:S(2)}) collective-permute-start(bf16[1,64,256]{2,1,0:T(8,128)(2,1)S(1)} %get-tuple-element.22.sel_ref), channel_id=1, source_target_pairs={{0,16},{1,17},{2,18},{3,19},{4,20},{5,21},{6,22},{7,23},{8,24},{9,... | collective-permute-start | bytes 98312 | tf_op jit(solution)/shard_map/ppermute | solution.py:147
  35.2 0.6 %collective-permute-start.11 = (bf16[1,64,256]{2,1,0:T(8,128)(2,1)S(1)}, bf16[1,64,256]{2,1,0:T(8,128)(2,1)S(1)}, u32[]{:S(2)}, u32[]{:S(2)}) collective-permute-start(bf16[1,64,256]{2,1,0:T(8,128)(2,1)S(1)} %get-tuple-element.23.sel_ref), channel_id=1, source_target_pairs={{0,16},{1,17},{2,18},{3,19},{4,20},{5,21},{6,22},{7,23},{8,24},{9,... | collective-permute-start | bytes 98312 | tf_op jit(solution)/shard_map/ppermute | solution.py:147
  35.9 2.1 %collective-permute-done.13.got_ref = bf16[1,64,256]{2,1,0:T(8,128)(2,1)S(1)} collective-permute-done((bf16[1,64,256]{2,1,0:T(8,128)(2,1)S(1)}, bf16[1,64,256]{2,1,0:T(8,128)(2,1)S(1)}, u32[]{:S(2)}, u32[]{:S(2)}) %collective-permute-start.13) | collective-permute-done | bytes 32800 | tf_op jit(solution)/shard_map/ppermute | solution.py:147
  38.1 2.1 %attend_sent.1 = bf16[1,64,384]{2,1,0:T(8,128)(2,1)S(1)} custom-call(bf16[1,64,256]{2,1,0:T(8,128)(2,1)S(1)} %get-tuple-element.23.sel_ref, bf16[1,64,256]{2,1,0:T(8,128)(2,1)S(1)} %collective-permute-done.13.got_ref, f32[1,4096]{1,0:T(1,128)S(1)} %bitcast.7, bf16[256,256]{1,0:T(8,128)(2,1)S(1)} %copy-done.4, bf16[256,256]{1,0:T(8,128)(2,1)S(1)} %copy-done.5, ...), custom_call_target="tpu_custom_call" | custom-call | flops 1073741824 | bytes 2097152 | tf_op jit(solution)/shard_map/attend_sent/pallas_call | solution.py:393
  40.2 2.2 %collective-permute-start.14 = (bf16[1,64,384]{2,1,0:T(8,128)(2,1)S(1)}, bf16[1,64,384]{2,1,0:T(8,128)(2,1)S(1)}, u32[]{:S(2)}, u32[]{:S(2)}) collective-permute-start(bf16[1,64,384]{2,1,0:T(8,128)(2,1)S(1)} %attend_sent.1), channel_id=1, source_target_pairs={{0,16},{1,17},{2,18},{3,19},{4,20},{5,21},{6,22},{7,23},{8,24},{9,... | collective-permute-start | bytes 147464 | tf_op jit(solution)/shard_map/ppermute | solution.py:147
  42.4 2.1 %attend_kept.1 = (f32[1,64,256]{2,1,0:T(8,128)S(1)}, f32[1,64,128]{2,1,0:T(8,128)S(1)}) custom-call(bf16[1,64,256]{2,1,0:T(8,128)(2,1)S(1)} %get-tuple-element.22.sel_ref, bf16[1,64,256]{2,1,0:T(8,128)(2,1)S(1)} %collective-permute-done.11.got_ref, f32[1,4096]{1,0:T(1,128)S(1)} %bitcast.8, bf16[256,256]{1,0:T(8,128)(2,1)S(1)} %copy-done.4, ...), custom_call_target="tpu_custom_call" | custom-call | flops 1073741824 | bytes 2097152 | tf_op jit(solution)/shard_map/attend_kept/pallas_call | solution.py:393
  44.5 0.7 %collective-permute-done.14.got_ref = bf16[1,64,384]{2,1,0:T(8,128)(2,1)S(1)} collective-permute-done((bf16[1,64,384]{2,1,0:T(8,128)(2,1)S(1)}, bf16[1,64,384]{2,1,0:T(8,128)(2,1)S(1)}, u32[]{:S(2)}, u32[]{:S(2)}) %collective-permute-start.14) | collective-permute-done | bytes 49184 | tf_op jit(solution)/shard_map/ppermute | solution.py:147
  45.3 0.9 %finish.1 = bf16[1,64,256]{2,1,0:T(8,128)(2,1)} custom-call(f32[1,64,256]{2,1,0:T(8,128)S(1)} %get-tuple-element.25.keep_ref, f32[1,64,128]{2,1,0:T(8,128)S(1)} %get-tuple-element.26.lse_ref, bf16[1,64,384]{2,1,0:T(8,128)(2,1)S(1)} %collective-permute-done.14.got_ref, bf16[256,256]{1,0:T(8,128)(2,1)S(1)} %copy-done.3), custom_call_target="tpu_custom_call" | custom-call | tf_op jit(solution)/shard_map/finish/pallas_call | solution.py:432
  (53 shorter events, 2.7 us)
Async XLA Ops:
  0.0 4.5 %copy-start = (s32[16]{0:T(128)S(1)}, s32[16]{0:T(128)}, u32[]{:S(2)}) copy-start(s32[16]{0:T(128)} %param.10) | copy-start | bytes 196
  0.0 6.0 %copy-start.1 = (bf16[5,3,73,256]{3,2,1,0:T(8,128)(2,1)S(1)}, bf16[5,3,73,256]{3,2,1,0:T(8,128)(2,1)}, u32[]{:S(2)}) copy-start(bf16[5,3,73,256]{3,2,1,0:T(8,128)(2,1)} %weight_ref.1) | copy-start | bytes 1681924
  0.0 1.0 %copy-start.2 = (bf16[73,8,128]{2,1,0:T(8,128)(2,1)S(1)}, bf16[73,8,128]{2,1,0:T(8,128)(2,1)}, u32[]{:S(2)}) copy-start(bf16[73,8,128]{2,1,0:T(8,128)(2,1)} %own_ref.1) | copy-start | bytes 448516
  1.1 5.0 %collective-permute-start.1 = (bf16[2,80,128]{2,1,0:T(8,128)(2,1)S(1)}, bf16[2,80,128]{2,1,0:T(8,128)(2,1)S(1)}, u32[]{:S(2)}, u32[]{:S(2)}) collective-permute-start(bf16[2,80,128]{2,1,0:T(8,128)(2,1)S(1)} %get-tuple-element.18), channel_id=1, source_target_pairs={{0,1},{1,0},{2,3},{3,2},{4,5},{5,4},{6,7},{7,6},{8,9},{9,8},{10,11... | collective-permute-start | bytes 122888 | tf_op jit(solution)/shard_map/ppermute | solution.py:147
  4.1 5.7 %collective-permute-start = (bf16[8,80,128]{2,1,0:T(8,128)(2,1)S(1)}, bf16[8,80,128]{2,1,0:T(8,128)(2,1)S(1)}, u32[]{:S(2)}, u32[]{:S(2)}) collective-permute-start(bf16[8,80,128]{2,1,0:T(8,128)(2,1)S(1)} %get-tuple-element.16.own_ref), channel_id=1, source_target_pairs={{0,1},{1,0},{2,3},{3,2},{4,5},{5,4},{6,7},{7,6},{8,9},{9,8},{10,11... | collective-permute-start | bytes 491528 | tf_op jit(solution)/shard_map/ppermute | solution.py:147
  5.2 0.7 %copy-start.7 = (s32[4,5]{1,0:T(4,128)S(1)}, s32[4,5]{1,0:T(4,128)}, u32[]{:S(2)}) copy-start(s32[4,5]{1,0:T(4,128)} %param.9) | copy-start | bytes 244
  6.1 0.7 %collective-permute-start.2 = (bf16[4,80,128]{2,1,0:T(8,128)(2,1)S(1)}, bf16[4,80,128]{2,1,0:T(8,128)(2,1)S(1)}, u32[]{:S(2)}, u32[]{:S(2)}) collective-permute-start(bf16[4,80,128]{2,1,0:T(8,128)(2,1)S(1)} %pad_maximum_fusion), channel_id=1, source_target_pairs={{1,3},{3,1},{2,4},{4,2},{5,7},{7,5},{6,8},{8,6},{9,11},{11,9},{10,... | collective-permute-start | bytes 245768 | tf_op jit(solution)/shard_map/ppermute | solution.py:156
  11.5 7.1 %collective-permute-start.3 = (bf16[256,256]{1,0:T(8,128)(2,1)S(1)}, bf16[256,256]{1,0:T(8,128)(2,1)S(1)}, u32[]{:S(2)}, u32[]{:S(2)}) collective-permute-start(bf16[256,256]{1,0:T(8,128)(2,1)S(1)} %conv.1), channel_id=1, source_target_pairs={{0,1},{1,0},{2,3},{3,2},{4,5},{5,4},{6,7},{7,6},{8,9},{9,8},{10,11... | collective-permute-start | bytes 393224 | tf_op jit(solution)/shard_map/ppermute | solution.py:147
  13.6 10.4 %collective-permute-start.4 = (bf16[256,256]{1,0:T(8,128)(2,1)S(1)}, bf16[256,256]{1,0:T(8,128)(2,1)S(1)}, u32[]{:S(2)}, u32[]{:S(2)}) collective-permute-start(bf16[256,256]{1,0:T(8,128)(2,1)S(1)} %conv.1), channel_id=1, source_target_pairs={{0,4},{1,5},{2,6},{3,7},{4,0},{5,1},{6,2},{7,3},{8,12},{9,13},{10,... | collective-permute-start | bytes 393224 | tf_op jit(solution)/shard_map/ppermute | solution.py:147
  17.0 5.0 %collective-permute-start.6 = (bf16[256,256]{1,0:T(8,128)(2,1)S(1)}, bf16[256,256]{1,0:T(8,128)(2,1)S(1)}, u32[]{:S(2)}, u32[]{:S(2)}) collective-permute-start(bf16[256,256]{1,0:T(8,128)(2,1)S(1)} %conv.1), channel_id=1, source_target_pairs={{0,8},{1,9},{2,10},{3,11},{4,12},{5,13},{6,14},{7,15},{8,0},{9,1},... | collective-permute-start | bytes 393224 | tf_op jit(solution)/shard_map/ppermute | solution.py:147
  18.6 7.0 %collective-permute-start.5 = (bf16[256,256]{1,0:T(8,128)(2,1)S(1)}, bf16[256,256]{1,0:T(8,128)(2,1)S(1)}, u32[]{:S(2)}, u32[]{:S(2)}) collective-permute-start(bf16[256,256]{1,0:T(8,128)(2,1)S(1)} %collective-permute-done.3), channel_id=1, source_target_pairs={{0,4},{1,5},{2,6},{3,7},{4,0},{5,1},{6,2},{7,3},{8,12},{9,13},{10,... | collective-permute-start | bytes 393224 | tf_op jit(solution)/shard_map/ppermute | solution.py:147
  22.0 5.0 %collective-permute-start.7 = (bf16[256,256]{1,0:T(8,128)(2,1)S(1)}, bf16[256,256]{1,0:T(8,128)(2,1)S(1)}, u32[]{:S(2)}, u32[]{:S(2)}) collective-permute-start(bf16[256,256]{1,0:T(8,128)(2,1)S(1)} %collective-permute-done.6), channel_id=1, source_target_pairs={{0,1},{1,0},{2,3},{3,2},{4,5},{5,4},{6,7},{7,6},{8,9},{9,8},{10,11... | collective-permute-start | bytes 393224 | tf_op jit(solution)/shard_map/ppermute | solution.py:147
  24.0 5.0 %collective-permute-start.8 = (bf16[256,256]{1,0:T(8,128)(2,1)S(1)}, bf16[256,256]{1,0:T(8,128)(2,1)S(1)}, u32[]{:S(2)}, u32[]{:S(2)}) collective-permute-start(bf16[256,256]{1,0:T(8,128)(2,1)S(1)} %collective-permute-done.4), channel_id=1, source_target_pairs={{0,8},{1,9},{2,10},{3,11},{4,12},{5,13},{6,14},{7,15},{8,0},{9,1},... | collective-permute-start | bytes 393224 | tf_op jit(solution)/shard_map/ppermute | solution.py:147
  25.6 5.0 %collective-permute-start.9 = (bf16[256,256]{1,0:T(8,128)(2,1)S(1)}, bf16[256,256]{1,0:T(8,128)(2,1)S(1)}, u32[]{:S(2)}, u32[]{:S(2)}) collective-permute-start(bf16[256,256]{1,0:T(8,128)(2,1)S(1)} %collective-permute-done.5), channel_id=1, source_target_pairs={{0,8},{1,9},{2,10},{3,11},{4,12},{5,13},{6,14},{7,15},{8,0},{9,1},... | collective-permute-start | bytes 393224 | tf_op jit(solution)/shard_map/ppermute | solution.py:147
  30.6 7.4 %copy-start.5 = (bf16[256,256]{1,0:T(8,128)(2,1)S(1)}, bf16[256,256]{1,0:T(8,128)(2,1)}, u32[]{:S(2)}) copy-start(bf16[256,256]{1,0:T(8,128)(2,1)} %wk_ref.3) | copy-start | bytes 393220
  30.6 7.4 %copy-start.6 = (bf16[256,256]{1,0:T(8,128)(2,1)S(1)}, bf16[256,256]{1,0:T(8,128)(2,1)}, u32[]{:S(2)}) copy-start(bf16[256,256]{1,0:T(8,128)(2,1)} %wv_ref.3) | copy-start | bytes 393220
  31.3 6.8 %copy-start.4 = (bf16[256,256]{1,0:T(8,128)(2,1)S(1)}, bf16[256,256]{1,0:T(8,128)(2,1)}, u32[]{:S(2)}) copy-start(bf16[256,256]{1,0:T(8,128)(2,1)} %wq_ref.3) | copy-start | bytes 393220
  31.3 1.3 %collective-permute-start.10 = (bf16[2,64,256]{2,1,0:T(8,128)(2,1)S(1)}, bf16[2,64,256]{2,1,0:T(8,128)(2,1)S(1)}, u32[]{:S(2)}, u32[]{:S(2)}) collective-permute-start(bf16[2,64,256]{2,1,0:T(8,128)(2,1)S(1)} %get-tuple-element.20), channel_id=1, source_target_pairs={{0,2},{1,3},{2,0},{3,1},{4,6},{5,7},{6,4},{7,5},{8,10},{9,11},{10,... | collective-permute-start | bytes 196616 | tf_op jit(solution)/shard_map/ppermute | solution.py:147
  32.6 5.4 %collective-permute-start.12 = (bf16[2048,256]{1,0:T(8,128)(2,1)S(1)}, bf16[2048,256]{1,0:T(8,128)(2,1)S(1)}, u32[]{:S(2)}, u32[]{:S(2)}) collective-permute-start(bf16[2048,256]{1,0:T(8,128)(2,1)S(1)} %constant_dynamic-update-slice_fusion.near_ref.refs_0_), channel_id=1, source_target_pairs={{0,2},{1,3},{2,0},{3,1},{4,6},{5,7},{6,4},{7,5},{8,10},{9,11},{10,... | collective-permute-start | bytes 3145736 | tf_op jit(solution)/shard_map/ppermute | solution.py:147
  32.8 5.2 %collective-permute-start.13 = (bf16[1,64,256]{2,1,0:T(8,128)(2,1)S(1)}, bf16[1,64,256]{2,1,0:T(8,128)(2,1)S(1)}, u32[]{:S(2)}, u32[]{:S(2)}) collective-permute-start(bf16[1,64,256]{2,1,0:T(8,128)(2,1)S(1)} %get-tuple-element.22.sel_ref), channel_id=1, source_target_pairs={{0,16},{1,17},{2,18},{3,19},{4,20},{5,21},{6,22},{7,23},{8,24},{9,... | collective-permute-start | bytes 98312 | tf_op jit(solution)/shard_map/ppermute | solution.py:147
  35.2 7.2 %collective-permute-start.11 = (bf16[1,64,256]{2,1,0:T(8,128)(2,1)S(1)}, bf16[1,64,256]{2,1,0:T(8,128)(2,1)S(1)}, u32[]{:S(2)}, u32[]{:S(2)}) collective-permute-start(bf16[1,64,256]{2,1,0:T(8,128)(2,1)S(1)} %get-tuple-element.23.sel_ref), channel_id=1, source_target_pairs={{0,16},{1,17},{2,18},{3,19},{4,20},{5,21},{6,22},{7,23},{8,24},{9,... | collective-permute-start | bytes 98312 | tf_op jit(solution)/shard_map/ppermute | solution.py:147
  40.2 5.1 %copy-start.3 = (bf16[256,256]{1,0:T(8,128)(2,1)S(1)}, bf16[256,256]{1,0:T(8,128)(2,1)}, u32[]{:S(2)}) copy-start(bf16[256,256]{1,0:T(8,128)(2,1)} %wo_ref.1) | copy-start | bytes 393220
  40.2 5.1 %collective-permute-start.14 = (bf16[1,64,384]{2,1,0:T(8,128)(2,1)S(1)}, bf16[1,64,384]{2,1,0:T(8,128)(2,1)S(1)}, u32[]{:S(2)}, u32[]{:S(2)}) collective-permute-start(bf16[1,64,384]{2,1,0:T(8,128)(2,1)S(1)} %attend_sent.1), channel_id=1, source_target_pairs={{0,16},{1,17},{2,18},{3,19},{4,20},{5,21},{6,22},{7,23},{8,24},{9,... | collective-permute-start | bytes 147464 | tf_op jit(solution)/shard_map/ppermute | solution.py:147

commit v4 on v3

--- a/solution.py
+++ b/solution.py
@@ -441,18 +441,17 @@
 
 def gathered(block, masks):
     blocks = {(0, 0): block}
-    for size in range(1, len(masks) + 1):
+    for mask in masks:
+        blocks[mask] = exchange(block, *mask)
+    whole = (sum(mask[0] for mask in masks), sum(mask[1] for mask in masks))
+    if whole not in blocks:
+        blocks[whole] = exchange(block, *whole)
+    for size in range(2, len(masks)):
         for start in range(len(masks)):
-            if size == len(masks) and start > 0:
-                break
             chosen = [masks[(start + k) % len(masks)] for k in range(size)]
-            key = (0, 0)
-            for mask in chosen:
-                key = (key[0] ^ mask[0], key[1] ^ mask[1])
+            key = (sum(mask[0] for mask in chosen), sum(mask[1] for mask in chosen))
             step = chosen[-1]
-            before = (key[0] ^ step[0], key[1] ^ step[1])
-            if key not in blocks:
-                blocks[key] = exchange(blocks[before], *step)
+            blocks[key] = exchange(blocks[key[0] ^ step[0], key[1] ^ step[1]], *step)
     return blocks
 
 

time: 46.4 us -> 44.8 us (0.966)
  starting transfers between devices: 24.6 us -> 23.4 us
    ppermute x14, starting transfers between devices: 23.9 us -> 22.8 us  [exchange(): return lax.ppermute(x, AXES, pairs)]
  transfers between devices with their start and end apart: 15 -> 15, of which waited for: 7 -> 8; matrix products, arithmetic and copies ran while one was open for 3% -> 3% of each run, Pallas kernels for 9% -> 9%
where the time goes in v4:
time: 44.8 us; the launch traced here: 44.6 us
  starting transfers between devices  23.4 us (52%)
  waiting for transfers between devices  10.3 us (23%)
  Pallas kernels  7.55 us (17%)
  local copies, waits for them, and re-layouts  2.65 us (6%)
  other arithmetic  0.47 us (1%)
    ppermute x14, starting transfers between devices, exchange(): return lax.ppermute(x, AXES, pairs)  22.8 us
    ppermute x14, waiting for transfers between devices, exchange(): return lax.ppermute(x, AXES, pairs)  10.3 us
    pallas_call x2, Pallas kernels, attended(): pl.pallas_call(functools.partial(attend_kernel, len(held)), out_shape=out...  4.18 us
    unnamed x23, local copies, waits for them, and re-layouts  1.73 us
    pallas_call x1, Pallas kernels, features_of(): pl.pallas_call(conv_kernel, out_shape=jax.ShapeDtypeStruct((bands * lons,...  1.72 us
    pallas_call x1, Pallas kernels, finished(): pl.pallas_call(finish_kernel, out_shape=jax.ShapeDtypeStruct(keep.shape,...  0.94 us
  transfers between devices with their start and end apart: 15, of which 8 were waited for; matrix products, arithmetic and copies ran while one was open for 3% of the time, Pallas kernels for 9%

profile of v4, /device:TPU:0, one launch (start us, length us, event | category | flops | bytes accessed | tf_op | source)
XLA Modules:
  0.0 44.6 jit_solution(16457491901007890805)
XLA Ops:
  0.0 1.0 %copy-done.2 = bf16[73,8,128]{2,1,0:T(8,128)(2,1)S(1)} copy-done((bf16[73,8,128]{2,1,0:T(8,128)(2,1)S(1)}, bf16[73,8,128]{2,1,0:T(8,128)(2,1)}, u32[]{:S(2)}) %copy-start.2) | copy-done | bytes 149528
  1.1 3.0 %collective-permute-start.1 = (bf16[2,80,128]{2,1,0:T(8,128)(2,1)S(1)}, bf16[2,80,128]{2,1,0:T(8,128)(2,1)S(1)}, u32[]{:S(2)}, u32[]{:S(2)}) collective-permute-start(bf16[2,80,128]{2,1,0:T(8,128)(2,1)S(1)} %get-tuple-element.18), channel_id=1, source_target_pairs={{0,1},{1,0},{2,3},{3,2},{4,5},{5,4},{6,7},{7,6},{8,9},{9,8},{10,11... | collective-permute-start | bytes 122888 | tf_op jit(solution)/shard_map/ppermute | solution.py:147
  4.5 0.6 %gather_fusion = s32[4]{0:T(128)S(1)} fusion(s32[16]{0:T(128)S(1)} %copy-done, s32[1024]{0:T(1024)S(1)} %pad_clamp_fusion), kind=kCustom, calls=%fused_computation | custom fusion | bytes 48 | tf_op jit(solution)/shard_map/gather | solution.py:487
  5.2 0.7 %copy-done.7 = s32[4,5]{1,0:T(4,128)S(1)} copy-done((s32[4,5]{1,0:T(4,128)S(1)}, s32[4,5]{1,0:T(4,128)}, u32[]{:S(2)}) %copy-start.7) | copy-done | bytes 104
  6.1 0.7 %collective-permute-start.2 = (bf16[4,80,128]{2,1,0:T(8,128)(2,1)S(1)}, bf16[4,80,128]{2,1,0:T(8,128)(2,1)S(1)}, u32[]{:S(2)}, u32[]{:S(2)}) collective-permute-start(bf16[4,80,128]{2,1,0:T(8,128)(2,1)S(1)} %pad_maximum_fusion), channel_id=1, source_target_pairs={{1,3},{3,1},{2,4},{4,2},{5,7},{7,5},{6,8},{8,6},{9,11},{11,9},{10,... | collective-permute-start | bytes 245768 | tf_op jit(solution)/shard_map/ppermute | solution.py:156
  6.8 3.0 %collective-permute-done.other_ref = bf16[8,80,128]{2,1,0:T(8,128)(2,1)S(1)} collective-permute-done((bf16[8,80,128]{2,1,0:T(8,128)(2,1)S(1)}, bf16[8,80,128]{2,1,0:T(8,128)(2,1)S(1)}, u32[]{:S(2)}, u32[]{:S(2)}) %collective-permute-start) | collective-permute-done | bytes 163872 | tf_op jit(solution)/shard_map/ppermute | solution.py:147
  9.7 1.7 %conv.1 = bf16[256,256]{1,0:T(8,128)(2,1)S(1)} custom-call(s32[2,5]{1,0:T(2,128)S(1)} %constant_dynamic-slice_fusion.rows_ref, bf16[8,80,128]{2,1,0:T(8,128)(2,1)S(1)} %get-tuple-element.16.own_ref, bf16[8,80,128]{2,1,0:T(8,128)(2,1)S(1)} %collective-permute-done.other_ref, bf16[4,80,128]{2,1,0:T(8,128)(2,1)S(1)} %collective-permute-done.2.edge_ref, ...), custom_call_target="tpu_custom_call" | custom-call | tf_op jit(solution)/shard_map/conv/pallas_call | solution.py:269
  11.5 2.1 %collective-permute-start.3 = (bf16[256,256]{1,0:T(8,128)(2,1)S(1)}, bf16[256,256]{1,0:T(8,128)(2,1)S(1)}, u32[]{:S(2)}, u32[]{:S(2)}) collective-permute-start(bf16[256,256]{1,0:T(8,128)(2,1)S(1)} %conv.1), channel_id=1, source_target_pairs={{0,1},{1,0},{2,3},{3,2},{4,5},{5,4},{6,7},{7,6},{8,9},{9,8},{10,11... | collective-permute-start | bytes 393224 | tf_op jit(solution)/shard_map/ppermute | solution.py:147
  13.6 3.4 %collective-permute-start.4 = (bf16[256,256]{1,0:T(8,128)(2,1)S(1)}, bf16[256,256]{1,0:T(8,128)(2,1)S(1)}, u32[]{:S(2)}, u32[]{:S(2)}) collective-permute-start(bf16[256,256]{1,0:T(8,128)(2,1)S(1)} %conv.1), channel_id=1, source_target_pairs={{0,4},{1,5},{2,6},{3,7},{4,0},{5,1},{6,2},{7,3},{8,12},{9,13},{10,... | collective-permute-start | bytes 393224 | tf_op jit(solution)/shard_map/ppermute | solution.py:147
  17.0 1.6 %collective-permute-start.6 = (bf16[256,256]{1,0:T(8,128)(2,1)S(1)}, bf16[256,256]{1,0:T(8,128)(2,1)S(1)}, u32[]{:S(2)}, u32[]{:S(2)}) collective-permute-start(bf16[256,256]{1,0:T(8,128)(2,1)S(1)} %conv.1), channel_id=1, source_target_pairs={{0,8},{1,9},{2,10},{3,11},{4,12},{5,13},{6,14},{7,15},{8,0},{9,1},... | collective-permute-start | bytes 393224 | tf_op jit(solution)/shard_map/ppermute | solution.py:147
  18.6 1.5 %collective-permute-start.9 = (bf16[256,256]{1,0:T(8,128)(2,1)S(1)}, bf16[256,256]{1,0:T(8,128)(2,1)S(1)}, u32[]{:S(2)}, u32[]{:S(2)}) collective-permute-start(bf16[256,256]{1,0:T(8,128)(2,1)S(1)} %conv.1), channel_id=1, source_target_pairs={{0,13},{1,12},{2,15},{3,14},{4,9},{5,8},{6,11},{7,10},{8,5},{9,4},... | collective-permute-start | bytes 393224 | tf_op jit(solution)/shard_map/ppermute | solution.py:147
  20.1 1.9 %collective-permute-start.5 = (bf16[256,256]{1,0:T(8,128)(2,1)S(1)}, bf16[256,256]{1,0:T(8,128)(2,1)S(1)}, u32[]{:S(2)}, u32[]{:S(2)}) collective-permute-start(bf16[256,256]{1,0:T(8,128)(2,1)S(1)} %collective-permute-done.3), channel_id=1, source_target_pairs={{0,4},{1,5},{2,6},{3,7},{4,0},{5,1},{6,2},{7,3},{8,12},{9,13},{10,... | collective-permute-start | bytes 393224 | tf_op jit(solution)/shard_map/ppermute | solution.py:147
  22.0 0.9 %collective-permute-done.6 = bf16[256,256]{1,0:T(8,128)(2,1)S(1)} collective-permute-done((bf16[256,256]{1,0:T(8,128)(2,1)S(1)}, bf16[256,256]{1,0:T(8,128)(2,1)S(1)}, u32[]{:S(2)}, u32[]{:S(2)}) %collective-permute-start.6) | collective-permute-done | bytes 131104 | tf_op jit(solution)/shard_map/ppermute | solution.py:147
  22.9 1.5 %collective-permute-start.7 = (bf16[256,256]{1,0:T(8,128)(2,1)S(1)}, bf16[256,256]{1,0:T(8,128)(2,1)S(1)}, u32[]{:S(2)}, u32[]{:S(2)}) collective-permute-start(bf16[256,256]{1,0:T(8,128)(2,1)S(1)} %collective-permute-done.6), channel_id=1, source_target_pairs={{0,1},{1,0},{2,3},{3,2},{4,5},{5,4},{6,7},{7,6},{8,9},{9,8},{10,11... | collective-permute-start | bytes 393224 | tf_op jit(solution)/shard_map/ppermute | solution.py:147
  24.4 1.6 %collective-permute-start.8 = (bf16[256,256]{1,0:T(8,128)(2,1)S(1)}, bf16[256,256]{1,0:T(8,128)(2,1)S(1)}, u32[]{:S(2)}, u32[]{:S(2)}) collective-permute-start(bf16[256,256]{1,0:T(8,128)(2,1)S(1)} %collective-permute-done.4), channel_id=1, source_target_pairs={{0,8},{1,9},{2,10},{3,11},{4,12},{5,13},{6,14},{7,15},{8,0},{9,1},... | collective-permute-start | bytes 393224 | tf_op jit(solution)/shard_map/ppermute | solution.py:147
  26.6 1.3 %collective-permute-done.7 = bf16[256,256]{1,0:T(8,128)(2,1)S(1)} collective-permute-done((bf16[256,256]{1,0:T(8,128)(2,1)S(1)}, bf16[256,256]{1,0:T(8,128)(2,1)S(1)}, u32[]{:S(2)}, u32[]{:S(2)}) %collective-permute-start.7) | collective-permute-done | bytes 131104 | tf_op jit(solution)/shard_map/ppermute | solution.py:147
  28.0 1.4 %collective-permute-done.8 = bf16[256,256]{1,0:T(8,128)(2,1)S(1)} collective-permute-done((bf16[256,256]{1,0:T(8,128)(2,1)S(1)}, bf16[256,256]{1,0:T(8,128)(2,1)S(1)}, u32[]{:S(2)}, u32[]{:S(2)}) %collective-permute-start.8) | collective-permute-done | bytes 131104 | tf_op jit(solution)/shard_map/ppermute | solution.py:147
  30.1 1.2 %collective-permute-done.10 = bf16[2,64,256]{2,1,0:T(8,128)(2,1)S(1)} collective-permute-done((bf16[2,64,256]{2,1,0:T(8,128)(2,1)S(1)}, bf16[2,64,256]{2,1,0:T(8,128)(2,1)S(1)}, u32[]{:S(2)}, u32[]{:S(2)}) %collective-permute-start.10) | collective-permute-done | bytes 65568 | tf_op jit(solution)/shard_map/ppermute | solution.py:147
  31.6 2.6 %collective-permute-start.13 = (bf16[1,64,256]{2,1,0:T(8,128)(2,1)S(1)}, bf16[1,64,256]{2,1,0:T(8,128)(2,1)S(1)}, u32[]{:S(2)}, u32[]{:S(2)}) collective-permute-start(bf16[1,64,256]{2,1,0:T(8,128)(2,1)S(1)} %get-tuple-element.22.sel_ref), channel_id=1, source_target_pairs={{0,16},{1,17},{2,18},{3,19},{4,20},{5,21},{6,22},{7,23},{8,24},{9,... | collective-permute-start | bytes 98312 | tf_op jit(solution)/shard_map/ppermute | solution.py:147
  34.7 1.8 %collective-permute-done.13.got_ref = bf16[1,64,256]{2,1,0:T(8,128)(2,1)S(1)} collective-permute-done((bf16[1,64,256]{2,1,0:T(8,128)(2,1)S(1)}, bf16[1,64,256]{2,1,0:T(8,128)(2,1)S(1)}, u32[]{:S(2)}, u32[]{:S(2)}) %collective-permute-start.13) | collective-permute-done | bytes 32800 | tf_op jit(solution)/shard_map/ppermute | solution.py:147
  36.5 2.1 %attend_sent.1 = bf16[1,64,384]{2,1,0:T(8,128)(2,1)S(1)} custom-call(bf16[1,64,256]{2,1,0:T(8,128)(2,1)S(1)} %get-tuple-element.23.sel_ref, bf16[1,64,256]{2,1,0:T(8,128)(2,1)S(1)} %collective-permute-done.13.got_ref, f32[1,4096]{1,0:T(1,128)S(1)} %bitcast.7, bf16[256,256]{1,0:T(8,128)(2,1)S(1)} %copy-done.4, bf16[256,256]{1,0:T(8,128)(2,1)S(1)} %copy-done.5, ...), custom_call_target="tpu_custom_call" | custom-call | flops 1073741824 | bytes 2097152 | tf_op jit(solution)/shard_map/attend_sent/pallas_call | solution.py:393
  38.6 2.8 %collective-permute-start.14 = (bf16[1,64,384]{2,1,0:T(8,128)(2,1)S(1)}, bf16[1,64,384]{2,1,0:T(8,128)(2,1)S(1)}, u32[]{:S(2)}, u32[]{:S(2)}) collective-permute-start(bf16[1,64,384]{2,1,0:T(8,128)(2,1)S(1)} %attend_sent.1), channel_id=1, source_target_pairs={{0,16},{1,17},{2,18},{3,19},{4,20},{5,21},{6,22},{7,23},{8,24},{9,... | collective-permute-start | bytes 147464 | tf_op jit(solution)/shard_map/ppermute | solution.py:147
  41.5 2.1 %attend_kept.1 = (f32[1,64,256]{2,1,0:T(8,128)S(1)}, f32[1,64,128]{2,1,0:T(8,128)S(1)}) custom-call(bf16[1,64,256]{2,1,0:T(8,128)(2,1)S(1)} %get-tuple-element.22.sel_ref, bf16[1,64,256]{2,1,0:T(8,128)(2,1)S(1)} %collective-permute-done.11.got_ref, f32[1,4096]{1,0:T(1,128)S(1)} %bitcast.8, bf16[256,256]{1,0:T(8,128)(2,1)S(1)} %copy-done.4, ...), custom_call_target="tpu_custom_call" | custom-call | flops 1073741824 | bytes 2097152 | tf_op jit(solution)/shard_map/attend_kept/pallas_call | solution.py:393
  43.7 0.9 %finish.1 = bf16[1,64,256]{2,1,0:T(8,128)(2,1)} custom-call(f32[1,64,256]{2,1,0:T(8,128)S(1)} %get-tuple-element.25.keep_ref, f32[1,64,128]{2,1,0:T(8,128)S(1)} %get-tuple-element.26.lse_ref, bf16[1,64,384]{2,1,0:T(8,128)(2,1)S(1)} %collective-permute-done.14.got_ref, bf16[256,256]{1,0:T(8,128)(2,1)S(1)} %copy-done.3), custom_call_target="tpu_custom_call" | custom-call | tf_op jit(solution)/shard_map/finish/pallas_call | solution.py:432
  (53 shorter events, 3.1 us)
Async XLA Ops:
  0.0 4.5 %copy-start = (s32[16]{0:T(128)S(1)}, s32[16]{0:T(128)}, u32[]{:S(2)}) copy-start(s32[16]{0:T(128)} %param.10) | copy-start | bytes 196
  0.0 6.0 %copy-start.1 = (bf16[5,3,73,256]{3,2,1,0:T(8,128)(2,1)S(1)}, bf16[5,3,73,256]{3,2,1,0:T(8,128)(2,1)}, u32[]{:S(2)}) copy-start(bf16[5,3,73,256]{3,2,1,0:T(8,128)(2,1)} %weight_ref.1) | copy-start | bytes 1681924
  0.0 1.0 %copy-start.2 = (bf16[73,8,128]{2,1,0:T(8,128)(2,1)S(1)}, bf16[73,8,128]{2,1,0:T(8,128)(2,1)}, u32[]{:S(2)}) copy-start(bf16[73,8,128]{2,1,0:T(8,128)(2,1)} %own_ref.1) | copy-start | bytes 448516
  1.1 5.0 %collective-permute-start.1 = (bf16[2,80,128]{2,1,0:T(8,128)(2,1)S(1)}, bf16[2,80,128]{2,1,0:T(8,128)(2,1)S(1)}, u32[]{:S(2)}, u32[]{:S(2)}) collective-permute-start(bf16[2,80,128]{2,1,0:T(8,128)(2,1)S(1)} %get-tuple-element.18), channel_id=1, source_target_pairs={{0,1},{1,0},{2,3},{3,2},{4,5},{5,4},{6,7},{7,6},{8,9},{9,8},{10,11... | collective-permute-start | bytes 122888 | tf_op jit(solution)/shard_map/ppermute | solution.py:147
  4.1 5.7 %collective-permute-start = (bf16[8,80,128]{2,1,0:T(8,128)(2,1)S(1)}, bf16[8,80,128]{2,1,0:T(8,128)(2,1)S(1)}, u32[]{:S(2)}, u32[]{:S(2)}) collective-permute-start(bf16[8,80,128]{2,1,0:T(8,128)(2,1)S(1)} %get-tuple-element.16.own_ref), channel_id=1, source_target_pairs={{0,1},{1,0},{2,3},{3,2},{4,5},{5,4},{6,7},{7,6},{8,9},{9,8},{10,11... | collective-permute-start | bytes 491528 | tf_op jit(solution)/shard_map/ppermute | solution.py:147
  5.2 0.7 %copy-start.7 = (s32[4,5]{1,0:T(4,128)S(1)}, s32[4,5]{1,0:T(4,128)}, u32[]{:S(2)}) copy-start(s32[4,5]{1,0:T(4,128)} %param.9) | copy-start | bytes 244
  6.1 0.7 %collective-permute-start.2 = (bf16[4,80,128]{2,1,0:T(8,128)(2,1)S(1)}, bf16[4,80,128]{2,1,0:T(8,128)(2,1)S(1)}, u32[]{:S(2)}, u32[]{:S(2)}) collective-permute-start(bf16[4,80,128]{2,1,0:T(8,128)(2,1)S(1)} %pad_maximum_fusion), channel_id=1, source_target_pairs={{1,3},{3,1},{2,4},{4,2},{5,7},{7,5},{6,8},{8,6},{9,11},{11,9},{10,... | collective-permute-start | bytes 245768 | tf_op jit(solution)/shard_map/ppermute | solution.py:156
  11.5 8.7 %collective-permute-start.3 = (bf16[256,256]{1,0:T(8,128)(2,1)S(1)}, bf16[256,256]{1,0:T(8,128)(2,1)S(1)}, u32[]{:S(2)}, u32[]{:S(2)}) collective-permute-start(bf16[256,256]{1,0:T(8,128)(2,1)S(1)} %conv.1), channel_id=1, source_target_pairs={{0,1},{1,0},{2,3},{3,2},{4,5},{5,4},{6,7},{7,6},{8,9},{9,8},{10,11... | collective-permute-start | bytes 393224 | tf_op jit(solution)/shard_map/ppermute | solution.py:147
  13.6 10.8 %collective-permute-start.4 = (bf16[256,256]{1,0:T(8,128)(2,1)S(1)}, bf16[256,256]{1,0:T(8,128)(2,1)S(1)}, u32[]{:S(2)}, u32[]{:S(2)}) collective-permute-start(bf16[256,256]{1,0:T(8,128)(2,1)S(1)} %conv.1), channel_id=1, source_target_pairs={{0,4},{1,5},{2,6},{3,7},{4,0},{5,1},{6,2},{7,3},{8,12},{9,13},{10,... | collective-permute-start | bytes 393224 | tf_op jit(solution)/shard_map/ppermute | solution.py:147
  17.0 5.9 %collective-permute-start.6 = (bf16[256,256]{1,0:T(8,128)(2,1)S(1)}, bf16[256,256]{1,0:T(8,128)(2,1)S(1)}, u32[]{:S(2)}, u32[]{:S(2)}) collective-permute-start(bf16[256,256]{1,0:T(8,128)(2,1)S(1)} %conv.1), channel_id=1, source_target_pairs={{0,8},{1,9},{2,10},{3,11},{4,12},{5,13},{6,14},{7,15},{8,0},{9,1},... | collective-permute-start | bytes 393224 | tf_op jit(solution)/shard_map/ppermute | solution.py:147
  18.6 10.8 %collective-permute-start.9 = (bf16[256,256]{1,0:T(8,128)(2,1)S(1)}, bf16[256,256]{1,0:T(8,128)(2,1)S(1)}, u32[]{:S(2)}, u32[]{:S(2)}) collective-permute-start(bf16[256,256]{1,0:T(8,128)(2,1)S(1)} %conv.1), channel_id=1, source_target_pairs={{0,13},{1,12},{2,15},{3,14},{4,9},{5,8},{6,11},{7,10},{8,5},{9,4},... | collective-permute-start | bytes 393224 | tf_op jit(solution)/shard_map/ppermute | solution.py:147
  20.1 6.4 %collective-permute-start.5 = (bf16[256,256]{1,0:T(8,128)(2,1)S(1)}, bf16[256,256]{1,0:T(8,128)(2,1)S(1)}, u32[]{:S(2)}, u32[]{:S(2)}) collective-permute-start(bf16[256,256]{1,0:T(8,128)(2,1)S(1)} %collective-permute-done.3), channel_id=1, source_target_pairs={{0,4},{1,5},{2,6},{3,7},{4,0},{5,1},{6,2},{7,3},{8,12},{9,13},{10,... | collective-permute-start | bytes 393224 | tf_op jit(solution)/shard_map/ppermute | solution.py:147
  22.9 5.1 %collective-permute-start.7 = (bf16[256,256]{1,0:T(8,128)(2,1)S(1)}, bf16[256,256]{1,0:T(8,128)(2,1)S(1)}, u32[]{:S(2)}, u32[]{:S(2)}) collective-permute-start(bf16[256,256]{1,0:T(8,128)(2,1)S(1)} %collective-permute-done.6), channel_id=1, source_target_pairs={{0,1},{1,0},{2,3},{3,2},{4,5},{5,4},{6,7},{7,6},{8,9},{9,8},{10,11... | collective-permute-start | bytes 393224 | tf_op jit(solution)/shard_map/ppermute | solution.py:147
  24.4 5.0 %collective-permute-start.8 = (bf16[256,256]{1,0:T(8,128)(2,1)S(1)}, bf16[256,256]{1,0:T(8,128)(2,1)S(1)}, u32[]{:S(2)}, u32[]{:S(2)}) collective-permute-start(bf16[256,256]{1,0:T(8,128)(2,1)S(1)} %collective-permute-done.4), channel_id=1, source_target_pairs={{0,8},{1,9},{2,10},{3,11},{4,12},{5,13},{6,14},{7,15},{8,0},{9,1},... | collective-permute-start | bytes 393224 | tf_op jit(solution)/shard_map/ppermute | solution.py:147
  29.4 7.1 %copy-start.5 = (bf16[256,256]{1,0:T(8,128)(2,1)S(1)}, bf16[256,256]{1,0:T(8,128)(2,1)}, u32[]{:S(2)}) copy-start(bf16[256,256]{1,0:T(8,128)(2,1)} %wk_ref.3) | copy-start | bytes 393220
  29.4 7.1 %copy-start.6 = (bf16[256,256]{1,0:T(8,128)(2,1)S(1)}, bf16[256,256]{1,0:T(8,128)(2,1)}, u32[]{:S(2)}) copy-start(bf16[256,256]{1,0:T(8,128)(2,1)} %wv_ref.3) | copy-start | bytes 393220
  30.0 6.5 %copy-start.4 = (bf16[256,256]{1,0:T(8,128)(2,1)S(1)}, bf16[256,256]{1,0:T(8,128)(2,1)}, u32[]{:S(2)}) copy-start(bf16[256,256]{1,0:T(8,128)(2,1)} %wq_ref.3) | copy-start | bytes 393220
  30.0 1.3 %collective-permute-start.10 = (bf16[2,64,256]{2,1,0:T(8,128)(2,1)S(1)}, bf16[2,64,256]{2,1,0:T(8,128)(2,1)S(1)}, u32[]{:S(2)}, u32[]{:S(2)}) collective-permute-start(bf16[2,64,256]{2,1,0:T(8,128)(2,1)S(1)} %get-tuple-element.20), channel_id=1, source_target_pairs={{0,2},{1,3},{2,0},{3,1},{4,6},{5,7},{6,4},{7,5},{8,10},{9,11},{10,... | collective-permute-start | bytes 196616 | tf_op jit(solution)/shard_map/ppermute | solution.py:147
  31.4 5.0 %collective-permute-start.12 = (bf16[2048,256]{1,0:T(8,128)(2,1)S(1)}, bf16[2048,256]{1,0:T(8,128)(2,1)S(1)}, u32[]{:S(2)}, u32[]{:S(2)}) collective-permute-start(bf16[2048,256]{1,0:T(8,128)(2,1)S(1)} %constant_dynamic-update-slice_fusion.near_ref.refs_0_), channel_id=1, source_target_pairs={{0,2},{1,3},{2,0},{3,1},{4,6},{5,7},{6,4},{7,5},{8,10},{9,11},{10,... | collective-permute-start | bytes 3145736 | tf_op jit(solution)/shard_map/ppermute | solution.py:147
  31.6 4.8 %collective-permute-start.13 = (bf16[1,64,256]{2,1,0:T(8,128)(2,1)S(1)}, bf16[1,64,256]{2,1,0:T(8,128)(2,1)S(1)}, u32[]{:S(2)}, u32[]{:S(2)}) collective-permute-start(bf16[1,64,256]{2,1,0:T(8,128)(2,1)S(1)} %get-tuple-element.22.sel_ref), channel_id=1, source_target_pairs={{0,16},{1,17},{2,18},{3,19},{4,20},{5,21},{6,22},{7,23},{8,24},{9,... | collective-permute-start | bytes 98312 | tf_op jit(solution)/shard_map/ppermute | solution.py:147
  34.3 7.2 %collective-permute-start.11 = (bf16[1,64,256]{2,1,0:T(8,128)(2,1)S(1)}, bf16[1,64,256]{2,1,0:T(8,128)(2,1)S(1)}, u32[]{:S(2)}, u32[]{:S(2)}) collective-permute-start(bf16[1,64,256]{2,1,0:T(8,128)(2,1)S(1)} %get-tuple-element.23.sel_ref), channel_id=1, source_target_pairs={{0,16},{1,17},{2,18},{3,19},{4,20},{5,21},{6,22},{7,23},{8,24},{9,... | collective-permute-start | bytes 98312 | tf_op jit(solution)/shard_map/ppermute | solution.py:147
  38.6 5.1 %copy-start.3 = (bf16[256,256]{1,0:T(8,128)(2,1)S(1)}, bf16[256,256]{1,0:T(8,128)(2,1)}, u32[]{:S(2)}) copy-start(bf16[256,256]{1,0:T(8,128)(2,1)} %wo_ref.1) | copy-start | bytes 393220
  38.6 5.1 %collective-permute-start.14 = (bf16[1,64,384]{2,1,0:T(8,128)(2,1)S(1)}, bf16[1,64,384]{2,1,0:T(8,128)(2,1)S(1)}, u32[]{:S(2)}, u32[]{:S(2)}) collective-permute-start(bf16[1,64,384]{2,1,0:T(8,128)(2,1)S(1)} %attend_sent.1), channel_id=1, source_target_pairs={{0,16},{1,17},{2,18},{3,19},{4,20},{5,21},{6,22},{7,23},{8,24},{9,... | collective-permute-start | bytes 147464 | tf_op jit(solution)/shard_map/ppermute | solution.py:147

commit v5 on v4

--- a/solution.py
+++ b/solution.py
@@ -147,36 +147,32 @@
     return lax.ppermute(x, AXES, pairs)
 
 
-def vertical(x):
+def across(x):
     lats, lons = lax.axis_size("lat"), lax.axis_size("lon")
     pairs = []
-    for i in range(1, lats):
-        j = i % lons
-        pairs += [((i - 1) * lons + j, i * lons + j), (i * lons + j, (i - 1) * lons + j)]
+    for i in range(2, lats, 2):
+        for j in range(lons):
+            pairs += [((i - 1) * lons + j, i * lons + j), (i * lons + j, (i - 1) * lons + j)]
     return lax.ppermute(x, AXES, pairs)
 
 
-def lines_of(ref, strided, deep):
-    channels, rows, lons = ref.shape
-    strided[0 : channels * rows] = ref[...].astype(F32).reshape(channels * rows, lons)
+def rows_kernel(odd_ref, own_ref, lines_ref, far_ref, chip_ref, strided):
+    channels, rows, lons = own_ref.shape
+    deep = lines_ref.shape[1]
+    edge = far_ref.shape[0]
+    strided[0 : channels * rows] = own_ref[...].astype(F32).reshape(channels * rows, lons)
     strided[channels * rows :] = jnp.zeros(((deep - channels) * rows, lons), F32)
-    return [strided[pl.ds(row, deep, stride=rows), :].astype(BF16) for row in range(rows)]
-
-
-def rows_kernel(lower_ref, own_ref, lines_ref, same_ref, cross_ref, strided):
-    rows, deep, _ = lines_ref.shape
-    edge = same_ref.shape[0]
-    lines = lines_of(own_ref, strided, deep)
+    lines = [strided[pl.ds(row, deep, stride=rows), :].astype(BF16) for row in range(rows)]
     for row in range(rows):
         lines_ref[row] = lines[row]
-    lower = lower_ref[0] != 0
+    odd = odd_ref[0] != 0
     for row in range(edge):
         top, bottom = lines[row], lines[rows - edge + row]
-        same_ref[row] = jnp.where(lower, bottom, top)
-        cross_ref[row] = jnp.where(lower, top, bottom)
-
-
-def rows_of(lower, own, edge, deep):
+        far_ref[row] = jnp.where(odd, bottom, top)
+        chip_ref[row] = jnp.where(odd, top, bottom)
+
+
+def rows_of(odd, own, edge, deep):
     _, rows, lons = own.shape
     vmem = pl.BlockSpec(memory_space=pltpu.VMEM)
     return pl.pallas_call(
@@ -191,10 +187,10 @@
         scratch_shapes=[pltpu.VMEM((deep * rows, lons), F32)],
         compiler_params=pltpu.CompilerParams(vmem_limit_bytes=4 * 2**20),
         name="rows",
-    )(lower, own)
-
-
-def weights_kernel(weight_ref, out_ref):
+    )(odd, own)
+
+
+def weights_kernel(weight_ref, picks_ref, out_ref, hits_ref):
     slots, taps, channels, width = weight_ref.shape
     deep = out_ref.shape[0] // (slots * taps)
     blank = jnp.zeros((deep - channels, width), BF16)
@@ -202,90 +198,169 @@
         for tap in range(taps):
             at = (slot * taps + tap) * deep
             out_ref[at : at + deep] = jnp.concatenate([weight_ref[slot, tap], blank], axis=0)
-
-
-def weights_of(conv_weight, deep):
+    picks = picks_ref[...]
+    row = lax.broadcasted_iota(jnp.int32, (128, 128), 0)
+    lane = lax.broadcasted_iota(jnp.int32, (128, 128), 1)
+    for slot in range(slots):
+        hits = jnp.zeros((128, 128), F32)
+        for band in range(picks.shape[0]):
+            hits = jnp.where((row == picks[band, slot]) & (lane == band), 1.0, hits)
+        hits_ref[:, slot * 128 : (slot + 1) * 128] = hits.astype(BF16)
+
+
+def weights_of(conv_weight, picks, deep):
     slots, taps, _, width = conv_weight.shape
     vmem = pl.BlockSpec(memory_space=pltpu.VMEM)
     return pl.pallas_call(
         weights_kernel,
-        out_shape=jax.ShapeDtypeStruct((slots * taps * deep, width), BF16),
-        in_specs=[vmem],
-        out_specs=vmem,
+        out_shape=(
+            jax.ShapeDtypeStruct((slots * taps * deep, width), BF16),
+            jax.ShapeDtypeStruct((128, slots * 128), BF16),
+        ),
+        in_specs=[vmem, vmem],
+        out_specs=(vmem, vmem),
         compiler_params=pltpu.CompilerParams(vmem_limit_bytes=4 * 2**20),
         cost_estimate=pl.CostEstimate(
             flops=0, bytes_accessed=4 * conv_weight.size, transcendentals=0
         ),
         name="weights",
-    )(conv_weight)
+    )(conv_weight, picks)
+
+
+def columns_kernel(lines_ref, above_ref, below_ref, out_ref):
+    rows = [ref[k] for ref in (above_ref, lines_ref, below_ref) for k in range(ref.shape[0])]
+    lane = lax.broadcasted_iota(jnp.int32, (1, 128), 1)
+    out = jnp.zeros(out_ref.shape, F32)
+    for index, row in enumerate(rows):
+        last = row[:, row.shape[1] - 128 :].astype(F32)[:, 127:128]
+        out = jnp.where(lane == index, last, out)
+    out_ref[...] = out.astype(BF16)
+
+
+def last_columns(lines, above, below):
+    vmem = pl.BlockSpec(memory_space=pltpu.VMEM)
+    return pl.pallas_call(
+        columns_kernel,
+        out_shape=jax.ShapeDtypeStruct((lines.shape[1], 128), BF16),
+        in_specs=[vmem] * 3,
+        out_specs=vmem,
+        compiler_params=pltpu.CompilerParams(vmem_limit_bytes=4 * 2**20),
+        name="columns",
+    )(lines, above, below)
+
+
+def normed(raw):
+    return raw * lax.rsqrt(jnp.mean(raw * raw, axis=-1, keepdims=True) + 1e-06)
 
 
 def conv_kernel(
-    rows_ref, own_ref, other_ref, edge_ref, weight_ref, out_ref, taken, patches
+    picks_ref, lines_ref, above_ref, below_ref, weight_ref, out_ref, first_ref, taken, patches
 ):
-    rows, deep, lons = own_ref.shape
-    edge = edge_ref.shape[0] // 2
-    width = lons
-    bands = out_ref.shape[0] // width
-    slots = rows_ref.shape[1]
+    _, deep, lons = lines_ref.shape
+    width = lons // 2
+    bands, slots = picks_ref.shape
     taps = weight_ref.shape[0] // (slots * deep)
-    column = lax.broadcasted_iota(jnp.int32, (2 * lons, taps * width), 0)
-    place = lax.broadcasted_iota(jnp.int32, (2 * lons, taps * width), 1)
-    wanted = lax.rem(2 * (place % width) + place // width - 1 + 2 * lons, 2 * lons)
+    rows = [ref[k] for ref in (above_ref, lines_ref, below_ref) for k in range(ref.shape[0])]
+    column = lax.broadcasted_iota(jnp.int32, (lons, taps * lons), 0)
+    place = lax.broadcasted_iota(jnp.int32, (lons, taps * lons), 1)
+    wanted = 2 * (place % width) + place // lons - 1
     choose = (column == wanted).astype(F32).astype(BF16)
-    near = [own_ref[row] for row in range(rows)] + [edge_ref[row] for row in range(edge)]
-    far = [other_ref[row] for row in range(rows)] + [edge_ref[edge + row] for row in range(edge)]
-    both = jnp.concatenate(
-        [jnp.concatenate(near, axis=0), jnp.concatenate(far, axis=0)], axis=1
-    )
-    split = jnp.dot(both, choose, preferred_element_type=F32).astype(BF16)
-    for row in range(rows):
-        taken[edge + row] = split[row * deep : (row + 1) * deep]
-    for row in range(edge):
-        piece = split[(rows + row) * deep : (rows + row + 1) * deep]
-        taken[row] = piece
-        taken[edge + rows + row] = piece
+    split = jnp.dot(
+        jnp.concatenate(rows, axis=0), choose, preferred_element_type=F32
+    ).astype(BF16)
+    for row in range(len(rows)):
+        taken[row] = split[row * deep : (row + 1) * deep]
+    left = lax.broadcasted_iota(jnp.int32, (1, lons), 1) < width
+    picks = picks_ref[...]
     for slot in range(slots):
-        for band in range(bands):
-            line = taken[rows_ref[band, slot]]
+        for band in range(0, bands, 2):
+            one, two = taken[picks[band, slot]], taken[picks[band + 1, slot]]
             for tap in range(taps):
                 at = (slot * taps + tap) * deep
-                patches[at : at + deep, band * width : (band + 1) * width] = line[
-                    :, tap * width : (tap + 1) * width
-                ]
+                patches[at : at + deep, band * width : (band + 2) * width] = jnp.where(
+                    left,
+                    one[:, tap * lons : (tap + 1) * lons],
+                    two[:, tap * lons : (tap + 1) * lons],
+                )
     raw = lax.dot_general(
         patches[...], weight_ref[...], (((0,), (0,)), ((), ())), preferred_element_type=F32
     )
-    factor = lax.rsqrt(jnp.mean(raw * raw, axis=-1, keepdims=True) + 1e-06)
-    out_ref[...] = (raw * factor).astype(BF16)
-
-
-def features_of(own, other, edge, row_index, weights):
-    rows, deep, lons = own.shape
+    out_ref[...] = normed(raw).astype(BF16)
+    for band in range(bands):
+        first_ref[band] = raw[band * width : band * width + 8]
+
+
+def local_features(picks, lines, above, below, weights):
+    _, deep, lons = lines.shape
     width = weights.shape[1]
-    bands = row_index.shape[0]
-    taps = weights.shape[0] // (row_index.shape[1] * deep)
+    bands = picks.shape[0]
+    count = lines.shape[0] + above.shape[0] + below.shape[0]
+    taps = weights.shape[0] // (picks.shape[1] * deep)
+    tokens = bands * lons // 2
     vmem = pl.BlockSpec(memory_space=pltpu.VMEM)
     return pl.pallas_call(
         conv_kernel,
-        out_shape=jax.ShapeDtypeStruct((bands * lons, width), BF16),
-        in_specs=[pl.BlockSpec(memory_space=pltpu.SMEM)] + [vmem] * 4,
-        out_specs=vmem,
+        out_shape=(
+            jax.ShapeDtypeStruct((tokens, width), BF16),
+            jax.ShapeDtypeStruct((bands, 8, width), F32),
+        ),
+        in_specs=[vmem] * 5,
+        out_specs=(vmem, vmem),
         scratch_shapes=[
-            pltpu.VMEM((rows + edge.shape[0], deep, taps * lons), BF16),
-            pltpu.VMEM((weights.shape[0], bands * lons), BF16),
+            pltpu.VMEM((count, deep, taps * lons), BF16),
+            pltpu.VMEM((weights.shape[0], tokens), BF16),
         ],
         compiler_params=pltpu.CompilerParams(vmem_limit_bytes=12 * 2**20),
+        cost_estimate=pl.CostEstimate(
+            flops=2 * weights.size * tokens, bytes_accessed=2 * weights.size, transcendentals=0
+        ),
         name="conv",
-    )(row_index, own, other, edge, weights)
+    )(picks, lines, above, below, weights)
+
+
+def west_kernel(west_ref, hits_ref, weight_ref, some_ref, first_ref, out_ref):
+    deep = west_ref.shape[0]
+    slots = hits_ref.shape[1] // 128
+    stride = weight_ref.shape[0] // slots
+    bands = first_ref.shape[0]
+    width = out_ref.shape[0] // bands
+    chosen = jnp.dot(west_ref[...], hits_ref[...], preferred_element_type=F32).astype(BF16)
+    columns = jnp.concatenate(
+        [chosen[:, slot * 128 : (slot + 1) * 128] for slot in range(slots)], axis=0
+    )
+    filters = jnp.concatenate(
+        [weight_ref[slot * stride : slot * stride + deep] for slot in range(slots)], axis=0
+    )
+    more = lax.dot_general(
+        columns, filters, (((0,), (0,)), ((), ())), preferred_element_type=F32
+    )
+    out_ref[...] = some_ref[...]
+    head = lax.broadcasted_iota(jnp.int32, (16, 1), 0) == 0
+    for band in range(bands):
+        fixed = normed(first_ref[band, 0:1] + more[band : band + 1])
+        rest = some_ref[band * width : band * width + 16].astype(F32)
+        out_ref[band * width : band * width + 16] = jnp.where(head, fixed, rest).astype(BF16)
+
+
+def west_added(west, hits, weights, some, first):
+    vmem = pl.BlockSpec(memory_space=pltpu.VMEM)
+    return pl.pallas_call(
+        west_kernel,
+        out_shape=jax.ShapeDtypeStruct(some.shape, BF16),
+        in_specs=[vmem] * 5,
+        out_specs=vmem,
+        compiler_params=pltpu.CompilerParams(vmem_limit_bytes=6 * 2**20),
+        name="west",
+    )(west, hits, weights, some, first)
 
 
 def select_kernel(where_ref, near_ref, own_ref, pair_ref, other_ref):
     slots, rows, _ = own_ref.shape
+    where = where_ref[...]
     for index in range(4 * slots):
-        start = pl.multiple_of(where_ref[index, 1], rows)
+        start = pl.multiple_of(where[index, 1], rows)
         picked = near_ref[pl.ds(start, rows)]
-        picked = jnp.where(where_ref[index, 0] != 0, picked, jnp.zeros_like(picked))
+        picked = jnp.where(where[index, 0] != 0, picked, jnp.zeros_like(picked))
         if index < 2 * slots:
             (own_ref if index < slots else pair_ref)[index % slots] = picked
         else:
@@ -300,7 +375,7 @@
     return pl.pallas_call(
         select_kernel,
         out_shape=(shape, shape, both),
-        in_specs=[pl.BlockSpec(memory_space=pltpu.SMEM), vmem],
+        in_specs=[vmem, vmem],
         out_specs=(vmem, vmem, vmem),
         compiler_params=pltpu.CompilerParams(vmem_limit_bytes=2**20 + 2 * near.size),
         name="select",
@@ -460,20 +535,22 @@
     lat, lon = lax.axis_index("lat"), lax.axis_index("lon")
     channels, rows, lons = state_field.shape
     lat_tile = support_rows.shape[0]
-    bands = lat_tile // 2
     lon_tile = lons // 2
     band_total = lat_tile * lats
     pair = lats // 2
 
     deep = -(-channels // 16) * 16
-    lower = (lon ^ lat) & 1
-    own, same, cross = rows_of(lower.astype(jnp.int32).reshape(1), state_field, 2, deep)
-    edge = vertical(jnp.concatenate([same, exchange(cross, 0, 1)], axis=0))
-    other = exchange(own, 0, 1)
-    weights = weights_of(conv_weight, deep)
-    row_index = 2 * jnp.arange(lat_tile, dtype=jnp.int32)[:, None] + support_rows + 2
-    row_index = lax.dynamic_slice_in_dim(row_index, lower * bands, bands, axis=0)
-    features = features_of(own, other, edge, row_index, weights)
+    odd = lat & 1
+    lines, out_far, out_chip = rows_of(odd.astype(jnp.int32).reshape(1), state_field, 2, deep)
+    far_rows = across(out_far)
+    chip_rows = exchange(out_chip, 1, 0)
+    above = jnp.where(odd != 0, chip_rows, far_rows)
+    below = jnp.where(odd != 0, far_rows, chip_rows)
+    west = exchange(last_columns(lines, above, below), 0, 1)
+    picks = 2 * jnp.arange(lat_tile, dtype=jnp.int32)[:, None] + support_rows + 2
+    weights, hits = weights_of(conv_weight, picks, deep)
+    some, first = local_features(picks, lines, above, below, weights)
+    features = west_added(west, hits, weights, some, first)
 
     bits = [1 << k for k in range(1, lats.bit_length() - 1) if 1 << k != pair]
     masks = [(0, 1)] + [(bit, 0) for bit in bits]
@@ -481,18 +558,15 @@
     order = [(i, j) for i in range(0, pair, 2) for j in range(2)]
     near = jnp.concatenate([blocks[key] for key in order], axis=0)
 
-    size = bands * lons
+    size = lat_tile * lon_tile
     slot_count = window_bands.shape[0] // lats
     sides = jnp.stack([lat, lat ^ pair, lat ^ 1, lat ^ pair ^ 1])
     wanted = window_bands[
         (sides[:, None] * slot_count + jnp.arange(slot_count)[None, :]).reshape(-1)
     ]
     owner = wanted // lat_tile
-    band = wanted % lat_tile
-    owner_lower = band // bands
-    turn = owner_lower ^ (owner & 1) ^ lon
     apart = owner ^ lat
-    place = ((apart & (pair - 2)) + turn) * size + band % bands * lons + turn * lon_tile
+    place = (apart & (pair - 2)) * size + wanted % lat_tile * lon_tile
     within = apart & (pair | 1) == 0
     where = jnp.stack([within.astype(jnp.int32), place.astype(jnp.int32)], axis=1)
     sel_own, sel_pair, sel_other = selected(where, near, lon_tile)
@@ -504,12 +578,12 @@
     got_own = exchange(sel_pair, pair, 0)
     held = (near, exchange(near, 1, 0))
 
-    step = jnp.arange(2 * len(order) * bands, dtype=jnp.int32)
-    masks = (step // bands) % len(order)
-    tile = lat ^ ((masks & ~1) | (step // (len(order) * bands)))
-    key_band = tile * lat_tile + ((tile ^ lon ^ masks) & 1) * bands + step % bands
+    step = jnp.arange(2 * len(order) * lat_tile, dtype=jnp.int32)
+    masks = (step // lat_tile) % len(order)
+    tile = lat ^ ((masks & ~1) | (step // (len(order) * lat_tile)))
+    key_band = tile * lat_tile + step % lat_tile
     area = LOG2E * log_area(key_band, band_total)
-    area = jnp.repeat(area, lons)[None, :]
+    area = jnp.repeat(area, lon_tile)[None, :]
     shared = (area, w_query, w_key, w_value, held)
     (send,) = attended(True, sel_pair, got_pair, *shared)
     received = exchange(send, pair, 0)

time: 44.8 us -> 42.5 us (0.949)
  waiting for transfers between devices: 10.3 us -> 8.35 us
  starting transfers between devices: 23.4 us -> 22.9 us
    ppermute x14, waiting for transfers between devices: 10.3 us -> 8.35 us  [exchange(): return lax.ppermute(x, AXES, pairs)]
    ppermute x14, starting transfers between devices: 22.8 us -> 22.2 us  [exchange(): return lax.ppermute(x, AXES, pairs)]
    pallas_call x3 -> x5, Pallas kernels: 2.35 us -> 2.16 us  [the longest x1 1.19 us: local_features(): pl.pallas_call(conv_kernel, out_shape=(jax.ShapeDtypeStruct((tokens, widt...]
  transfers between devices with their start and end apart: 15 -> 15, of which waited for: 8 -> 7; matrix products, arithmetic and copies ran while one was open for 3% -> 4% of each run, Pallas kernels for 9% -> 14%
where the time goes in v5:
time: 42.5 us; the launch traced here: 42.3 us
  starting transfers between devices  22.9 us (54%)
  waiting for transfers between devices  8.35 us (20%)
  Pallas kernels  7.68 us (18%)
  local copies, waits for them, and re-layouts  2.67 us (6%)
  other arithmetic  0.46 us (1%)
    ppermute x14, starting transfers between devices, exchange(): return lax.ppermute(x, AXES, pairs)  22.2 us
    ppermute x14, waiting for transfers between devices, exchange(): return lax.ppermute(x, AXES, pairs)  8.35 us
    pallas_call x2, Pallas kernels, attended(): pl.pallas_call(functools.partial(attend_kernel, len(held)), out_shape=out...  4.5 us
    unnamed x23, local copies, waits for them, and re-layouts  1.66 us
    pallas_call x1, Pallas kernels, local_features(): pl.pallas_call(conv_kernel, out_shape=(jax.ShapeDtypeStruct((tokens, widt...  1.19 us
    pallas_call x1, Pallas kernels, finished(): pl.pallas_call(finish_kernel, out_shape=jax.ShapeDtypeStruct(keep.shape,...  0.94 us
  transfers between devices with their start and end apart: 15, of which 7 were waited for; matrix products, arithmetic and copies ran while one was open for 4% of the time, Pallas kernels for 14%

profile of v5, /device:TPU:0, one launch (start us, length us, event | category | flops | bytes accessed | tf_op | source)
XLA Modules:
  0.0 42.3 jit_solution(13666061541964500385)
XLA Ops:
  0.0 1.0 %copy-done.2 = bf16[73,8,128]{2,1,0:T(8,128)(2,1)S(1)} copy-done((bf16[73,8,128]{2,1,0:T(8,128)(2,1)S(1)}, bf16[73,8,128]{2,1,0:T(8,128)(2,1)}, u32[]{:S(2)}) %copy-start.2) | copy-done | bytes 149528
  1.1 0.5 %collective-permute-start = (bf16[2,80,128]{2,1,0:T(8,128)(2,1)S(1)}, bf16[2,80,128]{2,1,0:T(8,128)(2,1)S(1)}, u32[]{:S(2)}, u32[]{:S(2)}) collective-permute-start(bf16[2,80,128]{2,1,0:T(8,128)(2,1)S(1)} %get-tuple-element.21), channel_id=1, source_target_pairs={{0,2},{1,3},{2,0},{3,1},{4,6},{5,7},{6,4},{7,5},{8,10},{9,11},{10,... | collective-permute-start | bytes 122888 | tf_op jit(solution)/shard_map/ppermute | solution.py:147
  1.6 0.7 %collective-permute-start.1 = (bf16[2,80,128]{2,1,0:T(8,128)(2,1)S(1)}, bf16[2,80,128]{2,1,0:T(8,128)(2,1)S(1)}, u32[]{:S(2)}, u32[]{:S(2)}) collective-permute-start(bf16[2,80,128]{2,1,0:T(8,128)(2,1)S(1)} %get-tuple-element.22), channel_id=1, source_target_pairs={{2,4},{4,2},{3,5},{5,3},{6,8},{8,6},{7,9},{9,7},{10,12},{12,10},{1... | collective-permute-start | bytes 122888 | tf_op jit(solution)/shard_map/ppermute | solution.py:156
  2.6 0.6 %gather_fusion = s32[4]{0:T(128)S(1)} fusion(s32[16]{0:T(128)S(1)} %copy-done, s32[1024]{0:T(1024)S(1)} %pad_clamp_fusion), kind=kCustom, calls=%fused_computation | custom fusion | bytes 48 | tf_op jit(solution)/shard_map/gather | solution.py:564
  3.3 0.6 %copy-done.7 = s32[4,5]{1,0:T(4,128)S(1)} copy-done((s32[4,5]{1,0:T(4,128)S(1)}, s32[4,5]{1,0:T(4,128)}, u32[]{:S(2)}) %copy-start.7) | copy-done | bytes 104
  4.2 2.6 %collective-permute-start.2 = (bf16[80,128]{1,0:T(8,128)(2,1)S(1)}, bf16[80,128]{1,0:T(8,128)(2,1)S(1)}, u32[]{:S(2)}, u32[]{:S(2)}) collective-permute-start(bf16[80,128]{1,0:T(8,128)(2,1)S(1)} %columns.1), channel_id=1, source_target_pairs={{0,1},{1,0},{2,3},{3,2},{4,5},{5,4},{6,7},{7,6},{8,9},{9,8},{10,11... | collective-permute-start | bytes 61448 | tf_op jit(solution)/shard_map/ppermute | solution.py:147
  7.0 1.2 %conv.1 = (bf16[256,256]{1,0:T(8,128)(2,1)S(1)}, f32[4,8,256]{2,1,0:T(8,128)S(1)}) custom-call(s32[4,5]{1,0:T(4,128)S(1)} %add_add_fusion.picks_ref, bf16[8,80,128]{2,1,0:T(8,128)(2,1)S(1)} %get-tuple-element.20.lines_ref, bf16[2,80,128]{2,1,0:T(8,128)(2,1)S(1)} %get-tuple-element.36.above_ref, bf16[2,80,128]{2,1,0:T(8,128)(2,1)S(1)} %get-tuple-element.35.below_ref, ...), custom_call_target="tpu_custom_call" | custom-call | flops 157286400 | bytes 614400 | tf_op jit(solution)/shard_map/conv/pallas_call | solution.py:301
  8.5 0.5 %west.1 = bf16[256,256]{1,0:T(8,128)(2,1)S(1)} custom-call(bf16[80,128]{1,0:T(8,128)(2,1)S(1)} %collective-permute-done.2.west_ref, bf16[128,640]{1,0:T(8,128)(2,1)S(1)} %get-tuple-element.23.hits_ref, bf16[1200,256]{1,0:T(8,128)(2,1)S(1)} %get-tuple-element.24.weight_ref, bf16[256,256]{1,0:T(8,128)(2,1)S(1)} %get-tuple-element.25.some_ref, ...), custom_call_target="tpu_custom_call" | custom-call | tf_op jit(solution)/shard_map/west/pallas_call | solution.py:347
  9.0 2.1 %collective-permute-start.3 = (bf16[256,256]{1,0:T(8,128)(2,1)S(1)}, bf16[256,256]{1,0:T(8,128)(2,1)S(1)}, u32[]{:S(2)}, u32[]{:S(2)}) collective-permute-start(bf16[256,256]{1,0:T(8,128)(2,1)S(1)} %west.1), channel_id=1, source_target_pairs={{0,1},{1,0},{2,3},{3,2},{4,5},{5,4},{6,7},{7,6},{8,9},{9,8},{10,11... | collective-permute-start | bytes 393224 | tf_op jit(solution)/shard_map/ppermute | solution.py:147
  11.1 4.4 %collective-permute-start.4 = (bf16[256,256]{1,0:T(8,128)(2,1)S(1)}, bf16[256,256]{1,0:T(8,128)(2,1)S(1)}, u32[]{:S(2)}, u32[]{:S(2)}) collective-permute-start(bf16[256,256]{1,0:T(8,128)(2,1)S(1)} %west.1), channel_id=1, source_target_pairs={{0,4},{1,5},{2,6},{3,7},{4,0},{5,1},{6,2},{7,3},{8,12},{9,13},{10,... | collective-permute-start | bytes 393224 | tf_op jit(solution)/shard_map/ppermute | solution.py:147
  15.5 1.6 %collective-permute-start.6 = (bf16[256,256]{1,0:T(8,128)(2,1)S(1)}, bf16[256,256]{1,0:T(8,128)(2,1)S(1)}, u32[]{:S(2)}, u32[]{:S(2)}) collective-permute-start(bf16[256,256]{1,0:T(8,128)(2,1)S(1)} %west.1), channel_id=1, source_target_pairs={{0,8},{1,9},{2,10},{3,11},{4,12},{5,13},{6,14},{7,15},{8,0},{9,1},... | collective-permute-start | bytes 393224 | tf_op jit(solution)/shard_map/ppermute | solution.py:147
  17.1 1.0 %collective-permute-start.9 = (bf16[256,256]{1,0:T(8,128)(2,1)S(1)}, bf16[256,256]{1,0:T(8,128)(2,1)S(1)}, u32[]{:S(2)}, u32[]{:S(2)}) collective-permute-start(bf16[256,256]{1,0:T(8,128)(2,1)S(1)} %west.1), channel_id=1, source_target_pairs={{0,13},{1,12},{2,15},{3,14},{4,9},{5,8},{6,11},{7,10},{8,5},{9,4},... | collective-permute-start | bytes 393224 | tf_op jit(solution)/shard_map/ppermute | solution.py:147
  18.1 1.5 %collective-permute-start.5 = (bf16[256,256]{1,0:T(8,128)(2,1)S(1)}, bf16[256,256]{1,0:T(8,128)(2,1)S(1)}, u32[]{:S(2)}, u32[]{:S(2)}) collective-permute-start(bf16[256,256]{1,0:T(8,128)(2,1)S(1)} %collective-permute-done.3), channel_id=1, source_target_pairs={{0,4},{1,5},{2,6},{3,7},{4,0},{5,1},{6,2},{7,3},{8,12},{9,13},{10,... | collective-permute-start | bytes 393224 | tf_op jit(solution)/shard_map/ppermute | solution.py:147
  19.7 2.3 %collective-permute-done.6 = bf16[256,256]{1,0:T(8,128)(2,1)S(1)} collective-permute-done((bf16[256,256]{1,0:T(8,128)(2,1)S(1)}, bf16[256,256]{1,0:T(8,128)(2,1)S(1)}, u32[]{:S(2)}, u32[]{:S(2)}) %collective-permute-start.6) | collective-permute-done | bytes 131104 | tf_op jit(solution)/shard_map/ppermute | solution.py:147
  22.1 2.0 %collective-permute-start.8 = (bf16[256,256]{1,0:T(8,128)(2,1)S(1)}, bf16[256,256]{1,0:T(8,128)(2,1)S(1)}, u32[]{:S(2)}, u32[]{:S(2)}) collective-permute-start(bf16[256,256]{1,0:T(8,128)(2,1)S(1)} %collective-permute-done.4), channel_id=1, source_target_pairs={{0,8},{1,9},{2,10},{3,11},{4,12},{5,13},{6,14},{7,15},{8,0},{9,1},... | collective-permute-start | bytes 393224 | tf_op jit(solution)/shard_map/ppermute | solution.py:147
  24.1 1.5 %collective-permute-done.5 = bf16[256,256]{1,0:T(8,128)(2,1)S(1)} collective-permute-done((bf16[256,256]{1,0:T(8,128)(2,1)S(1)}, bf16[256,256]{1,0:T(8,128)(2,1)S(1)}, u32[]{:S(2)}, u32[]{:S(2)}) %collective-permute-start.5) | collective-permute-done | bytes 131104 | tf_op jit(solution)/shard_map/ppermute | solution.py:147
  25.7 1.3 %collective-permute-done.7 = bf16[256,256]{1,0:T(8,128)(2,1)S(1)} collective-permute-done((bf16[256,256]{1,0:T(8,128)(2,1)S(1)}, bf16[256,256]{1,0:T(8,128)(2,1)S(1)}, u32[]{:S(2)}, u32[]{:S(2)}) %collective-permute-start.7) | collective-permute-done | bytes 131104 | tf_op jit(solution)/shard_map/ppermute | solution.py:147
  27.3 1.2 %collective-permute-done.10 = bf16[2,64,256]{2,1,0:T(8,128)(2,1)S(1)} collective-permute-done((bf16[2,64,256]{2,1,0:T(8,128)(2,1)S(1)}, bf16[2,64,256]{2,1,0:T(8,128)(2,1)S(1)}, u32[]{:S(2)}, u32[]{:S(2)}) %collective-permute-start.10) | collective-permute-done | bytes 65568 | tf_op jit(solution)/shard_map/ppermute | solution.py:147
  28.8 2.9 %collective-permute-start.13 = (bf16[1,64,256]{2,1,0:T(8,128)(2,1)S(1)}, bf16[1,64,256]{2,1,0:T(8,128)(2,1)S(1)}, u32[]{:S(2)}, u32[]{:S(2)}) collective-permute-start(bf16[1,64,256]{2,1,0:T(8,128)(2,1)S(1)} %get-tuple-element.30.sel_ref), channel_id=1, source_target_pairs={{0,16},{1,17},{2,18},{3,19},{4,20},{5,21},{6,22},{7,23},{8,24},{9,... | collective-permute-start | bytes 98312 | tf_op jit(solution)/shard_map/ppermute | solution.py:147
  32.0 1.6 %collective-permute-done.13.got_ref = bf16[1,64,256]{2,1,0:T(8,128)(2,1)S(1)} collective-permute-done((bf16[1,64,256]{2,1,0:T(8,128)(2,1)S(1)}, bf16[1,64,256]{2,1,0:T(8,128)(2,1)S(1)}, u32[]{:S(2)}, u32[]{:S(2)}) %collective-permute-start.13) | collective-permute-done | bytes 32800 | tf_op jit(solution)/shard_map/ppermute | solution.py:147
  33.7 2.2 %attend_sent.1 = bf16[1,64,384]{2,1,0:T(8,128)(2,1)S(1)} custom-call(bf16[1,64,256]{2,1,0:T(8,128)(2,1)S(1)} %get-tuple-element.31.sel_ref, bf16[1,64,256]{2,1,0:T(8,128)(2,1)S(1)} %collective-permute-done.13.got_ref, f32[1,4096]{1,0:T(1,128)S(1)} %broadcast_in_dim_reshape.3.area_ref, bf16[256,256]{1,0:T(8,128)(2,1)S(1)} %copy-done.4, ...), custom_call_target="tpu_custom_call" | custom-call | flops 1073741824 | bytes 2097152 | tf_op jit(solution)/shard_map/attend_sent/pallas_call | solution.py:468
  35.9 3.1 %collective-permute-start.14 = (bf16[1,64,384]{2,1,0:T(8,128)(2,1)S(1)}, bf16[1,64,384]{2,1,0:T(8,128)(2,1)S(1)}, u32[]{:S(2)}, u32[]{:S(2)}) collective-permute-start(bf16[1,64,384]{2,1,0:T(8,128)(2,1)S(1)} %attend_sent.1), channel_id=1, source_target_pairs={{0,16},{1,17},{2,18},{3,19},{4,20},{5,21},{6,22},{7,23},{8,24},{9,... | collective-permute-start | bytes 147464 | tf_op jit(solution)/shard_map/ppermute | solution.py:147
  39.1 2.2 %attend_kept.1 = (f32[1,64,256]{2,1,0:T(8,128)S(1)}, f32[1,64,128]{2,1,0:T(8,128)S(1)}) custom-call(bf16[1,64,256]{2,1,0:T(8,128)(2,1)S(1)} %get-tuple-element.30.sel_ref, bf16[1,64,256]{2,1,0:T(8,128)(2,1)S(1)} %collective-permute-done.11.got_ref, f32[1,4096]{1,0:T(1,128)S(1)} %broadcast_in_dim_reshape.3.area_ref, bf16[256,256]{1,0:T(8,128)(2,1)S(1)} %copy-done.4, ...), custom_call_target="tpu_custom_call" | custom-call | flops 1073741824 | bytes 2097152 | tf_op jit(solution)/shard_map/attend_kept/pallas_call | solution.py:468
  41.4 0.9 %finish.1 = bf16[1,64,256]{2,1,0:T(8,128)(2,1)} custom-call(f32[1,64,256]{2,1,0:T(8,128)S(1)} %get-tuple-element.33.keep_ref, f32[1,64,128]{2,1,0:T(8,128)S(1)} %get-tuple-element.34.lse_ref, bf16[1,64,384]{2,1,0:T(8,128)(2,1)S(1)} %collective-permute-done.14.got_ref, bf16[256,256]{1,0:T(8,128)(2,1)S(1)} %copy-done.3), custom_call_target="tpu_custom_call" | custom-call | tf_op jit(solution)/shard_map/finish/pallas_call | solution.py:507
  (55 shorter events, 2.5 us)
Async XLA Ops:
  0.0 2.6 %copy-start = (s32[16]{0:T(128)S(1)}, s32[16]{0:T(128)}, u32[]{:S(2)}) copy-start(s32[16]{0:T(128)} %param.10) | copy-start | bytes 196
  0.0 6.8 %copy-start.1 = (bf16[5,3,73,256]{3,2,1,0:T(8,128)(2,1)S(1)}, bf16[5,3,73,256]{3,2,1,0:T(8,128)(2,1)}, u32[]{:S(2)}) copy-start(bf16[5,3,73,256]{3,2,1,0:T(8,128)(2,1)} %weight_ref.1) | copy-start | bytes 1681924
  0.0 1.0 %copy-start.2 = (bf16[73,8,128]{2,1,0:T(8,128)(2,1)S(1)}, bf16[73,8,128]{2,1,0:T(8,128)(2,1)}, u32[]{:S(2)}) copy-start(bf16[73,8,128]{2,1,0:T(8,128)(2,1)} %own_ref.1) | copy-start | bytes 448516
  1.1 2.9 %collective-permute-start = (bf16[2,80,128]{2,1,0:T(8,128)(2,1)S(1)}, bf16[2,80,128]{2,1,0:T(8,128)(2,1)S(1)}, u32[]{:S(2)}, u32[]{:S(2)}) collective-permute-start(bf16[2,80,128]{2,1,0:T(8,128)(2,1)S(1)} %get-tuple-element.21), channel_id=1, source_target_pairs={{0,2},{1,3},{2,0},{3,1},{4,6},{5,7},{6,4},{7,5},{8,10},{9,11},{10,... | collective-permute-start | bytes 122888 | tf_op jit(solution)/shard_map/ppermute | solution.py:147
  1.6 2.4 %collective-permute-start.1 = (bf16[2,80,128]{2,1,0:T(8,128)(2,1)S(1)}, bf16[2,80,128]{2,1,0:T(8,128)(2,1)S(1)}, u32[]{:S(2)}, u32[]{:S(2)}) collective-permute-start(bf16[2,80,128]{2,1,0:T(8,128)(2,1)S(1)} %get-tuple-element.22), channel_id=1, source_target_pairs={{2,4},{4,2},{3,5},{5,3},{6,8},{8,6},{7,9},{9,7},{10,12},{12,10},{1... | collective-permute-start | bytes 122888 | tf_op jit(solution)/shard_map/ppermute | solution.py:156
  3.2 0.7 %copy-start.7 = (s32[4,5]{1,0:T(4,128)S(1)}, s32[4,5]{1,0:T(4,128)}, u32[]{:S(2)}) copy-start(s32[4,5]{1,0:T(4,128)} %param.9) | copy-start | bytes 244
  4.2 4.3 %collective-permute-start.2 = (bf16[80,128]{1,0:T(8,128)(2,1)S(1)}, bf16[80,128]{1,0:T(8,128)(2,1)S(1)}, u32[]{:S(2)}, u32[]{:S(2)}) collective-permute-start(bf16[80,128]{1,0:T(8,128)(2,1)S(1)} %columns.1), channel_id=1, source_target_pairs={{0,1},{1,0},{2,3},{3,2},{4,5},{5,4},{6,7},{7,6},{8,9},{9,8},{10,11... | collective-permute-start | bytes 61448 | tf_op jit(solution)/shard_map/ppermute | solution.py:147
  9.0 9.1 %collective-permute-start.3 = (bf16[256,256]{1,0:T(8,128)(2,1)S(1)}, bf16[256,256]{1,0:T(8,128)(2,1)S(1)}, u32[]{:S(2)}, u32[]{:S(2)}) collective-permute-start(bf16[256,256]{1,0:T(8,128)(2,1)S(1)} %west.1), channel_id=1, source_target_pairs={{0,1},{1,0},{2,3},{3,2},{4,5},{5,4},{6,7},{7,6},{8,9},{9,8},{10,11... | collective-permute-start | bytes 393224 | tf_op jit(solution)/shard_map/ppermute | solution.py:147
  11.1 11.0 %collective-permute-start.4 = (bf16[256,256]{1,0:T(8,128)(2,1)S(1)}, bf16[256,256]{1,0:T(8,128)(2,1)S(1)}, u32[]{:S(2)}, u32[]{:S(2)}) collective-permute-start(bf16[256,256]{1,0:T(8,128)(2,1)S(1)} %west.1), channel_id=1, source_target_pairs={{0,4},{1,5},{2,6},{3,7},{4,0},{5,1},{6,2},{7,3},{8,12},{9,13},{10,... | collective-permute-start | bytes 393224 | tf_op jit(solution)/shard_map/ppermute | solution.py:147
  15.5 6.4 %collective-permute-start.6 = (bf16[256,256]{1,0:T(8,128)(2,1)S(1)}, bf16[256,256]{1,0:T(8,128)(2,1)S(1)}, u32[]{:S(2)}, u32[]{:S(2)}) collective-permute-start(bf16[256,256]{1,0:T(8,128)(2,1)S(1)} %west.1), channel_id=1, source_target_pairs={{0,8},{1,9},{2,10},{3,11},{4,12},{5,13},{6,14},{7,15},{8,0},{9,1},... | collective-permute-start | bytes 393224 | tf_op jit(solution)/shard_map/ppermute | solution.py:147
  17.1 9.9 %collective-permute-start.9 = (bf16[256,256]{1,0:T(8,128)(2,1)S(1)}, bf16[256,256]{1,0:T(8,128)(2,1)S(1)}, u32[]{:S(2)}, u32[]{:S(2)}) collective-permute-start(bf16[256,256]{1,0:T(8,128)(2,1)S(1)} %west.1), channel_id=1, source_target_pairs={{0,13},{1,12},{2,15},{3,14},{4,9},{5,8},{6,11},{7,10},{8,5},{9,4},... | collective-permute-start | bytes 393224 | tf_op jit(solution)/shard_map/ppermute | solution.py:147
  18.1 7.5 %collective-permute-start.5 = (bf16[256,256]{1,0:T(8,128)(2,1)S(1)}, bf16[256,256]{1,0:T(8,128)(2,1)S(1)}, u32[]{:S(2)}, u32[]{:S(2)}) collective-permute-start(bf16[256,256]{1,0:T(8,128)(2,1)S(1)} %collective-permute-done.3), channel_id=1, source_target_pairs={{0,4},{1,5},{2,6},{3,7},{4,0},{5,1},{6,2},{7,3},{8,12},{9,13},{10,... | collective-permute-start | bytes 393224 | tf_op jit(solution)/shard_map/ppermute | solution.py:147
  22.0 5.0 %collective-permute-start.7 = (bf16[256,256]{1,0:T(8,128)(2,1)S(1)}, bf16[256,256]{1,0:T(8,128)(2,1)S(1)}, u32[]{:S(2)}, u32[]{:S(2)}) collective-permute-start(bf16[256,256]{1,0:T(8,128)(2,1)S(1)} %collective-permute-done.6), channel_id=1, source_target_pairs={{0,1},{1,0},{2,3},{3,2},{4,5},{5,4},{6,7},{7,6},{8,9},{9,8},{10,11... | collective-permute-start | bytes 393224 | tf_op jit(solution)/shard_map/ppermute | solution.py:147
  22.1 5.0 %collective-permute-start.8 = (bf16[256,256]{1,0:T(8,128)(2,1)S(1)}, bf16[256,256]{1,0:T(8,128)(2,1)S(1)}, u32[]{:S(2)}, u32[]{:S(2)}) collective-permute-start(bf16[256,256]{1,0:T(8,128)(2,1)S(1)} %collective-permute-done.4), channel_id=1, source_target_pairs={{0,8},{1,9},{2,10},{3,11},{4,12},{5,13},{6,14},{7,15},{8,0},{9,1},... | collective-permute-start | bytes 393224 | tf_op jit(solution)/shard_map/ppermute | solution.py:147
  27.1 6.5 %copy-start.6 = (bf16[256,256]{1,0:T(8,128)(2,1)S(1)}, bf16[256,256]{1,0:T(8,128)(2,1)}, u32[]{:S(2)}) copy-start(bf16[256,256]{1,0:T(8,128)(2,1)} %wv_ref.3) | copy-start | bytes 393220
  27.2 1.3 %collective-permute-start.10 = (bf16[2,64,256]{2,1,0:T(8,128)(2,1)S(1)}, bf16[2,64,256]{2,1,0:T(8,128)(2,1)S(1)}, u32[]{:S(2)}, u32[]{:S(2)}) collective-permute-start(bf16[2,64,256]{2,1,0:T(8,128)(2,1)S(1)} %get-tuple-element.28), channel_id=1, source_target_pairs={{0,2},{1,3},{2,0},{3,1},{4,6},{5,7},{6,4},{7,5},{8,10},{9,11},{10,... | collective-permute-start | bytes 196616 | tf_op jit(solution)/shard_map/ppermute | solution.py:147
  28.6 5.1 %copy-start.4 = (bf16[256,256]{1,0:T(8,128)(2,1)S(1)}, bf16[256,256]{1,0:T(8,128)(2,1)}, u32[]{:S(2)}) copy-start(bf16[256,256]{1,0:T(8,128)(2,1)} %wq_ref.3) | copy-start | bytes 393220
  28.6 5.1 %copy-start.5 = (bf16[256,256]{1,0:T(8,128)(2,1)S(1)}, bf16[256,256]{1,0:T(8,128)(2,1)}, u32[]{:S(2)}) copy-start(bf16[256,256]{1,0:T(8,128)(2,1)} %wk_ref.3) | copy-start | bytes 393220
  28.6 5.0 %collective-permute-start.12 = (bf16[2048,256]{1,0:T(8,128)(2,1)S(1)}, bf16[2048,256]{1,0:T(8,128)(2,1)S(1)}, u32[]{:S(2)}, u32[]{:S(2)}) collective-permute-start(bf16[2048,256]{1,0:T(8,128)(2,1)S(1)} %constant_dynamic-update-slice_fusion.near_ref.refs_0_), channel_id=1, source_target_pairs={{0,2},{1,3},{2,0},{3,1},{4,6},{5,7},{6,4},{7,5},{8,10},{9,11},{10,... | collective-permute-start | bytes 3145736 | tf_op jit(solution)/shard_map/ppermute | solution.py:147
  28.8 4.8 %collective-permute-start.13 = (bf16[1,64,256]{2,1,0:T(8,128)(2,1)S(1)}, bf16[1,64,256]{2,1,0:T(8,128)(2,1)S(1)}, u32[]{:S(2)}, u32[]{:S(2)}) collective-permute-start(bf16[1,64,256]{2,1,0:T(8,128)(2,1)S(1)} %get-tuple-element.30.sel_ref), channel_id=1, source_target_pairs={{0,16},{1,17},{2,18},{3,19},{4,20},{5,21},{6,22},{7,23},{8,24},{9,... | collective-permute-start | bytes 98312 | tf_op jit(solution)/shard_map/ppermute | solution.py:147
  32.0 7.1 %collective-permute-start.11 = (bf16[1,64,256]{2,1,0:T(8,128)(2,1)S(1)}, bf16[1,64,256]{2,1,0:T(8,128)(2,1)S(1)}, u32[]{:S(2)}, u32[]{:S(2)}) collective-permute-start(bf16[1,64,256]{2,1,0:T(8,128)(2,1)S(1)} %get-tuple-element.31.sel_ref), channel_id=1, source_target_pairs={{0,16},{1,17},{2,18},{3,19},{4,20},{5,21},{6,22},{7,23},{8,24},{9,... | collective-permute-start | bytes 98312 | tf_op jit(solution)/shard_map/ppermute | solution.py:147
  35.9 5.4 %copy-start.3 = (bf16[256,256]{1,0:T(8,128)(2,1)S(1)}, bf16[256,256]{1,0:T(8,128)(2,1)}, u32[]{:S(2)}) copy-start(bf16[256,256]{1,0:T(8,128)(2,1)} %wo_ref.1) | copy-start | bytes 393220
  35.9 5.4 %collective-permute-start.14 = (bf16[1,64,384]{2,1,0:T(8,128)(2,1)S(1)}, bf16[1,64,384]{2,1,0:T(8,128)(2,1)S(1)}, u32[]{:S(2)}, u32[]{:S(2)}) collective-permute-start(bf16[1,64,384]{2,1,0:T(8,128)(2,1)S(1)} %attend_sent.1), channel_id=1, source_target_pairs={{0,16},{1,17},{2,18},{3,19},{4,20},{5,21},{6,22},{7,23},{8,24},{9,... | collective-permute-start | bytes 147464 | tf_op jit(solution)/shard_map/ppermute | solution.py:147

commit v6 on v5

--- a/solution.py
+++ b/solution.py
@@ -445,12 +445,14 @@
         out = jnp.where(lane == head, value[head * count : (head + 1) * count], out)
         for order, piece in enumerate(split3(lse[head * count : (head + 1) * count])):
             stats = jnp.where(stat_lane == 3 * head + order, piece, stats)
-    out_ref[:, :, 0:width] = out.reshape(sel_ref.shape).astype(out_ref.dtype)
+    out_ref[:, 0:rows, :] = out.reshape(sel_ref.shape).astype(out_ref.dtype)
     stats = stats.reshape(slots, rows, 128)
     if rest:
         rest[0][...] = stats
     else:
-        out_ref[:, :, width:] = stats.astype(out_ref.dtype)
+        out_ref[:, rows:, :] = jnp.zeros((slots, 16, width), out_ref.dtype)
+        for slot in range(slots):
+            out_ref[slot, rows:, 0:rows] = stats[slot].T[0:16].astype(out_ref.dtype)
 
 
 def attended(sent, sel, got, area, w_query, w_key, w_value, held):
@@ -459,7 +461,7 @@
     count = slots * rows
     vmem = pl.BlockSpec(memory_space=pltpu.VMEM)
     if sent:
-        out_shape = (jax.ShapeDtypeStruct((slots, rows, width + 128), BF16),)
+        out_shape = (jax.ShapeDtypeStruct((slots, rows + 16, width), BF16),)
     else:
         out_shape = (
             jax.ShapeDtypeStruct((slots, rows, width), F32),
@@ -484,16 +486,22 @@
     slots, rows, width = keep_ref.shape
     count = slots * rows
     keep = keep_ref[...].reshape(count, width)
-    got = got_ref[:, :, 0:width].astype(F32).reshape(count, width)
+    got = got_ref[:, 0:rows, :].astype(F32).reshape(count, width)
     ours = lse_ref[...].reshape(count, 128).astype(BF16)
-    theirs = got_ref[:, :, width:].reshape(count, 128)
     piece = lax.broadcasted_iota(jnp.int32, (128, width), 0) // 3
     head = lax.broadcasted_iota(jnp.int32, (128, width), 1) // (width // H)
     spread = (piece == head).astype(F32).astype(BF16)
-    sums = jnp.dot(
-        jnp.concatenate([ours, theirs], axis=0), spread, preferred_element_type=F32
-    )
-    own, far = sums[:count], sums[count:]
+    own = jnp.dot(ours, spread, preferred_element_type=F32)
+    far = jnp.concatenate(
+        [
+            lax.dot_general(
+                got_ref[slot, rows:, 0:rows], spread[0:16], (((0,), (0,)), ((), ())),
+                preferred_element_type=F32,
+            )
+            for slot in range(slots)
+        ],
+        axis=0,
+    )
     top = jnp.maximum(own, far)
     own = jnp.exp2(own - top)
     far = jnp.exp2(far - top)
@@ -591,11 +599,18 @@
     return finished(keep, lse, received, w_out)
 
 
+def per_device(state_field, support_rows, *rest):
+    lats, lons = lax.axis_size("lat"), lax.axis_size("lon")
+    _, rows, columns = state_field.shape
+    paired = lons == 2 and lats >= 4 and lats & (lats - 1) == 0
+    tiled = columns == 128 and rows % 8 == 0 and support_rows.shape[0] % 2 == 0
+    plan = halves if paired and tiled else general
+    return plan(state_field, support_rows, *rest)
+
+
 def solution(mesh):
-    lats, lons = mesh.shape["lat"], mesh.shape["lon"]
-    paired = lons == 2 and lats >= 4 and lats & (lats - 1) == 0
     return jax.shard_map(
-        halves if paired else general,
+        per_device,
         mesh=mesh,
         in_specs=(P(None, "lat", "lon"), P("lat", None), P(), P(), P(), P(), P(), P()),
         out_specs=P("lat", "lon", None),

time: 42.5 us -> 42.5 us (level)
  no operation moved by 1% of the time
where the time goes in v6:
time: 42.5 us; the launch traced here: 42.3 us
  starting transfers between devices  22.9 us (54%)
  waiting for transfers between devices  8.35 us (20%)
  Pallas kernels  7.7 us (18%)
  local copies, waits for them, and re-layouts  2.67 us (6%)
  other arithmetic  0.46 us (1%)
    ppermute x14, starting transfers between devices, exchange(): return lax.ppermute(x, AXES, pairs)  22.2 us
    ppermute x14, waiting for transfers between devices, exchange(): return lax.ppermute(x, AXES, pairs)  8.35 us
    pallas_call x2, Pallas kernels, attended(): pl.pallas_call(functools.partial(attend_kernel, len(held)), out_shape=out...  4.51 us
    unnamed x23, local copies, waits for them, and re-layouts  1.66 us
    pallas_call x1, Pallas kernels, local_features(): pl.pallas_call(conv_kernel, out_shape=(jax.ShapeDtypeStruct((tokens, widt...  1.2 us
    pallas_call x1, Pallas kernels, finished(): pl.pallas_call(finish_kernel, out_shape=jax.ShapeDtypeStruct(keep.shape,...  0.95 us
  transfers between devices with their start and end apart: 15, of which 7 were waited for; matrix products, arithmetic and copies ran while one was open for 4% of the time, Pallas kernels for 14%

profile of v6, /device:TPU:0, one launch (start us, length us, event | category | flops | bytes accessed | tf_op | source)
XLA Modules:
  0.0 42.3 jit_solution(16139903979654615459)
XLA Ops:
  0.0 1.0 %copy-done.2 = bf16[73,8,128]{2,1,0:T(8,128)(2,1)S(1)} copy-done((bf16[73,8,128]{2,1,0:T(8,128)(2,1)S(1)}, bf16[73,8,128]{2,1,0:T(8,128)(2,1)}, u32[]{:S(2)}) %copy-start.2) | copy-done | bytes 149528
  1.1 0.5 %collective-permute-start = (bf16[2,80,128]{2,1,0:T(8,128)(2,1)S(1)}, bf16[2,80,128]{2,1,0:T(8,128)(2,1)S(1)}, u32[]{:S(2)}, u32[]{:S(2)}) collective-permute-start(bf16[2,80,128]{2,1,0:T(8,128)(2,1)S(1)} %get-tuple-element.21), channel_id=1, source_target_pairs={{0,2},{1,3},{2,0},{3,1},{4,6},{5,7},{6,4},{7,5},{8,10},{9,11},{10,... | collective-permute-start | bytes 122888 | tf_op jit(solution)/shard_map/ppermute | solution.py:147
  1.6 0.7 %collective-permute-start.1 = (bf16[2,80,128]{2,1,0:T(8,128)(2,1)S(1)}, bf16[2,80,128]{2,1,0:T(8,128)(2,1)S(1)}, u32[]{:S(2)}, u32[]{:S(2)}) collective-permute-start(bf16[2,80,128]{2,1,0:T(8,128)(2,1)S(1)} %get-tuple-element.22), channel_id=1, source_target_pairs={{2,4},{4,2},{3,5},{5,3},{6,8},{8,6},{7,9},{9,7},{10,12},{12,10},{1... | collective-permute-start | bytes 122888 | tf_op jit(solution)/shard_map/ppermute | solution.py:156
  2.6 0.6 %gather_fusion = s32[4]{0:T(128)S(1)} fusion(s32[16]{0:T(128)S(1)} %copy-done, s32[1024]{0:T(1024)S(1)} %pad_clamp_fusion), kind=kCustom, calls=%fused_computation | custom fusion | bytes 48 | tf_op jit(solution)/shard_map/gather | solution.py:572
  3.3 0.6 %copy-done.7 = s32[4,5]{1,0:T(4,128)S(1)} copy-done((s32[4,5]{1,0:T(4,128)S(1)}, s32[4,5]{1,0:T(4,128)}, u32[]{:S(2)}) %copy-start.7) | copy-done | bytes 104
  4.2 2.6 %collective-permute-start.2 = (bf16[80,128]{1,0:T(8,128)(2,1)S(1)}, bf16[80,128]{1,0:T(8,128)(2,1)S(1)}, u32[]{:S(2)}, u32[]{:S(2)}) collective-permute-start(bf16[80,128]{1,0:T(8,128)(2,1)S(1)} %columns.1), channel_id=1, source_target_pairs={{0,1},{1,0},{2,3},{3,2},{4,5},{5,4},{6,7},{7,6},{8,9},{9,8},{10,11... | collective-permute-start | bytes 61448 | tf_op jit(solution)/shard_map/ppermute | solution.py:147
  7.0 1.2 %conv.1 = (bf16[256,256]{1,0:T(8,128)(2,1)S(1)}, f32[4,8,256]{2,1,0:T(8,128)S(1)}) custom-call(s32[4,5]{1,0:T(4,128)S(1)} %add_add_fusion.picks_ref, bf16[8,80,128]{2,1,0:T(8,128)(2,1)S(1)} %get-tuple-element.20.lines_ref, bf16[2,80,128]{2,1,0:T(8,128)(2,1)S(1)} %get-tuple-element.36.above_ref, bf16[2,80,128]{2,1,0:T(8,128)(2,1)S(1)} %get-tuple-element.35.below_ref, ...), custom_call_target="tpu_custom_call" | custom-call | flops 157286400 | bytes 614400 | tf_op jit(solution)/shard_map/conv/pallas_call | solution.py:301
  8.5 0.5 %west.1 = bf16[256,256]{1,0:T(8,128)(2,1)S(1)} custom-call(bf16[80,128]{1,0:T(8,128)(2,1)S(1)} %collective-permute-done.2.west_ref, bf16[128,640]{1,0:T(8,128)(2,1)S(1)} %get-tuple-element.23.hits_ref, bf16[1200,256]{1,0:T(8,128)(2,1)S(1)} %get-tuple-element.24.weight_ref, bf16[256,256]{1,0:T(8,128)(2,1)S(1)} %get-tuple-element.25.some_ref, ...), custom_call_target="tpu_custom_call" | custom-call | tf_op jit(solution)/shard_map/west/pallas_call | solution.py:347
  9.0 2.1 %collective-permute-start.3 = (bf16[256,256]{1,0:T(8,128)(2,1)S(1)}, bf16[256,256]{1,0:T(8,128)(2,1)S(1)}, u32[]{:S(2)}, u32[]{:S(2)}) collective-permute-start(bf16[256,256]{1,0:T(8,128)(2,1)S(1)} %west.1), channel_id=1, source_target_pairs={{0,1},{1,0},{2,3},{3,2},{4,5},{5,4},{6,7},{7,6},{8,9},{9,8},{10,11... | collective-permute-start | bytes 393224 | tf_op jit(solution)/shard_map/ppermute | solution.py:147
  11.1 4.4 %collective-permute-start.4 = (bf16[256,256]{1,0:T(8,128)(2,1)S(1)}, bf16[256,256]{1,0:T(8,128)(2,1)S(1)}, u32[]{:S(2)}, u32[]{:S(2)}) collective-permute-start(bf16[256,256]{1,0:T(8,128)(2,1)S(1)} %west.1), channel_id=1, source_target_pairs={{0,4},{1,5},{2,6},{3,7},{4,0},{5,1},{6,2},{7,3},{8,12},{9,13},{10,... | collective-permute-start | bytes 393224 | tf_op jit(solution)/shard_map/ppermute | solution.py:147
  15.5 1.6 %collective-permute-start.6 = (bf16[256,256]{1,0:T(8,128)(2,1)S(1)}, bf16[256,256]{1,0:T(8,128)(2,1)S(1)}, u32[]{:S(2)}, u32[]{:S(2)}) collective-permute-start(bf16[256,256]{1,0:T(8,128)(2,1)S(1)} %west.1), channel_id=1, source_target_pairs={{0,8},{1,9},{2,10},{3,11},{4,12},{5,13},{6,14},{7,15},{8,0},{9,1},... | collective-permute-start | bytes 393224 | tf_op jit(solution)/shard_map/ppermute | solution.py:147
  17.1 1.0 %collective-permute-start.9 = (bf16[256,256]{1,0:T(8,128)(2,1)S(1)}, bf16[256,256]{1,0:T(8,128)(2,1)S(1)}, u32[]{:S(2)}, u32[]{:S(2)}) collective-permute-start(bf16[256,256]{1,0:T(8,128)(2,1)S(1)} %west.1), channel_id=1, source_target_pairs={{0,13},{1,12},{2,15},{3,14},{4,9},{5,8},{6,11},{7,10},{8,5},{9,4},... | collective-permute-start | bytes 393224 | tf_op jit(solution)/shard_map/ppermute | solution.py:147
  18.1 1.6 %collective-permute-start.5 = (bf16[256,256]{1,0:T(8,128)(2,1)S(1)}, bf16[256,256]{1,0:T(8,128)(2,1)S(1)}, u32[]{:S(2)}, u32[]{:S(2)}) collective-permute-start(bf16[256,256]{1,0:T(8,128)(2,1)S(1)} %collective-permute-done.3), channel_id=1, source_target_pairs={{0,4},{1,5},{2,6},{3,7},{4,0},{5,1},{6,2},{7,3},{8,12},{9,13},{10,... | collective-permute-start | bytes 393224 | tf_op jit(solution)/shard_map/ppermute | solution.py:147
  19.7 2.3 %collective-permute-done.6 = bf16[256,256]{1,0:T(8,128)(2,1)S(1)} collective-permute-done((bf16[256,256]{1,0:T(8,128)(2,1)S(1)}, bf16[256,256]{1,0:T(8,128)(2,1)S(1)}, u32[]{:S(2)}, u32[]{:S(2)}) %collective-permute-start.6) | collective-permute-done | bytes 131104 | tf_op jit(solution)/shard_map/ppermute | solution.py:147
  22.1 2.0 %collective-permute-start.8 = (bf16[256,256]{1,0:T(8,128)(2,1)S(1)}, bf16[256,256]{1,0:T(8,128)(2,1)S(1)}, u32[]{:S(2)}, u32[]{:S(2)}) collective-permute-start(bf16[256,256]{1,0:T(8,128)(2,1)S(1)} %collective-permute-done.4), channel_id=1, source_target_pairs={{0,8},{1,9},{2,10},{3,11},{4,12},{5,13},{6,14},{7,15},{8,0},{9,1},... | collective-permute-start | bytes 393224 | tf_op jit(solution)/shard_map/ppermute | solution.py:147
  24.1 1.6 %collective-permute-done.5 = bf16[256,256]{1,0:T(8,128)(2,1)S(1)} collective-permute-done((bf16[256,256]{1,0:T(8,128)(2,1)S(1)}, bf16[256,256]{1,0:T(8,128)(2,1)S(1)}, u32[]{:S(2)}, u32[]{:S(2)}) %collective-permute-start.5) | collective-permute-done | bytes 131104 | tf_op jit(solution)/shard_map/ppermute | solution.py:147
  25.7 1.3 %collective-permute-done.7 = bf16[256,256]{1,0:T(8,128)(2,1)S(1)} collective-permute-done((bf16[256,256]{1,0:T(8,128)(2,1)S(1)}, bf16[256,256]{1,0:T(8,128)(2,1)S(1)}, u32[]{:S(2)}, u32[]{:S(2)}) %collective-permute-start.7) | collective-permute-done | bytes 131104 | tf_op jit(solution)/shard_map/ppermute | solution.py:147
  27.3 1.2 %collective-permute-done.10 = bf16[2,64,256]{2,1,0:T(8,128)(2,1)S(1)} collective-permute-done((bf16[2,64,256]{2,1,0:T(8,128)(2,1)S(1)}, bf16[2,64,256]{2,1,0:T(8,128)(2,1)S(1)}, u32[]{:S(2)}, u32[]{:S(2)}) %collective-permute-start.10) | collective-permute-done | bytes 65568 | tf_op jit(solution)/shard_map/ppermute | solution.py:147
  28.8 2.9 %collective-permute-start.13 = (bf16[1,64,256]{2,1,0:T(8,128)(2,1)S(1)}, bf16[1,64,256]{2,1,0:T(8,128)(2,1)S(1)}, u32[]{:S(2)}, u32[]{:S(2)}) collective-permute-start(bf16[1,64,256]{2,1,0:T(8,128)(2,1)S(1)} %get-tuple-element.30.sel_ref), channel_id=1, source_target_pairs={{0,16},{1,17},{2,18},{3,19},{4,20},{5,21},{6,22},{7,23},{8,24},{9,... | collective-permute-start | bytes 98312 | tf_op jit(solution)/shard_map/ppermute | solution.py:147
  32.0 1.6 %collective-permute-done.13.got_ref = bf16[1,64,256]{2,1,0:T(8,128)(2,1)S(1)} collective-permute-done((bf16[1,64,256]{2,1,0:T(8,128)(2,1)S(1)}, bf16[1,64,256]{2,1,0:T(8,128)(2,1)S(1)}, u32[]{:S(2)}, u32[]{:S(2)}) %collective-permute-start.13) | collective-permute-done | bytes 32800 | tf_op jit(solution)/shard_map/ppermute | solution.py:147
  33.7 2.3 %attend_sent.1 = bf16[1,80,256]{2,1,0:T(8,128)(2,1)S(1)} custom-call(bf16[1,64,256]{2,1,0:T(8,128)(2,1)S(1)} %get-tuple-element.31.sel_ref, bf16[1,64,256]{2,1,0:T(8,128)(2,1)S(1)} %collective-permute-done.13.got_ref, f32[1,4096]{1,0:T(1,128)S(1)} %broadcast_in_dim_reshape.3.area_ref, bf16[256,256]{1,0:T(8,128)(2,1)S(1)} %copy-done.4, ...), custom_call_target="tpu_custom_call" | custom-call | flops 1073741824 | bytes 2097152 | tf_op jit(solution)/shard_map/attend_sent/pallas_call | solution.py:470
  35.9 3.1 %collective-permute-start.14 = (bf16[1,80,256]{2,1,0:T(8,128)(2,1)S(1)}, bf16[1,80,256]{2,1,0:T(8,128)(2,1)S(1)}, u32[]{:S(2)}, u32[]{:S(2)}) collective-permute-start(bf16[1,80,256]{2,1,0:T(8,128)(2,1)S(1)} %attend_sent.1), channel_id=1, source_target_pairs={{0,16},{1,17},{2,18},{3,19},{4,20},{5,21},{6,22},{7,23},{8,24},{9,... | collective-permute-start | bytes 122888 | tf_op jit(solution)/shard_map/ppermute | solution.py:147
  39.1 2.3 %attend_kept.1 = (f32[1,64,256]{2,1,0:T(8,128)S(1)}, f32[1,64,128]{2,1,0:T(8,128)S(1)}) custom-call(bf16[1,64,256]{2,1,0:T(8,128)(2,1)S(1)} %get-tuple-element.30.sel_ref, bf16[1,64,256]{2,1,0:T(8,128)(2,1)S(1)} %collective-permute-done.11.got_ref, f32[1,4096]{1,0:T(1,128)S(1)} %broadcast_in_dim_reshape.3.area_ref, bf16[256,256]{1,0:T(8,128)(2,1)S(1)} %copy-done.4, ...), custom_call_target="tpu_custom_call" | custom-call | flops 1073741824 | bytes 2097152 | tf_op jit(solution)/shard_map/attend_kept/pallas_call | solution.py:470
  41.4 0.9 %finish.1 = bf16[1,64,256]{2,1,0:T(8,128)(2,1)} custom-call(f32[1,64,256]{2,1,0:T(8,128)S(1)} %get-tuple-element.33.keep_ref, f32[1,64,128]{2,1,0:T(8,128)S(1)} %get-tuple-element.34.lse_ref, bf16[1,80,256]{2,1,0:T(8,128)(2,1)S(1)} %collective-permute-done.14.got_ref, bf16[256,256]{1,0:T(8,128)(2,1)S(1)} %copy-done.3), custom_call_target="tpu_custom_call" | custom-call | tf_op jit(solution)/shard_map/finish/pallas_call | solution.py:515
  (55 shorter events, 2.5 us)
Async XLA Ops:
  0.0 2.6 %copy-start = (s32[16]{0:T(128)S(1)}, s32[16]{0:T(128)}, u32[]{:S(2)}) copy-start(s32[16]{0:T(128)} %param.10) | copy-start | bytes 196
  0.0 6.8 %copy-start.1 = (bf16[5,3,73,256]{3,2,1,0:T(8,128)(2,1)S(1)}, bf16[5,3,73,256]{3,2,1,0:T(8,128)(2,1)}, u32[]{:S(2)}) copy-start(bf16[5,3,73,256]{3,2,1,0:T(8,128)(2,1)} %weight_ref.1) | copy-start | bytes 1681924
  0.0 1.0 %copy-start.2 = (bf16[73,8,128]{2,1,0:T(8,128)(2,1)S(1)}, bf16[73,8,128]{2,1,0:T(8,128)(2,1)}, u32[]{:S(2)}) copy-start(bf16[73,8,128]{2,1,0:T(8,128)(2,1)} %own_ref.1) | copy-start | bytes 448516
  1.1 2.9 %collective-permute-start = (bf16[2,80,128]{2,1,0:T(8,128)(2,1)S(1)}, bf16[2,80,128]{2,1,0:T(8,128)(2,1)S(1)}, u32[]{:S(2)}, u32[]{:S(2)}) collective-permute-start(bf16[2,80,128]{2,1,0:T(8,128)(2,1)S(1)} %get-tuple-element.21), channel_id=1, source_target_pairs={{0,2},{1,3},{2,0},{3,1},{4,6},{5,7},{6,4},{7,5},{8,10},{9,11},{10,... | collective-permute-start | bytes 122888 | tf_op jit(solution)/shard_map/ppermute | solution.py:147
  1.6 2.4 %collective-permute-start.1 = (bf16[2,80,128]{2,1,0:T(8,128)(2,1)S(1)}, bf16[2,80,128]{2,1,0:T(8,128)(2,1)S(1)}, u32[]{:S(2)}, u32[]{:S(2)}) collective-permute-start(bf16[2,80,128]{2,1,0:T(8,128)(2,1)S(1)} %get-tuple-element.22), channel_id=1, source_target_pairs={{2,4},{4,2},{3,5},{5,3},{6,8},{8,6},{7,9},{9,7},{10,12},{12,10},{1... | collective-permute-start | bytes 122888 | tf_op jit(solution)/shard_map/ppermute | solution.py:156
  3.2 0.7 %copy-start.7 = (s32[4,5]{1,0:T(4,128)S(1)}, s32[4,5]{1,0:T(4,128)}, u32[]{:S(2)}) copy-start(s32[4,5]{1,0:T(4,128)} %param.9) | copy-start | bytes 244
  4.2 4.3 %collective-permute-start.2 = (bf16[80,128]{1,0:T(8,128)(2,1)S(1)}, bf16[80,128]{1,0:T(8,128)(2,1)S(1)}, u32[]{:S(2)}, u32[]{:S(2)}) collective-permute-start(bf16[80,128]{1,0:T(8,128)(2,1)S(1)} %columns.1), channel_id=1, source_target_pairs={{0,1},{1,0},{2,3},{3,2},{4,5},{5,4},{6,7},{7,6},{8,9},{9,8},{10,11... | collective-permute-start | bytes 61448 | tf_op jit(solution)/shard_map/ppermute | solution.py:147
  9.0 9.1 %collective-permute-start.3 = (bf16[256,256]{1,0:T(8,128)(2,1)S(1)}, bf16[256,256]{1,0:T(8,128)(2,1)S(1)}, u32[]{:S(2)}, u32[]{:S(2)}) collective-permute-start(bf16[256,256]{1,0:T(8,128)(2,1)S(1)} %west.1), channel_id=1, source_target_pairs={{0,1},{1,0},{2,3},{3,2},{4,5},{5,4},{6,7},{7,6},{8,9},{9,8},{10,11... | collective-permute-start | bytes 393224 | tf_op jit(solution)/shard_map/ppermute | solution.py:147
  11.1 11.0 %collective-permute-start.4 = (bf16[256,256]{1,0:T(8,128)(2,1)S(1)}, bf16[256,256]{1,0:T(8,128)(2,1)S(1)}, u32[]{:S(2)}, u32[]{:S(2)}) collective-permute-start(bf16[256,256]{1,0:T(8,128)(2,1)S(1)} %west.1), channel_id=1, source_target_pairs={{0,4},{1,5},{2,6},{3,7},{4,0},{5,1},{6,2},{7,3},{8,12},{9,13},{10,... | collective-permute-start | bytes 393224 | tf_op jit(solution)/shard_map/ppermute | solution.py:147
  15.5 6.4 %collective-permute-start.6 = (bf16[256,256]{1,0:T(8,128)(2,1)S(1)}, bf16[256,256]{1,0:T(8,128)(2,1)S(1)}, u32[]{:S(2)}, u32[]{:S(2)}) collective-permute-start(bf16[256,256]{1,0:T(8,128)(2,1)S(1)} %west.1), channel_id=1, source_target_pairs={{0,8},{1,9},{2,10},{3,11},{4,12},{5,13},{6,14},{7,15},{8,0},{9,1},... | collective-permute-start | bytes 393224 | tf_op jit(solution)/shard_map/ppermute | solution.py:147
  17.1 10.0 %collective-permute-start.9 = (bf16[256,256]{1,0:T(8,128)(2,1)S(1)}, bf16[256,256]{1,0:T(8,128)(2,1)S(1)}, u32[]{:S(2)}, u32[]{:S(2)}) collective-permute-start(bf16[256,256]{1,0:T(8,128)(2,1)S(1)} %west.1), channel_id=1, source_target_pairs={{0,13},{1,12},{2,15},{3,14},{4,9},{5,8},{6,11},{7,10},{8,5},{9,4},... | collective-permute-start | bytes 393224 | tf_op jit(solution)/shard_map/ppermute | solution.py:147
  18.1 7.5 %collective-permute-start.5 = (bf16[256,256]{1,0:T(8,128)(2,1)S(1)}, bf16[256,256]{1,0:T(8,128)(2,1)S(1)}, u32[]{:S(2)}, u32[]{:S(2)}) collective-permute-start(bf16[256,256]{1,0:T(8,128)(2,1)S(1)} %collective-permute-done.3), channel_id=1, source_target_pairs={{0,4},{1,5},{2,6},{3,7},{4,0},{5,1},{6,2},{7,3},{8,12},{9,13},{10,... | collective-permute-start | bytes 393224 | tf_op jit(solution)/shard_map/ppermute | solution.py:147
  22.0 5.0 %collective-permute-start.7 = (bf16[256,256]{1,0:T(8,128)(2,1)S(1)}, bf16[256,256]{1,0:T(8,128)(2,1)S(1)}, u32[]{:S(2)}, u32[]{:S(2)}) collective-permute-start(bf16[256,256]{1,0:T(8,128)(2,1)S(1)} %collective-permute-done.6), channel_id=1, source_target_pairs={{0,1},{1,0},{2,3},{3,2},{4,5},{5,4},{6,7},{7,6},{8,9},{9,8},{10,11... | collective-permute-start | bytes 393224 | tf_op jit(solution)/shard_map/ppermute | solution.py:147
  22.1 5.0 %collective-permute-start.8 = (bf16[256,256]{1,0:T(8,128)(2,1)S(1)}, bf16[256,256]{1,0:T(8,128)(2,1)S(1)}, u32[]{:S(2)}, u32[]{:S(2)}) collective-permute-start(bf16[256,256]{1,0:T(8,128)(2,1)S(1)} %collective-permute-done.4), channel_id=1, source_target_pairs={{0,8},{1,9},{2,10},{3,11},{4,12},{5,13},{6,14},{7,15},{8,0},{9,1},... | collective-permute-start | bytes 393224 | tf_op jit(solution)/shard_map/ppermute | solution.py:147
  27.1 6.5 %copy-start.6 = (bf16[256,256]{1,0:T(8,128)(2,1)S(1)}, bf16[256,256]{1,0:T(8,128)(2,1)}, u32[]{:S(2)}) copy-start(bf16[256,256]{1,0:T(8,128)(2,1)} %wv_ref.3) | copy-start | bytes 393220
  27.3 1.3 %collective-permute-start.10 = (bf16[2,64,256]{2,1,0:T(8,128)(2,1)S(1)}, bf16[2,64,256]{2,1,0:T(8,128)(2,1)S(1)}, u32[]{:S(2)}, u32[]{:S(2)}) collective-permute-start(bf16[2,64,256]{2,1,0:T(8,128)(2,1)S(1)} %get-tuple-element.28), channel_id=1, source_target_pairs={{0,2},{1,3},{2,0},{3,1},{4,6},{5,7},{6,4},{7,5},{8,10},{9,11},{10,... | collective-permute-start | bytes 196616 | tf_op jit(solution)/shard_map/ppermute | solution.py:147
  28.6 5.1 %copy-start.4 = (bf16[256,256]{1,0:T(8,128)(2,1)S(1)}, bf16[256,256]{1,0:T(8,128)(2,1)}, u32[]{:S(2)}) copy-start(bf16[256,256]{1,0:T(8,128)(2,1)} %wq_ref.3) | copy-start | bytes 393220
  28.6 5.1 %copy-start.5 = (bf16[256,256]{1,0:T(8,128)(2,1)S(1)}, bf16[256,256]{1,0:T(8,128)(2,1)}, u32[]{:S(2)}) copy-start(bf16[256,256]{1,0:T(8,128)(2,1)} %wk_ref.3) | copy-start | bytes 393220
  28.6 5.0 %collective-permute-start.12 = (bf16[2048,256]{1,0:T(8,128)(2,1)S(1)}, bf16[2048,256]{1,0:T(8,128)(2,1)S(1)}, u32[]{:S(2)}, u32[]{:S(2)}) collective-permute-start(bf16[2048,256]{1,0:T(8,128)(2,1)S(1)} %constant_dynamic-update-slice_fusion.near_ref.refs_0_), channel_id=1, source_target_pairs={{0,2},{1,3},{2,0},{3,1},{4,6},{5,7},{6,4},{7,5},{8,10},{9,11},{10,... | collective-permute-start | bytes 3145736 | tf_op jit(solution)/shard_map/ppermute | solution.py:147
  28.8 4.8 %collective-permute-start.13 = (bf16[1,64,256]{2,1,0:T(8,128)(2,1)S(1)}, bf16[1,64,256]{2,1,0:T(8,128)(2,1)S(1)}, u32[]{:S(2)}, u32[]{:S(2)}) collective-permute-start(bf16[1,64,256]{2,1,0:T(8,128)(2,1)S(1)} %get-tuple-element.30.sel_ref), channel_id=1, source_target_pairs={{0,16},{1,17},{2,18},{3,19},{4,20},{5,21},{6,22},{7,23},{8,24},{9,... | collective-permute-start | bytes 98312 | tf_op jit(solution)/shard_map/ppermute | solution.py:147
  32.0 7.1 %collective-permute-start.11 = (bf16[1,64,256]{2,1,0:T(8,128)(2,1)S(1)}, bf16[1,64,256]{2,1,0:T(8,128)(2,1)S(1)}, u32[]{:S(2)}, u32[]{:S(2)}) collective-permute-start(bf16[1,64,256]{2,1,0:T(8,128)(2,1)S(1)} %get-tuple-element.31.sel_ref), channel_id=1, source_target_pairs={{0,16},{1,17},{2,18},{3,19},{4,20},{5,21},{6,22},{7,23},{8,24},{9,... | collective-permute-start | bytes 98312 | tf_op jit(solution)/shard_map/ppermute | solution.py:147
  35.9 5.4 %copy-start.3 = (bf16[256,256]{1,0:T(8,128)(2,1)S(1)}, bf16[256,256]{1,0:T(8,128)(2,1)}, u32[]{:S(2)}) copy-start(bf16[256,256]{1,0:T(8,128)(2,1)} %wo_ref.1) | copy-start | bytes 393220
  35.9 5.4 %collective-permute-start.14 = (bf16[1,80,256]{2,1,0:T(8,128)(2,1)S(1)}, bf16[1,80,256]{2,1,0:T(8,128)(2,1)S(1)}, u32[]{:S(2)}, u32[]{:S(2)}) collective-permute-start(bf16[1,80,256]{2,1,0:T(8,128)(2,1)S(1)} %attend_sent.1), channel_id=1, source_target_pairs={{0,16},{1,17},{2,18},{3,19},{4,20},{5,21},{6,22},{7,23},{8,24},{9,... | collective-permute-start | bytes 122888 | tf_op jit(solution)/shard_map/ppermute | solution.py:147

commit v7 on v6

--- a/solution.py
+++ b/solution.py
@@ -388,23 +388,45 @@
     return high, middle, x - high - middle
 
 
+def fold_kernel(wq_ref, wk_ref, out_ref):
+    width = wq_ref.shape[1]
+    head_size = width // H
+    lane = lax.broadcasted_iota(jnp.int32, (1, width), 1) // head_size
+    query = wq_ref[...]
+    for head in range(H):
+        part = jnp.where(lane == head, query, jnp.zeros_like(query))
+        both = lax.dot_general(
+            part, wk_ref[...], (((1,), (1,)), ((), ())), preferred_element_type=F32
+        )
+        both = both * (LOG2E / math.sqrt(head_size))
+        out_ref[:, head * width : (head + 1) * width] = both.astype(BF16)
+
+
+def folded(w_query, w_key):
+    vmem = pl.BlockSpec(memory_space=pltpu.VMEM)
+    return pl.pallas_call(
+        fold_kernel,
+        out_shape=jax.ShapeDtypeStruct((w_query.shape[0], H * w_key.shape[0]), BF16),
+        in_specs=[vmem, vmem],
+        out_specs=vmem,
+        compiler_params=pltpu.CompilerParams(vmem_limit_bytes=4 * 2**20),
+        name="fold",
+    )(w_query, w_key)
+
+
 def attend_kernel(
-    keys_count, sel_ref, got_ref, area_ref, wq_ref, wk_ref, wv_ref, *refs
+    keys_count, sel_ref, got_ref, area_ref, fold_ref, wv_ref, *refs
 ):
     held, (out_ref, *rest) = refs[:keys_count], refs[keys_count:]
     slots, rows, width = sel_ref.shape
     count = slots * rows
     head_size = width // H
     token = (sel_ref[...] + got_ref[...]).reshape(count, width)
-    query = jnp.dot(token, wq_ref[...], preferred_element_type=F32).astype(BF16)
     lane = lax.broadcasted_iota(jnp.int32, (1, width), 1) // head_size
-    spread = jnp.concatenate(
-        [jnp.where(lane == head, query, jnp.zeros_like(query)) for head in range(H)], axis=0
-    )
-    turned = lax.dot_general(
-        spread, wk_ref[...], (((1,), (1,)), ((), ())), preferred_element_type=F32
-    )
-    turned = (turned * (LOG2E / math.sqrt(head_size))).astype(BF16)
+    turned = jnp.dot(token, fold_ref[...], preferred_element_type=F32).astype(BF16)
+    turned = jnp.concatenate(
+        [turned[:, head * width : (head + 1) * width] for head in range(H)], axis=0
+    )
     parts, begin = [], 0
     for ref in held:
         for at in range(0, ref.shape[0], 512):
@@ -455,7 +477,7 @@
             out_ref[slot, rows:, 0:rows] = stats[slot].T[0:16].astype(out_ref.dtype)
 
 
-def attended(sent, sel, got, area, w_query, w_key, w_value, held):
+def attended(sent, sel, got, area, fold, w_value, held):
     slots, rows, width = sel.shape
     keys = sum(part.shape[0] for part in held)
     count = slots * rows
@@ -470,7 +492,7 @@
     return pl.pallas_call(
         functools.partial(attend_kernel, len(held)),
         out_shape=out_shape,
-        in_specs=[vmem] * (6 + len(held)),
+        in_specs=[vmem] * (5 + len(held)),
         out_specs=(vmem,) * len(out_shape),
         compiler_params=pltpu.CompilerParams(vmem_limit_bytes=20 * 2**20),
         cost_estimate=pl.CostEstimate(
@@ -479,7 +501,7 @@
             transcendentals=H * count * keys,
         ),
         name="attend_sent" if sent else "attend_kept",
-    )(sel, got, area, w_query, w_key, w_value, *held)
+    )(sel, got, area, fold, w_value, *held)
 
 
 def finish_kernel(keep_ref, lse_ref, got_ref, wo_ref, out_ref):
@@ -556,6 +578,7 @@
     below = jnp.where(odd != 0, far_rows, chip_rows)
     west = exchange(last_columns(lines, above, below), 0, 1)
     picks = 2 * jnp.arange(lat_tile, dtype=jnp.int32)[:, None] + support_rows + 2
+    fold = folded(w_query, w_key)
     weights, hits = weights_of(conv_weight, picks, deep)
     some, first = local_features(picks, lines, above, below, weights)
     features = west_added(west, hits, weights, some, first)
@@ -592,7 +615,7 @@
     key_band = tile * lat_tile + step % lat_tile
     area = LOG2E * log_area(key_band, band_total)
     area = jnp.repeat(area, lon_tile)[None, :]
-    shared = (area, w_query, w_key, w_value, held)
+    shared = (area, fold, w_value, held)
     (send,) = attended(True, sel_pair, got_pair, *shared)
     received = exchange(send, pair, 0)
     keep, lse = attended(False, sel_own, got_own, *shared)

time: 42.5 us -> 42.1 us (level)
  waiting for transfers between devices: 8.35 us -> 7.54 us
    ppermute x14, waiting for transfers between devices: 8.35 us -> 7.54 us  [exchange(): return lax.ppermute(x, AXES, pairs)]
  transfers between devices with their start and end apart: 15 -> 15, of which waited for: 7 -> 7; matrix products, arithmetic and copies ran while one was open for 4% -> 4% of each run, Pallas kernels for 14% -> 15%
where the time goes in v7:
time: 42.1 us; the launch traced here: 42 us
  starting transfers between devices  23.2 us (55%)
  Pallas kernels  7.86 us (19%)
  waiting for transfers between devices  7.54 us (18%)
  local copies, waits for them, and re-layouts  2.67 us (6%)
  other arithmetic  0.46 us (1%)
    ppermute x14, starting transfers between devices, exchange(): return lax.ppermute(x, AXES, pairs)  22.5 us
    ppermute x14, waiting for transfers between devices, exchange(): return lax.ppermute(x, AXES, pairs)  7.54 us
    pallas_call x2, Pallas kernels, attended(): pl.pallas_call(functools.partial(attend_kernel, len(held)), out_shape=out...  4.34 us
    unnamed x23, local copies, waits for them, and re-layouts  1.66 us
    pallas_call x1, Pallas kernels, local_features(): pl.pallas_call(conv_kernel, out_shape=(jax.ShapeDtypeStruct((tokens, widt...  1.19 us
    pallas_call x1, Pallas kernels, finished(): pl.pallas_call(finish_kernel, out_shape=jax.ShapeDtypeStruct(keep.shape,...  0.95 us
  transfers between devices with their start and end apart: 15, of which 7 were waited for; matrix products, arithmetic and copies ran while one was open for 4% of the time, Pallas kernels for 15%

profile of v7, /device:TPU:0, one launch (start us, length us, event | category | flops | bytes accessed | tf_op | source)
XLA Modules:
  0.0 42.0 jit_solution(13525956485939879828)
XLA Ops:
  0.0 1.0 %copy-done.2 = bf16[73,8,128]{2,1,0:T(8,128)(2,1)S(1)} copy-done((bf16[73,8,128]{2,1,0:T(8,128)(2,1)S(1)}, bf16[73,8,128]{2,1,0:T(8,128)(2,1)}, u32[]{:S(2)}) %copy-start.2) | copy-done | bytes 149528
  1.1 0.5 %collective-permute-start = (bf16[2,80,128]{2,1,0:T(8,128)(2,1)S(1)}, bf16[2,80,128]{2,1,0:T(8,128)(2,1)S(1)}, u32[]{:S(2)}, u32[]{:S(2)}) collective-permute-start(bf16[2,80,128]{2,1,0:T(8,128)(2,1)S(1)} %get-tuple-element.21), channel_id=1, source_target_pairs={{0,2},{1,3},{2,0},{3,1},{4,6},{5,7},{6,4},{7,5},{8,10},{9,11},{10,... | collective-permute-start | bytes 122888 | tf_op jit(solution)/shard_map/ppermute | solution.py:147
  1.6 0.7 %collective-permute-start.1 = (bf16[2,80,128]{2,1,0:T(8,128)(2,1)S(1)}, bf16[2,80,128]{2,1,0:T(8,128)(2,1)S(1)}, u32[]{:S(2)}, u32[]{:S(2)}) collective-permute-start(bf16[2,80,128]{2,1,0:T(8,128)(2,1)S(1)} %get-tuple-element.22), channel_id=1, source_target_pairs={{2,4},{4,2},{3,5},{5,3},{6,8},{8,6},{7,9},{9,7},{10,12},{12,10},{1... | collective-permute-start | bytes 122888 | tf_op jit(solution)/shard_map/ppermute | solution.py:156
  2.6 0.6 %gather_fusion = s32[4]{0:T(128)S(1)} fusion(s32[16]{0:T(128)S(1)} %copy-done, s32[1024]{0:T(1024)S(1)} %pad_clamp_fusion), kind=kCustom, calls=%fused_computation | custom fusion | bytes 48 | tf_op jit(solution)/shard_map/gather | solution.py:595
  3.3 0.6 %copy-done.7 = s32[4,5]{1,0:T(4,128)S(1)} copy-done((s32[4,5]{1,0:T(4,128)S(1)}, s32[4,5]{1,0:T(4,128)}, u32[]{:S(2)}) %copy-start.7) | copy-done | bytes 104
  4.2 2.6 %collective-permute-start.2 = (bf16[80,128]{1,0:T(8,128)(2,1)S(1)}, bf16[80,128]{1,0:T(8,128)(2,1)S(1)}, u32[]{:S(2)}, u32[]{:S(2)}) collective-permute-start(bf16[80,128]{1,0:T(8,128)(2,1)S(1)} %columns.1), channel_id=1, source_target_pairs={{0,1},{1,0},{2,3},{3,2},{4,5},{5,4},{6,7},{7,6},{8,9},{9,8},{10,11... | collective-permute-start | bytes 61448 | tf_op jit(solution)/shard_map/ppermute | solution.py:147
  7.0 1.2 %conv.1 = (bf16[256,256]{1,0:T(8,128)(2,1)S(1)}, f32[4,8,256]{2,1,0:T(8,128)S(1)}) custom-call(s32[4,5]{1,0:T(4,128)S(1)} %add_add_fusion.picks_ref, bf16[8,80,128]{2,1,0:T(8,128)(2,1)S(1)} %get-tuple-element.20.lines_ref, bf16[2,80,128]{2,1,0:T(8,128)(2,1)S(1)} %get-tuple-element.36.above_ref, bf16[2,80,128]{2,1,0:T(8,128)(2,1)S(1)} %get-tuple-element.35.below_ref, ...), custom_call_target="tpu_custom_call" | custom-call | flops 157286400 | bytes 614400 | tf_op jit(solution)/shard_map/conv/pallas_call | solution.py:301
  9.0 2.1 %collective-permute-start.3 = (bf16[256,256]{1,0:T(8,128)(2,1)S(1)}, bf16[256,256]{1,0:T(8,128)(2,1)S(1)}, u32[]{:S(2)}, u32[]{:S(2)}) collective-permute-start(bf16[256,256]{1,0:T(8,128)(2,1)S(1)} %west.1), channel_id=1, source_target_pairs={{0,1},{1,0},{2,3},{3,2},{4,5},{5,4},{6,7},{7,6},{8,9},{9,8},{10,11... | collective-permute-start | bytes 393224 | tf_op jit(solution)/shard_map/ppermute | solution.py:147
  11.1 4.4 %collective-permute-start.4 = (bf16[256,256]{1,0:T(8,128)(2,1)S(1)}, bf16[256,256]{1,0:T(8,128)(2,1)S(1)}, u32[]{:S(2)}, u32[]{:S(2)}) collective-permute-start(bf16[256,256]{1,0:T(8,128)(2,1)S(1)} %west.1), channel_id=1, source_target_pairs={{0,4},{1,5},{2,6},{3,7},{4,0},{5,1},{6,2},{7,3},{8,12},{9,13},{10,... | collective-permute-start | bytes 393224 | tf_op jit(solution)/shard_map/ppermute | solution.py:147
  15.5 1.6 %collective-permute-start.6 = (bf16[256,256]{1,0:T(8,128)(2,1)S(1)}, bf16[256,256]{1,0:T(8,128)(2,1)S(1)}, u32[]{:S(2)}, u32[]{:S(2)}) collective-permute-start(bf16[256,256]{1,0:T(8,128)(2,1)S(1)} %west.1), channel_id=1, source_target_pairs={{0,8},{1,9},{2,10},{3,11},{4,12},{5,13},{6,14},{7,15},{8,0},{9,1},... | collective-permute-start | bytes 393224 | tf_op jit(solution)/shard_map/ppermute | solution.py:147
  17.1 1.0 %collective-permute-start.9 = (bf16[256,256]{1,0:T(8,128)(2,1)S(1)}, bf16[256,256]{1,0:T(8,128)(2,1)S(1)}, u32[]{:S(2)}, u32[]{:S(2)}) collective-permute-start(bf16[256,256]{1,0:T(8,128)(2,1)S(1)} %west.1), channel_id=1, source_target_pairs={{0,13},{1,12},{2,15},{3,14},{4,9},{5,8},{6,11},{7,10},{8,5},{9,4},... | collective-permute-start | bytes 393224 | tf_op jit(solution)/shard_map/ppermute | solution.py:147
  18.1 1.6 %collective-permute-start.5 = (bf16[256,256]{1,0:T(8,128)(2,1)S(1)}, bf16[256,256]{1,0:T(8,128)(2,1)S(1)}, u32[]{:S(2)}, u32[]{:S(2)}) collective-permute-start(bf16[256,256]{1,0:T(8,128)(2,1)S(1)} %collective-permute-done.3), channel_id=1, source_target_pairs={{0,4},{1,5},{2,6},{3,7},{4,0},{5,1},{6,2},{7,3},{8,12},{9,13},{10,... | collective-permute-start | bytes 393224 | tf_op jit(solution)/shard_map/ppermute | solution.py:147
  19.7 2.3 %collective-permute-done.6 = bf16[256,256]{1,0:T(8,128)(2,1)S(1)} collective-permute-done((bf16[256,256]{1,0:T(8,128)(2,1)S(1)}, bf16[256,256]{1,0:T(8,128)(2,1)S(1)}, u32[]{:S(2)}, u32[]{:S(2)}) %collective-permute-start.6) | collective-permute-done | bytes 131104 | tf_op jit(solution)/shard_map/ppermute | solution.py:147
  22.1 2.0 %collective-permute-start.8 = (bf16[256,256]{1,0:T(8,128)(2,1)S(1)}, bf16[256,256]{1,0:T(8,128)(2,1)S(1)}, u32[]{:S(2)}, u32[]{:S(2)}) collective-permute-start(bf16[256,256]{1,0:T(8,128)(2,1)S(1)} %collective-permute-done.4), channel_id=1, source_target_pairs={{0,8},{1,9},{2,10},{3,11},{4,12},{5,13},{6,14},{7,15},{8,0},{9,1},... | collective-permute-start | bytes 393224 | tf_op jit(solution)/shard_map/ppermute | solution.py:147
  24.1 1.6 %collective-permute-done.5 = bf16[256,256]{1,0:T(8,128)(2,1)S(1)} collective-permute-done((bf16[256,256]{1,0:T(8,128)(2,1)S(1)}, bf16[256,256]{1,0:T(8,128)(2,1)S(1)}, u32[]{:S(2)}, u32[]{:S(2)}) %collective-permute-start.5) | collective-permute-done | bytes 131104 | tf_op jit(solution)/shard_map/ppermute | solution.py:147
  25.7 1.3 %collective-permute-done.7 = bf16[256,256]{1,0:T(8,128)(2,1)S(1)} collective-permute-done((bf16[256,256]{1,0:T(8,128)(2,1)S(1)}, bf16[256,256]{1,0:T(8,128)(2,1)S(1)}, u32[]{:S(2)}, u32[]{:S(2)}) %collective-permute-start.7) | collective-permute-done | bytes 131104 | tf_op jit(solution)/shard_map/ppermute | solution.py:147
  27.3 1.2 %collective-permute-done.10 = bf16[2,64,256]{2,1,0:T(8,128)(2,1)S(1)} collective-permute-done((bf16[2,64,256]{2,1,0:T(8,128)(2,1)S(1)}, bf16[2,64,256]{2,1,0:T(8,128)(2,1)S(1)}, u32[]{:S(2)}, u32[]{:S(2)}) %collective-permute-start.10) | collective-permute-done | bytes 65568 | tf_op jit(solution)/shard_map/ppermute | solution.py:147
  28.8 2.9 %collective-permute-start.13 = (bf16[1,64,256]{2,1,0:T(8,128)(2,1)S(1)}, bf16[1,64,256]{2,1,0:T(8,128)(2,1)S(1)}, u32[]{:S(2)}, u32[]{:S(2)}) collective-permute-start(bf16[1,64,256]{2,1,0:T(8,128)(2,1)S(1)} %get-tuple-element.30.sel_ref), channel_id=1, source_target_pairs={{0,16},{1,17},{2,18},{3,19},{4,20},{5,21},{6,22},{7,23},{8,24},{9,... | collective-permute-start | bytes 98312 | tf_op jit(solution)/shard_map/ppermute | solution.py:147
  32.3 0.5 %collective-permute-start.11 = (bf16[1,64,256]{2,1,0:T(8,128)(2,1)S(1)}, bf16[1,64,256]{2,1,0:T(8,128)(2,1)S(1)}, u32[]{:S(2)}, u32[]{:S(2)}) collective-permute-start(bf16[1,64,256]{2,1,0:T(8,128)(2,1)S(1)} %get-tuple-element.31.sel_ref), channel_id=1, source_target_pairs={{0,16},{1,17},{2,18},{3,19},{4,20},{5,21},{6,22},{7,23},{8,24},{9,... | collective-permute-start | bytes 98312 | tf_op jit(solution)/shard_map/ppermute | solution.py:147
  32.8 0.8 %collective-permute-done.13.got_ref = bf16[1,64,256]{2,1,0:T(8,128)(2,1)S(1)} collective-permute-done((bf16[1,64,256]{2,1,0:T(8,128)(2,1)S(1)}, bf16[1,64,256]{2,1,0:T(8,128)(2,1)S(1)}, u32[]{:S(2)}, u32[]{:S(2)}) %collective-permute-start.13) | collective-permute-done | bytes 32800 | tf_op jit(solution)/shard_map/ppermute | solution.py:147
  33.6 2.2 %attend_sent.1 = bf16[1,80,256]{2,1,0:T(8,128)(2,1)S(1)} custom-call(bf16[1,64,256]{2,1,0:T(8,128)(2,1)S(1)} %get-tuple-element.31.sel_ref, bf16[1,64,256]{2,1,0:T(8,128)(2,1)S(1)} %collective-permute-done.13.got_ref, f32[1,4096]{1,0:T(1,128)S(1)} %broadcast_in_dim_reshape.3.area_ref, bf16[256,1024]{1,0:T(8,128)(2,1)S(1)} %fold.1.fold_ref, ...), custom_call_target="tpu_custom_call" | custom-call | flops 1073741824 | bytes 2097152 | tf_op jit(solution)/shard_map/attend_sent/pallas_call | solution.py:492
  35.8 3.0 %collective-permute-start.14 = (bf16[1,80,256]{2,1,0:T(8,128)(2,1)S(1)}, bf16[1,80,256]{2,1,0:T(8,128)(2,1)S(1)}, u32[]{:S(2)}, u32[]{:S(2)}) collective-permute-start(bf16[1,80,256]{2,1,0:T(8,128)(2,1)S(1)} %attend_sent.1), channel_id=1, source_target_pairs={{0,16},{1,17},{2,18},{3,19},{4,20},{5,21},{6,22},{7,23},{8,24},{9,... | collective-permute-start | bytes 122888 | tf_op jit(solution)/shard_map/ppermute | solution.py:147
  38.8 2.2 %attend_kept.1 = (f32[1,64,256]{2,1,0:T(8,128)S(1)}, f32[1,64,128]{2,1,0:T(8,128)S(1)}) custom-call(bf16[1,64,256]{2,1,0:T(8,128)(2,1)S(1)} %get-tuple-element.30.sel_ref, bf16[1,64,256]{2,1,0:T(8,128)(2,1)S(1)} %collective-permute-done.11.got_ref, f32[1,4096]{1,0:T(1,128)S(1)} %broadcast_in_dim_reshape.3.area_ref, bf16[256,1024]{1,0:T(8,128)(2,1)S(1)} %fold.1.fold_ref, ...), custom_call_target="tpu_custom_call" | custom-call | flops 1073741824 | bytes 2097152 | tf_op jit(solution)/shard_map/attend_kept/pallas_call | solution.py:492
  41.0 0.9 %finish.1 = bf16[1,64,256]{2,1,0:T(8,128)(2,1)} custom-call(f32[1,64,256]{2,1,0:T(8,128)S(1)} %get-tuple-element.33.keep_ref, f32[1,64,128]{2,1,0:T(8,128)S(1)} %get-tuple-element.34.lse_ref, bf16[1,80,256]{2,1,0:T(8,128)(2,1)S(1)} %collective-permute-done.14.got_ref, bf16[256,256]{1,0:T(8,128)(2,1)S(1)} %copy-done.3), custom_call_target="tpu_custom_call" | custom-call | tf_op jit(solution)/shard_map/finish/pallas_call | solution.py:537
  (56 shorter events, 3.2 us)
Async XLA Ops:
  0.0 2.6 %copy-start = (s32[16]{0:T(128)S(1)}, s32[16]{0:T(128)}, u32[]{:S(2)}) copy-start(s32[16]{0:T(128)} %param.10) | copy-start | bytes 196
  0.0 6.8 %copy-start.1 = (bf16[5,3,73,256]{3,2,1,0:T(8,128)(2,1)S(1)}, bf16[5,3,73,256]{3,2,1,0:T(8,128)(2,1)}, u32[]{:S(2)}) copy-start(bf16[5,3,73,256]{3,2,1,0:T(8,128)(2,1)} %weight_ref.1) | copy-start | bytes 1681924
  0.0 1.0 %copy-start.2 = (bf16[73,8,128]{2,1,0:T(8,128)(2,1)S(1)}, bf16[73,8,128]{2,1,0:T(8,128)(2,1)}, u32[]{:S(2)}) copy-start(bf16[73,8,128]{2,1,0:T(8,128)(2,1)} %own_ref.1) | copy-start | bytes 448516
  1.1 2.9 %collective-permute-start = (bf16[2,80,128]{2,1,0:T(8,128)(2,1)S(1)}, bf16[2,80,128]{2,1,0:T(8,128)(2,1)S(1)}, u32[]{:S(2)}, u32[]{:S(2)}) collective-permute-start(bf16[2,80,128]{2,1,0:T(8,128)(2,1)S(1)} %get-tuple-element.21), channel_id=1, source_target_pairs={{0,2},{1,3},{2,0},{3,1},{4,6},{5,7},{6,4},{7,5},{8,10},{9,11},{10,... | collective-permute-start | bytes 122888 | tf_op jit(solution)/shard_map/ppermute | solution.py:147
  1.6 2.4 %collective-permute-start.1 = (bf16[2,80,128]{2,1,0:T(8,128)(2,1)S(1)}, bf16[2,80,128]{2,1,0:T(8,128)(2,1)S(1)}, u32[]{:S(2)}, u32[]{:S(2)}) collective-permute-start(bf16[2,80,128]{2,1,0:T(8,128)(2,1)S(1)} %get-tuple-element.22), channel_id=1, source_target_pairs={{2,4},{4,2},{3,5},{5,3},{6,8},{8,6},{7,9},{9,7},{10,12},{12,10},{1... | collective-permute-start | bytes 122888 | tf_op jit(solution)/shard_map/ppermute | solution.py:156
  3.2 0.7 %copy-start.7 = (s32[4,5]{1,0:T(4,128)S(1)}, s32[4,5]{1,0:T(4,128)}, u32[]{:S(2)}) copy-start(s32[4,5]{1,0:T(4,128)} %param.9) | copy-start | bytes 244
  4.2 4.3 %collective-permute-start.2 = (bf16[80,128]{1,0:T(8,128)(2,1)S(1)}, bf16[80,128]{1,0:T(8,128)(2,1)S(1)}, u32[]{:S(2)}, u32[]{:S(2)}) collective-permute-start(bf16[80,128]{1,0:T(8,128)(2,1)S(1)} %columns.1), channel_id=1, source_target_pairs={{0,1},{1,0},{2,3},{3,2},{4,5},{5,4},{6,7},{7,6},{8,9},{9,8},{10,11... | collective-permute-start | bytes 61448 | tf_op jit(solution)/shard_map/ppermute | solution.py:147
  9.0 9.1 %collective-permute-start.3 = (bf16[256,256]{1,0:T(8,128)(2,1)S(1)}, bf16[256,256]{1,0:T(8,128)(2,1)S(1)}, u32[]{:S(2)}, u32[]{:S(2)}) collective-permute-start(bf16[256,256]{1,0:T(8,128)(2,1)S(1)} %west.1), channel_id=1, source_target_pairs={{0,1},{1,0},{2,3},{3,2},{4,5},{5,4},{6,7},{7,6},{8,9},{9,8},{10,11... | collective-permute-start | bytes 393224 | tf_op jit(solution)/shard_map/ppermute | solution.py:147
  11.1 11.0 %collective-permute-start.4 = (bf16[256,256]{1,0:T(8,128)(2,1)S(1)}, bf16[256,256]{1,0:T(8,128)(2,1)S(1)}, u32[]{:S(2)}, u32[]{:S(2)}) collective-permute-start(bf16[256,256]{1,0:T(8,128)(2,1)S(1)} %west.1), channel_id=1, source_target_pairs={{0,4},{1,5},{2,6},{3,7},{4,0},{5,1},{6,2},{7,3},{8,12},{9,13},{10,... | collective-permute-start | bytes 393224 | tf_op jit(solution)/shard_map/ppermute | solution.py:147
  15.5 6.4 %collective-permute-start.6 = (bf16[256,256]{1,0:T(8,128)(2,1)S(1)}, bf16[256,256]{1,0:T(8,128)(2,1)S(1)}, u32[]{:S(2)}, u32[]{:S(2)}) collective-permute-start(bf16[256,256]{1,0:T(8,128)(2,1)S(1)} %west.1), channel_id=1, source_target_pairs={{0,8},{1,9},{2,10},{3,11},{4,12},{5,13},{6,14},{7,15},{8,0},{9,1},... | collective-permute-start | bytes 393224 | tf_op jit(solution)/shard_map/ppermute | solution.py:147
  17.1 10.0 %collective-permute-start.9 = (bf16[256,256]{1,0:T(8,128)(2,1)S(1)}, bf16[256,256]{1,0:T(8,128)(2,1)S(1)}, u32[]{:S(2)}, u32[]{:S(2)}) collective-permute-start(bf16[256,256]{1,0:T(8,128)(2,1)S(1)} %west.1), channel_id=1, source_target_pairs={{0,13},{1,12},{2,15},{3,14},{4,9},{5,8},{6,11},{7,10},{8,5},{9,4},... | collective-permute-start | bytes 393224 | tf_op jit(solution)/shard_map/ppermute | solution.py:147
  18.1 7.5 %collective-permute-start.5 = (bf16[256,256]{1,0:T(8,128)(2,1)S(1)}, bf16[256,256]{1,0:T(8,128)(2,1)S(1)}, u32[]{:S(2)}, u32[]{:S(2)}) collective-permute-start(bf16[256,256]{1,0:T(8,128)(2,1)S(1)} %collective-permute-done.3), channel_id=1, source_target_pairs={{0,4},{1,5},{2,6},{3,7},{4,0},{5,1},{6,2},{7,3},{8,12},{9,13},{10,... | collective-permute-start | bytes 393224 | tf_op jit(solution)/shard_map/ppermute | solution.py:147
  22.0 5.0 %collective-permute-start.7 = (bf16[256,256]{1,0:T(8,128)(2,1)S(1)}, bf16[256,256]{1,0:T(8,128)(2,1)S(1)}, u32[]{:S(2)}, u32[]{:S(2)}) collective-permute-start(bf16[256,256]{1,0:T(8,128)(2,1)S(1)} %collective-permute-done.6), channel_id=1, source_target_pairs={{0,1},{1,0},{2,3},{3,2},{4,5},{5,4},{6,7},{7,6},{8,9},{9,8},{10,11... | collective-permute-start | bytes 393224 | tf_op jit(solution)/shard_map/ppermute | solution.py:147
  22.1 5.0 %collective-permute-start.8 = (bf16[256,256]{1,0:T(8,128)(2,1)S(1)}, bf16[256,256]{1,0:T(8,128)(2,1)S(1)}, u32[]{:S(2)}, u32[]{:S(2)}) collective-permute-start(bf16[256,256]{1,0:T(8,128)(2,1)S(1)} %collective-permute-done.4), channel_id=1, source_target_pairs={{0,8},{1,9},{2,10},{3,11},{4,12},{5,13},{6,14},{7,15},{8,0},{9,1},... | collective-permute-start | bytes 393224 | tf_op jit(solution)/shard_map/ppermute | solution.py:147
  27.2 1.3 %collective-permute-start.10 = (bf16[2,64,256]{2,1,0:T(8,128)(2,1)S(1)}, bf16[2,64,256]{2,1,0:T(8,128)(2,1)S(1)}, u32[]{:S(2)}, u32[]{:S(2)}) collective-permute-start(bf16[2,64,256]{2,1,0:T(8,128)(2,1)S(1)} %get-tuple-element.28), channel_id=1, source_target_pairs={{0,2},{1,3},{2,0},{3,1},{4,6},{5,7},{6,4},{7,5},{8,10},{9,11},{10,... | collective-permute-start | bytes 196616 | tf_op jit(solution)/shard_map/ppermute | solution.py:147
  28.6 3.4 %copy-start.4 = (bf16[256,256]{1,0:T(8,128)(2,1)S(1)}, bf16[256,256]{1,0:T(8,128)(2,1)}, u32[]{:S(2)}) copy-start(bf16[256,256]{1,0:T(8,128)(2,1)} %wq_ref.1) | copy-start | bytes 393220
  28.6 3.4 %copy-start.5 = (bf16[256,256]{1,0:T(8,128)(2,1)S(1)}, bf16[256,256]{1,0:T(8,128)(2,1)}, u32[]{:S(2)}) copy-start(bf16[256,256]{1,0:T(8,128)(2,1)} %wk_ref.1) | copy-start | bytes 393220
  28.6 5.0 %collective-permute-start.12 = (bf16[2048,256]{1,0:T(8,128)(2,1)S(1)}, bf16[2048,256]{1,0:T(8,128)(2,1)S(1)}, u32[]{:S(2)}, u32[]{:S(2)}) collective-permute-start(bf16[2048,256]{1,0:T(8,128)(2,1)S(1)} %constant_dynamic-update-slice_fusion.near_ref.refs_0_), channel_id=1, source_target_pairs={{0,2},{1,3},{2,0},{3,1},{4,6},{5,7},{6,4},{7,5},{8,10},{9,11},{10,... | collective-permute-start | bytes 3145736 | tf_op jit(solution)/shard_map/ppermute | solution.py:147
  28.8 4.8 %collective-permute-start.13 = (bf16[1,64,256]{2,1,0:T(8,128)(2,1)S(1)}, bf16[1,64,256]{2,1,0:T(8,128)(2,1)S(1)}, u32[]{:S(2)}, u32[]{:S(2)}) collective-permute-start(bf16[1,64,256]{2,1,0:T(8,128)(2,1)S(1)} %get-tuple-element.30.sel_ref), channel_id=1, source_target_pairs={{0,16},{1,17},{2,18},{3,19},{4,20},{5,21},{6,22},{7,23},{8,24},{9,... | collective-permute-start | bytes 98312 | tf_op jit(solution)/shard_map/ppermute | solution.py:147
  32.0 1.7 %copy-start.6 = (bf16[256,256]{1,0:T(8,128)(2,1)S(1)}, bf16[256,256]{1,0:T(8,128)(2,1)}, u32[]{:S(2)}) copy-start(bf16[256,256]{1,0:T(8,128)(2,1)} %wv_ref.3) | copy-start | bytes 393220
  32.3 6.5 %collective-permute-start.11 = (bf16[1,64,256]{2,1,0:T(8,128)(2,1)S(1)}, bf16[1,64,256]{2,1,0:T(8,128)(2,1)S(1)}, u32[]{:S(2)}, u32[]{:S(2)}) collective-permute-start(bf16[1,64,256]{2,1,0:T(8,128)(2,1)S(1)} %get-tuple-element.31.sel_ref), channel_id=1, source_target_pairs={{0,16},{1,17},{2,18},{3,19},{4,20},{5,21},{6,22},{7,23},{8,24},{9,... | collective-permute-start | bytes 98312 | tf_op jit(solution)/shard_map/ppermute | solution.py:147
  35.8 5.2 %copy-start.3 = (bf16[256,256]{1,0:T(8,128)(2,1)S(1)}, bf16[256,256]{1,0:T(8,128)(2,1)}, u32[]{:S(2)}) copy-start(bf16[256,256]{1,0:T(8,128)(2,1)} %wo_ref.1) | copy-start | bytes 393220
  35.8 5.2 %collective-permute-start.14 = (bf16[1,80,256]{2,1,0:T(8,128)(2,1)S(1)}, bf16[1,80,256]{2,1,0:T(8,128)(2,1)S(1)}, u32[]{:S(2)}, u32[]{:S(2)}) collective-permute-start(bf16[1,80,256]{2,1,0:T(8,128)(2,1)S(1)} %attend_sent.1), channel_id=1, source_target_pairs={{0,16},{1,17},{2,18},{3,19},{4,20},{5,21},{6,22},{7,23},{8,24},{9,... | collective-permute-start | bytes 122888 | tf_op jit(solution)/shard_map/ppermute | solution.py:147

commit v8 on v6

--- a/solution.py
+++ b/solution.py
@@ -482,7 +482,7 @@
     )(sel, got, area, w_query, w_key, w_value, *held)
 
 
-def finish_kernel(keep_ref, lse_ref, got_ref, wo_ref, out_ref):
+def finish_kernel(keep_ref, lse_ref, got_ref, out_ref):
     slots, rows, width = keep_ref.shape
     count = slots * rows
     keep = keep_ref[...].reshape(count, width)
@@ -506,20 +506,21 @@
     own = jnp.exp2(own - top)
     far = jnp.exp2(far - top)
     mixed = ((keep * own + got * far) / (own + far)).astype(BF16)
-    result = jnp.dot(mixed, wo_ref[...], preferred_element_type=F32).astype(BF16)
-    out_ref[...] = result.reshape(out_ref.shape)
+    out_ref[...] = mixed.reshape(out_ref.shape)
 
 
 def finished(keep, lse, got, w_out):
     vmem = pl.BlockSpec(memory_space=pltpu.VMEM)
-    return pl.pallas_call(
+    mixed = pl.pallas_call(
         finish_kernel,
         out_shape=jax.ShapeDtypeStruct(keep.shape, BF16),
-        in_specs=[vmem] * 4,
+        in_specs=[vmem] * 3,
         out_specs=vmem,
         compiler_params=pltpu.CompilerParams(vmem_limit_bytes=4 * 2**20),
         name="finish",
-    )(keep, lse, got, w_out)
+    )(keep, lse, got)
+    result = jnp.dot(mixed.reshape(-1, keep.shape[2]), w_out, preferred_element_type=F32)
+    return result.astype(BF16).reshape(keep.shape)
 
 
 def gathered(block, masks):

time: 42.5 us -> 42.2 us (level)
  Pallas kernels: 7.7 us -> 6.63 us
  matrix products: 0 us -> 0.77 us
  starting transfers between devices: 22.9 us -> 22.2 us
  local copies, waits for them, and re-layouts: 2.67 us -> 3.33 us
    dot_general x0 -> x1, matrix products: none -> 0.77 us  [finished(): jnp.dot(mixed.reshape(-1, keep.shape[2]), w_out, preferred_element_type=F32)]
    pallas_call x1, Pallas kernels: 0.95 us -> 0.21 us  [finished(): pl.pallas_call(finish_kernel, out_shape=jax.ShapeDtypeStruct(keep.shape,...]
    gather x2, local copies, waits for them, and re-layouts: 0.73 us -> 1.39 us  [halves(): window_bands[(sides[:, None] * slot_count + jnp.arange(slot_count)[None,...]
    ppermute x14, starting transfers between devices: 22.2 us -> 21.6 us  [exchange(): return lax.ppermute(x, AXES, pairs)]
    unnamed x23 -> x21, local copies, waits for them, and re-layouts: 1.66 us -> 1.66 us
  transfers between devices with their start and end apart: 15 -> 15, of which waited for: 7 -> 7; matrix products, arithmetic and copies ran while one was open for 4% -> 5% of each run, Pallas kernels for 14% -> 13%
where the time goes in v8:
time: 42.2 us; the launch traced here: 42 us
  starting transfers between devices  22.2 us (53%)
  waiting for transfers between devices  8.35 us (20%)
  Pallas kernels  6.63 us (16%)
  local copies, waits for them, and re-layouts  3.33 us (8%)
  matrix products  0.77 us (2%)
  other arithmetic  0.46 us (1%)
    ppermute x14, starting transfers between devices, exchange(): return lax.ppermute(x, AXES, pairs)  21.6 us
    ppermute x14, waiting for transfers between devices, exchange(): return lax.ppermute(x, AXES, pairs)  8.35 us
    pallas_call x2, Pallas kernels, attended(): pl.pallas_call(functools.partial(attend_kernel, len(held)), out_shape=out...  4.18 us
    unnamed x21, local copies, waits for them, and re-layouts  1.66 us
    gather x2, local copies, waits for them, and re-layouts, halves(): window_bands[(sides[:, None] * slot_count + jnp.arange(slot_count)[None,...  1.39 us
    pallas_call x1, Pallas kernels, local_features(): pl.pallas_call(conv_kernel, out_shape=(jax.ShapeDtypeStruct((tokens, widt...  1.19 us
  transfers between devices with their start and end apart: 15, of which 7 were waited for; matrix products, arithmetic and copies ran while one was open for 5% of the time, Pallas kernels for 13%

profile of v8, /device:TPU:0, one launch (start us, length us, event | category | flops | bytes accessed | tf_op | source)
XLA Modules:
  0.0 42.0 jit_solution(3650531438101604963)
XLA Ops:
  0.0 1.0 %copy-done.2 = bf16[73,8,128]{2,1,0:T(8,128)(2,1)S(1)} copy-done((bf16[73,8,128]{2,1,0:T(8,128)(2,1)S(1)}, bf16[73,8,128]{2,1,0:T(8,128)(2,1)}, u32[]{:S(2)}) %copy-start.2) | copy-done | bytes 149528
  1.1 0.5 %collective-permute-start = (bf16[2,80,128]{2,1,0:T(8,128)(2,1)S(1)}, bf16[2,80,128]{2,1,0:T(8,128)(2,1)S(1)}, u32[]{:S(2)}, u32[]{:S(2)}) collective-permute-start(bf16[2,80,128]{2,1,0:T(8,128)(2,1)S(1)} %get-tuple-element.21), channel_id=1, source_target_pairs={{0,2},{1,3},{2,0},{3,1},{4,6},{5,7},{6,4},{7,5},{8,10},{9,11},{10,... | collective-permute-start | bytes 122888 | tf_op jit(solution)/shard_map/ppermute | solution.py:147
  1.6 0.7 %collective-permute-start.1 = (bf16[2,80,128]{2,1,0:T(8,128)(2,1)S(1)}, bf16[2,80,128]{2,1,0:T(8,128)(2,1)S(1)}, u32[]{:S(2)}, u32[]{:S(2)}) collective-permute-start(bf16[2,80,128]{2,1,0:T(8,128)(2,1)S(1)} %get-tuple-element.22), channel_id=1, source_target_pairs={{2,4},{4,2},{3,5},{5,3},{6,8},{8,6},{7,9},{9,7},{10,12},{12,10},{1... | collective-permute-start | bytes 122888 | tf_op jit(solution)/shard_map/ppermute | solution.py:156
  2.6 1.3 %gather_fusion = s32[4]{0:T(128)S(1)} fusion(s32[16]{0:T(128)} %param.10, s32[1024]{0:T(1024)S(1)} %pad_clamp_fusion), kind=kCustom, calls=%fused_computation | custom fusion | bytes 48 | tf_op jit(solution)/shard_map/gather | solution.py:573
  4.0 0.6 %copy-done.6 = s32[4,5]{1,0:T(4,128)S(1)} copy-done((s32[4,5]{1,0:T(4,128)S(1)}, s32[4,5]{1,0:T(4,128)}, u32[]{:S(2)}) %copy-start.6) | copy-done | bytes 104
  4.8 2.6 %collective-permute-start.2 = (bf16[80,128]{1,0:T(8,128)(2,1)S(1)}, bf16[80,128]{1,0:T(8,128)(2,1)S(1)}, u32[]{:S(2)}, u32[]{:S(2)}) collective-permute-start(bf16[80,128]{1,0:T(8,128)(2,1)S(1)} %columns.1), channel_id=1, source_target_pairs={{0,1},{1,0},{2,3},{3,2},{4,5},{5,4},{6,7},{7,6},{8,9},{9,8},{10,11... | collective-permute-start | bytes 61448 | tf_op jit(solution)/shard_map/ppermute | solution.py:147
  7.7 1.2 %conv.1 = (bf16[256,256]{1,0:T(8,128)(2,1)S(1)}, f32[4,8,256]{2,1,0:T(8,128)S(1)}) custom-call(s32[4,5]{1,0:T(4,128)S(1)} %add_add_fusion.picks_ref, bf16[8,80,128]{2,1,0:T(8,128)(2,1)S(1)} %get-tuple-element.20.lines_ref, bf16[2,80,128]{2,1,0:T(8,128)(2,1)S(1)} %get-tuple-element.36.above_ref, bf16[2,80,128]{2,1,0:T(8,128)(2,1)S(1)} %get-tuple-element.35.below_ref, ...), custom_call_target="tpu_custom_call" | custom-call | flops 157286400 | bytes 614400 | tf_op jit(solution)/shard_map/conv/pallas_call | solution.py:301
  9.2 0.5 %west.1 = bf16[256,256]{1,0:T(8,128)(2,1)S(1)} custom-call(bf16[80,128]{1,0:T(8,128)(2,1)S(1)} %collective-permute-done.2.west_ref, bf16[128,640]{1,0:T(8,128)(2,1)S(1)} %get-tuple-element.23.hits_ref, bf16[1200,256]{1,0:T(8,128)(2,1)S(1)} %get-tuple-element.24.weight_ref, bf16[256,256]{1,0:T(8,128)(2,1)S(1)} %get-tuple-element.25.some_ref, ...), custom_call_target="tpu_custom_call" | custom-call | tf_op jit(solution)/shard_map/west/pallas_call | solution.py:347
  9.6 2.1 %collective-permute-start.3 = (bf16[256,256]{1,0:T(8,128)(2,1)S(1)}, bf16[256,256]{1,0:T(8,128)(2,1)S(1)}, u32[]{:S(2)}, u32[]{:S(2)}) collective-permute-start(bf16[256,256]{1,0:T(8,128)(2,1)S(1)} %west.1), channel_id=1, source_target_pairs={{0,1},{1,0},{2,3},{3,2},{4,5},{5,4},{6,7},{7,6},{8,9},{9,8},{10,11... | collective-permute-start | bytes 393224 | tf_op jit(solution)/shard_map/ppermute | solution.py:147
  11.8 3.8 %collective-permute-start.4 = (bf16[256,256]{1,0:T(8,128)(2,1)S(1)}, bf16[256,256]{1,0:T(8,128)(2,1)S(1)}, u32[]{:S(2)}, u32[]{:S(2)}) collective-permute-start(bf16[256,256]{1,0:T(8,128)(2,1)S(1)} %west.1), channel_id=1, source_target_pairs={{0,4},{1,5},{2,6},{3,7},{4,0},{5,1},{6,2},{7,3},{8,12},{9,13},{10,... | collective-permute-start | bytes 393224 | tf_op jit(solution)/shard_map/ppermute | solution.py:147
  15.6 1.6 %collective-permute-start.6 = (bf16[256,256]{1,0:T(8,128)(2,1)S(1)}, bf16[256,256]{1,0:T(8,128)(2,1)S(1)}, u32[]{:S(2)}, u32[]{:S(2)}) collective-permute-start(bf16[256,256]{1,0:T(8,128)(2,1)S(1)} %west.1), channel_id=1, source_target_pairs={{0,8},{1,9},{2,10},{3,11},{4,12},{5,13},{6,14},{7,15},{8,0},{9,1},... | collective-permute-start | bytes 393224 | tf_op jit(solution)/shard_map/ppermute | solution.py:147
  17.1 1.0 %collective-permute-start.9 = (bf16[256,256]{1,0:T(8,128)(2,1)S(1)}, bf16[256,256]{1,0:T(8,128)(2,1)S(1)}, u32[]{:S(2)}, u32[]{:S(2)}) collective-permute-start(bf16[256,256]{1,0:T(8,128)(2,1)S(1)} %west.1), channel_id=1, source_target_pairs={{0,13},{1,12},{2,15},{3,14},{4,9},{5,8},{6,11},{7,10},{8,5},{9,4},... | collective-permute-start | bytes 393224 | tf_op jit(solution)/shard_map/ppermute | solution.py:147
  18.1 1.6 %collective-permute-start.5 = (bf16[256,256]{1,0:T(8,128)(2,1)S(1)}, bf16[256,256]{1,0:T(8,128)(2,1)S(1)}, u32[]{:S(2)}, u32[]{:S(2)}) collective-permute-start(bf16[256,256]{1,0:T(8,128)(2,1)S(1)} %collective-permute-done.3), channel_id=1, source_target_pairs={{0,4},{1,5},{2,6},{3,7},{4,0},{5,1},{6,2},{7,3},{8,12},{9,13},{10,... | collective-permute-start | bytes 393224 | tf_op jit(solution)/shard_map/ppermute | solution.py:147
  19.7 2.3 %collective-permute-done.6 = bf16[256,256]{1,0:T(8,128)(2,1)S(1)} collective-permute-done((bf16[256,256]{1,0:T(8,128)(2,1)S(1)}, bf16[256,256]{1,0:T(8,128)(2,1)S(1)}, u32[]{:S(2)}, u32[]{:S(2)}) %collective-permute-start.6) | collective-permute-done | bytes 131104 | tf_op jit(solution)/shard_map/ppermute | solution.py:147
  22.1 2.0 %collective-permute-start.8 = (bf16[256,256]{1,0:T(8,128)(2,1)S(1)}, bf16[256,256]{1,0:T(8,128)(2,1)S(1)}, u32[]{:S(2)}, u32[]{:S(2)}) collective-permute-start(bf16[256,256]{1,0:T(8,128)(2,1)S(1)} %collective-permute-done.4), channel_id=1, source_target_pairs={{0,8},{1,9},{2,10},{3,11},{4,12},{5,13},{6,14},{7,15},{8,0},{9,1},... | collective-permute-start | bytes 393224 | tf_op jit(solution)/shard_map/ppermute | solution.py:147
  24.1 1.6 %collective-permute-done.5 = bf16[256,256]{1,0:T(8,128)(2,1)S(1)} collective-permute-done((bf16[256,256]{1,0:T(8,128)(2,1)S(1)}, bf16[256,256]{1,0:T(8,128)(2,1)S(1)}, u32[]{:S(2)}, u32[]{:S(2)}) %collective-permute-start.5) | collective-permute-done | bytes 131104 | tf_op jit(solution)/shard_map/ppermute | solution.py:147
  25.7 1.3 %collective-permute-done.7 = bf16[256,256]{1,0:T(8,128)(2,1)S(1)} collective-permute-done((bf16[256,256]{1,0:T(8,128)(2,1)S(1)}, bf16[256,256]{1,0:T(8,128)(2,1)S(1)}, u32[]{:S(2)}, u32[]{:S(2)}) %collective-permute-start.7) | collective-permute-done | bytes 131104 | tf_op jit(solution)/shard_map/ppermute | solution.py:147
  27.3 1.2 %collective-permute-done.10 = bf16[2,64,256]{2,1,0:T(8,128)(2,1)S(1)} collective-permute-done((bf16[2,64,256]{2,1,0:T(8,128)(2,1)S(1)}, bf16[2,64,256]{2,1,0:T(8,128)(2,1)S(1)}, u32[]{:S(2)}, u32[]{:S(2)}) %collective-permute-start.10) | collective-permute-done | bytes 65568 | tf_op jit(solution)/shard_map/ppermute | solution.py:147
  28.8 2.9 %collective-permute-start.13 = (bf16[1,64,256]{2,1,0:T(8,128)(2,1)S(1)}, bf16[1,64,256]{2,1,0:T(8,128)(2,1)S(1)}, u32[]{:S(2)}, u32[]{:S(2)}) collective-permute-start(bf16[1,64,256]{2,1,0:T(8,128)(2,1)S(1)} %get-tuple-element.30.sel_ref), channel_id=1, source_target_pairs={{0,16},{1,17},{2,18},{3,19},{4,20},{5,21},{6,22},{7,23},{8,24},{9,... | collective-permute-start | bytes 98312 | tf_op jit(solution)/shard_map/ppermute | solution.py:147
  32.1 1.6 %collective-permute-done.13.got_ref = bf16[1,64,256]{2,1,0:T(8,128)(2,1)S(1)} collective-permute-done((bf16[1,64,256]{2,1,0:T(8,128)(2,1)S(1)}, bf16[1,64,256]{2,1,0:T(8,128)(2,1)S(1)}, u32[]{:S(2)}, u32[]{:S(2)}) %collective-permute-start.13) | collective-permute-done | bytes 32800 | tf_op jit(solution)/shard_map/ppermute | solution.py:147
  33.7 2.1 %attend_sent.1 = bf16[1,80,256]{2,1,0:T(8,128)(2,1)S(1)} custom-call(bf16[1,64,256]{2,1,0:T(8,128)(2,1)S(1)} %get-tuple-element.31.sel_ref, bf16[1,64,256]{2,1,0:T(8,128)(2,1)S(1)} %collective-permute-done.13.got_ref, f32[1,4096]{1,0:T(1,128)S(1)} %broadcast_in_dim_reshape.3.area_ref, bf16[256,256]{1,0:T(8,128)(2,1)S(1)} %copy-done.3, ...), custom_call_target="tpu_custom_call" | custom-call | flops 1073741824 | bytes 2097152 | tf_op jit(solution)/shard_map/attend_sent/pallas_call | solution.py:470
  35.8 3.2 %collective-permute-start.14 = (bf16[1,80,256]{2,1,0:T(8,128)(2,1)S(1)}, bf16[1,80,256]{2,1,0:T(8,128)(2,1)S(1)}, u32[]{:S(2)}, u32[]{:S(2)}) collective-permute-start(bf16[1,80,256]{2,1,0:T(8,128)(2,1)S(1)} %attend_sent.1), channel_id=1, source_target_pairs={{0,16},{1,17},{2,18},{3,19},{4,20},{5,21},{6,22},{7,23},{8,24},{9,... | collective-permute-start | bytes 122888 | tf_op jit(solution)/shard_map/ppermute | solution.py:147
  38.9 2.1 %attend_kept.1 = (f32[1,64,256]{2,1,0:T(8,128)S(1)}, f32[1,64,128]{2,1,0:T(8,128)S(1)}) custom-call(bf16[1,64,256]{2,1,0:T(8,128)(2,1)S(1)} %get-tuple-element.30.sel_ref, bf16[1,64,256]{2,1,0:T(8,128)(2,1)S(1)} %collective-permute-done.11.got_ref, f32[1,4096]{1,0:T(1,128)S(1)} %broadcast_in_dim_reshape.3.area_ref, bf16[256,256]{1,0:T(8,128)(2,1)S(1)} %copy-done.3, ...), custom_call_target="tpu_custom_call" | custom-call | flops 1073741824 | bytes 2097152 | tf_op jit(solution)/shard_map/attend_kept/pallas_call | solution.py:470
  41.2 0.8 %fusion = bf16[1,64,256]{2,1,0:T(8,128)(2,1)} fusion(bf16[256,256]{1,0:T(8,128)(2,1)S(1)} %copy-done, bf16[1,64,256]{2,1,0:T(8,128)(2,1)S(1)} %finish.1), kind=kOutput, calls=%fused_computation.2 | convolution fusion | flops 8404992 | bytes 196608 | tf_op jit(solution)/shard_map/dot_general | solution.py:522
  (54 shorter events, 2.7 us)
Async XLA Ops:
  0.0 41.2 %copy-start = (bf16[256,256]{1,0:T(8,128)(2,1)S(1)}, bf16[256,256]{1,0:T(8,128)(2,1)}, u32[]{:S(2)}) copy-start(bf16[256,256]{1,0:T(8,128)(2,1)} %param.15) | copy-start | bytes 393220
  0.0 7.4 %copy-start.1 = (bf16[5,3,73,256]{3,2,1,0:T(8,128)(2,1)S(1)}, bf16[5,3,73,256]{3,2,1,0:T(8,128)(2,1)}, u32[]{:S(2)}) copy-start(bf16[5,3,73,256]{3,2,1,0:T(8,128)(2,1)} %weight_ref.1) | copy-start | bytes 1681924
  0.0 1.0 %copy-start.2 = (bf16[73,8,128]{2,1,0:T(8,128)(2,1)S(1)}, bf16[73,8,128]{2,1,0:T(8,128)(2,1)}, u32[]{:S(2)}) copy-start(bf16[73,8,128]{2,1,0:T(8,128)(2,1)} %own_ref.1) | copy-start | bytes 448516
  1.1 3.6 %collective-permute-start = (bf16[2,80,128]{2,1,0:T(8,128)(2,1)S(1)}, bf16[2,80,128]{2,1,0:T(8,128)(2,1)S(1)}, u32[]{:S(2)}, u32[]{:S(2)}) collective-permute-start(bf16[2,80,128]{2,1,0:T(8,128)(2,1)S(1)} %get-tuple-element.21), channel_id=1, source_target_pairs={{0,2},{1,3},{2,0},{3,1},{4,6},{5,7},{6,4},{7,5},{8,10},{9,11},{10,... | collective-permute-start | bytes 122888 | tf_op jit(solution)/shard_map/ppermute | solution.py:147
  1.6 3.1 %collective-permute-start.1 = (bf16[2,80,128]{2,1,0:T(8,128)(2,1)S(1)}, bf16[2,80,128]{2,1,0:T(8,128)(2,1)S(1)}, u32[]{:S(2)}, u32[]{:S(2)}) collective-permute-start(bf16[2,80,128]{2,1,0:T(8,128)(2,1)S(1)} %get-tuple-element.22), channel_id=1, source_target_pairs={{2,4},{4,2},{3,5},{5,3},{6,8},{8,6},{7,9},{9,7},{10,12},{12,10},{1... | collective-permute-start | bytes 122888 | tf_op jit(solution)/shard_map/ppermute | solution.py:156
  3.9 0.7 %copy-start.6 = (s32[4,5]{1,0:T(4,128)S(1)}, s32[4,5]{1,0:T(4,128)}, u32[]{:S(2)}) copy-start(s32[4,5]{1,0:T(4,128)} %param.9) | copy-start | bytes 244
  4.8 4.3 %collective-permute-start.2 = (bf16[80,128]{1,0:T(8,128)(2,1)S(1)}, bf16[80,128]{1,0:T(8,128)(2,1)S(1)}, u32[]{:S(2)}, u32[]{:S(2)}) collective-permute-start(bf16[80,128]{1,0:T(8,128)(2,1)S(1)} %columns.1), channel_id=1, source_target_pairs={{0,1},{1,0},{2,3},{3,2},{4,5},{5,4},{6,7},{7,6},{8,9},{9,8},{10,11... | collective-permute-start | bytes 61448 | tf_op jit(solution)/shard_map/ppermute | solution.py:147
  9.6 8.5 %collective-permute-start.3 = (bf16[256,256]{1,0:T(8,128)(2,1)S(1)}, bf16[256,256]{1,0:T(8,128)(2,1)S(1)}, u32[]{:S(2)}, u32[]{:S(2)}) collective-permute-start(bf16[256,256]{1,0:T(8,128)(2,1)S(1)} %west.1), channel_id=1, source_target_pairs={{0,1},{1,0},{2,3},{3,2},{4,5},{5,4},{6,7},{7,6},{8,9},{9,8},{10,11... | collective-permute-start | bytes 393224 | tf_op jit(solution)/shard_map/ppermute | solution.py:147
  11.8 10.3 %collective-permute-start.4 = (bf16[256,256]{1,0:T(8,128)(2,1)S(1)}, bf16[256,256]{1,0:T(8,128)(2,1)S(1)}, u32[]{:S(2)}, u32[]{:S(2)}) collective-permute-start(bf16[256,256]{1,0:T(8,128)(2,1)S(1)} %west.1), channel_id=1, source_target_pairs={{0,4},{1,5},{2,6},{3,7},{4,0},{5,1},{6,2},{7,3},{8,12},{9,13},{10,... | collective-permute-start | bytes 393224 | tf_op jit(solution)/shard_map/ppermute | solution.py:147
  15.6 6.4 %collective-permute-start.6 = (bf16[256,256]{1,0:T(8,128)(2,1)S(1)}, bf16[256,256]{1,0:T(8,128)(2,1)S(1)}, u32[]{:S(2)}, u32[]{:S(2)}) collective-permute-start(bf16[256,256]{1,0:T(8,128)(2,1)S(1)} %west.1), channel_id=1, source_target_pairs={{0,8},{1,9},{2,10},{3,11},{4,12},{5,13},{6,14},{7,15},{8,0},{9,1},... | collective-permute-start | bytes 393224 | tf_op jit(solution)/shard_map/ppermute | solution.py:147
  17.1 10.0 %collective-permute-start.9 = (bf16[256,256]{1,0:T(8,128)(2,1)S(1)}, bf16[256,256]{1,0:T(8,128)(2,1)S(1)}, u32[]{:S(2)}, u32[]{:S(2)}) collective-permute-start(bf16[256,256]{1,0:T(8,128)(2,1)S(1)} %west.1), channel_id=1, source_target_pairs={{0,13},{1,12},{2,15},{3,14},{4,9},{5,8},{6,11},{7,10},{8,5},{9,4},... | collective-permute-start | bytes 393224 | tf_op jit(solution)/shard_map/ppermute | solution.py:147
  18.1 7.5 %collective-permute-start.5 = (bf16[256,256]{1,0:T(8,128)(2,1)S(1)}, bf16[256,256]{1,0:T(8,128)(2,1)S(1)}, u32[]{:S(2)}, u32[]{:S(2)}) collective-permute-start(bf16[256,256]{1,0:T(8,128)(2,1)S(1)} %collective-permute-done.3), channel_id=1, source_target_pairs={{0,4},{1,5},{2,6},{3,7},{4,0},{5,1},{6,2},{7,3},{8,12},{9,13},{10,... | collective-permute-start | bytes 393224 | tf_op jit(solution)/shard_map/ppermute | solution.py:147
  22.0 5.0 %collective-permute-start.7 = (bf16[256,256]{1,0:T(8,128)(2,1)S(1)}, bf16[256,256]{1,0:T(8,128)(2,1)S(1)}, u32[]{:S(2)}, u32[]{:S(2)}) collective-permute-start(bf16[256,256]{1,0:T(8,128)(2,1)S(1)} %collective-permute-done.6), channel_id=1, source_target_pairs={{0,1},{1,0},{2,3},{3,2},{4,5},{5,4},{6,7},{7,6},{8,9},{9,8},{10,11... | collective-permute-start | bytes 393224 | tf_op jit(solution)/shard_map/ppermute | solution.py:147
  22.1 5.0 %collective-permute-start.8 = (bf16[256,256]{1,0:T(8,128)(2,1)S(1)}, bf16[256,256]{1,0:T(8,128)(2,1)S(1)}, u32[]{:S(2)}, u32[]{:S(2)}) collective-permute-start(bf16[256,256]{1,0:T(8,128)(2,1)S(1)} %collective-permute-done.4), channel_id=1, source_target_pairs={{0,8},{1,9},{2,10},{3,11},{4,12},{5,13},{6,14},{7,15},{8,0},{9,1},... | collective-permute-start | bytes 393224 | tf_op jit(solution)/shard_map/ppermute | solution.py:147
  27.1 6.5 %copy-start.5 = (bf16[256,256]{1,0:T(8,128)(2,1)S(1)}, bf16[256,256]{1,0:T(8,128)(2,1)}, u32[]{:S(2)}) copy-start(bf16[256,256]{1,0:T(8,128)(2,1)} %wv_ref.3) | copy-start | bytes 393220
  27.3 1.3 %collective-permute-start.10 = (bf16[2,64,256]{2,1,0:T(8,128)(2,1)S(1)}, bf16[2,64,256]{2,1,0:T(8,128)(2,1)S(1)}, u32[]{:S(2)}, u32[]{:S(2)}) collective-permute-start(bf16[2,64,256]{2,1,0:T(8,128)(2,1)S(1)} %get-tuple-element.28), channel_id=1, source_target_pairs={{0,2},{1,3},{2,0},{3,1},{4,6},{5,7},{6,4},{7,5},{8,10},{9,11},{10,... | collective-permute-start | bytes 196616 | tf_op jit(solution)/shard_map/ppermute | solution.py:147
  28.6 5.1 %copy-start.3 = (bf16[256,256]{1,0:T(8,128)(2,1)S(1)}, bf16[256,256]{1,0:T(8,128)(2,1)}, u32[]{:S(2)}) copy-start(bf16[256,256]{1,0:T(8,128)(2,1)} %wq_ref.3) | copy-start | bytes 393220
  28.6 5.1 %copy-start.4 = (bf16[256,256]{1,0:T(8,128)(2,1)S(1)}, bf16[256,256]{1,0:T(8,128)(2,1)}, u32[]{:S(2)}) copy-start(bf16[256,256]{1,0:T(8,128)(2,1)} %wk_ref.3) | copy-start | bytes 393220
  28.6 5.0 %collective-permute-start.12 = (bf16[2048,256]{1,0:T(8,128)(2,1)S(1)}, bf16[2048,256]{1,0:T(8,128)(2,1)S(1)}, u32[]{:S(2)}, u32[]{:S(2)}) collective-permute-start(bf16[2048,256]{1,0:T(8,128)(2,1)S(1)} %constant_dynamic-update-slice_fusion.near_ref.refs_0_), channel_id=1, source_target_pairs={{0,2},{1,3},{2,0},{3,1},{4,6},{5,7},{6,4},{7,5},{8,10},{9,11},{10,... | collective-permute-start | bytes 3145736 | tf_op jit(solution)/shard_map/ppermute | solution.py:147
  28.8 4.8 %collective-permute-start.13 = (bf16[1,64,256]{2,1,0:T(8,128)(2,1)S(1)}, bf16[1,64,256]{2,1,0:T(8,128)(2,1)S(1)}, u32[]{:S(2)}, u32[]{:S(2)}) collective-permute-start(bf16[1,64,256]{2,1,0:T(8,128)(2,1)S(1)} %get-tuple-element.30.sel_ref), channel_id=1, source_target_pairs={{0,16},{1,17},{2,18},{3,19},{4,20},{5,21},{6,22},{7,23},{8,24},{9,... | collective-permute-start | bytes 98312 | tf_op jit(solution)/shard_map/ppermute | solution.py:147
  32.0 6.9 %collective-permute-start.11 = (bf16[1,64,256]{2,1,0:T(8,128)(2,1)S(1)}, bf16[1,64,256]{2,1,0:T(8,128)(2,1)S(1)}, u32[]{:S(2)}, u32[]{:S(2)}) collective-permute-start(bf16[1,64,256]{2,1,0:T(8,128)(2,1)S(1)} %get-tuple-element.31.sel_ref), channel_id=1, source_target_pairs={{0,16},{1,17},{2,18},{3,19},{4,20},{5,21},{6,22},{7,23},{8,24},{9,... | collective-permute-start | bytes 98312 | tf_op jit(solution)/shard_map/ppermute | solution.py:147
  35.8 5.3 %collective-permute-start.14 = (bf16[1,80,256]{2,1,0:T(8,128)(2,1)S(1)}, bf16[1,80,256]{2,1,0:T(8,128)(2,1)S(1)}, u32[]{:S(2)}, u32[]{:S(2)}) collective-permute-start(bf16[1,80,256]{2,1,0:T(8,128)(2,1)S(1)} %attend_sent.1), channel_id=1, source_target_pairs={{0,16},{1,17},{2,18},{3,19},{4,20},{5,21},{6,22},{7,23},{8,24},{9,... | collective-permute-start | bytes 122888 | tf_op jit(solution)/shard_map/ppermute | solution.py:147
